TPU v7x, 32 devices: a whole 2x2x4 slice. The times are simulated.
32 devices in a mesh: batch: 8 (over z, y), col: 4 (over x, core).
Axes of the slice: x: 2, y: 2, z: 4, core: 2. Of those that a mesh axis runs over, the one named last changes fastest.
Arguments:
- watch_ids: int32 [1024, 50], P('batch'), may hold values from 0 to 65535
- search_ids: int32 [1024, 50], P('batch'), may hold values from 0 to 65535
- demo_ids: int32 [1024, 4], P('batch'), may hold values from 0 to 255
- pos_ids: int32 [1024], P('batch'), may hold values from 0 to 65535
- neg_ids: int32 [5120], replicated, may hold values from 0 to 65535
- valid_counts: int32 [8], P('batch'), may hold values from 1 to 128, as said below
- watch_table: bfloat16 [256, 65536], P('col', 'batch'), may hold values from -15 to 15
- search_table: bfloat16 [256, 65536], P('col', 'batch'), may hold values from -15 to 15
- demo_table: bfloat16 [256, 88], replicated, may hold values from -3 to 3
- out_table: bfloat16 [256, 65536], P('col', 'batch'), may hold values from -1.796875 to 1.796875
- w_first: bfloat16 [600, 1024], replicated, may hold values from -0.25 to 0.25
- b_first: float32 [1024], replicated, may hold values from -1.8 to 1.8
- w_second: bfloat16 [1024, 512], replicated, may hold values from -0.1875 to 0.1875
- b_second: float32 [512], replicated, may hold values from -1.8 to 1.8
- w_third: bfloat16 [512, 256], replicated, may hold values from -0.25 to 0.25
- b_third: float32 [256], replicated, may hold values from -1.8 to 1.8
Outputs:
- user_vecs: bfloat16 [1024, 256], P(('batch', 'col'))
- loss: float32 [], replicated
- grad_watch: float32 [256, 65536], P('col', 'batch')
- grad_search: float32 [256, 65536], P('col', 'batch')
- grad_out: float32 [256, 65536], P('col', 'batch')
- grad_demo: float32 [256, 88], replicated
- grad_w_first: float32 [600, 1024], replicated
- grad_b_first: float32 [1024], replicated
- grad_w_second: float32 [1024, 512], replicated
- grad_b_second: float32 [512], replicated
- grad_w_third: float32 [512, 256], replicated
- grad_b_third: float32 [256], replicated
Inputs may be any that keep to these rules, and one draw needn't show every extreme that they name: `valid_counts`: each index of batch has that many valid examples, its first slots; the last index of batch has exactly 128.
All inputs are finite; a program needn't handle non-finite values.
Results may differ from a plain program's by a relative error of at most 0.015.
Values may be sent and summed in bfloat16 or wider, within the bound.
A program may use at most 128 MiB of HBM per device.

v0:
```python
import math

import jax
import jax.numpy as jnp
from jax import lax
from jax.sharding import PartitionSpec as P


def contract_rows(left, right):
    return lax.dot_general(
        left, right, (((0,), (0,)), ((), ())), preferred_element_type=jnp.float32
    )


def contract_cols(left, right):
    return lax.dot_general(
        left, right, (((1,), (1,)), ((), ())), preferred_element_type=jnp.float32
    )


def gelu_back(pre_value, grad_value):
    return jax.vjp(jax.nn.gelu, pre_value)[1](grad_value)[0]


def per_device(
    watch_ids,
    search_ids,
    demo_ids,
    pos_ids,
    neg_ids,
    valid_counts,
    watch_table,
    search_table,
    demo_table,
    out_table,
    w_first,
    b_first,
    w_second,
    b_second,
    w_third,
    b_third,
):
    row_count = watch_ids.shape[0]
    bag_size = watch_ids.shape[1]
    col_width = watch_table.shape[0]
    vocab_rows = watch_table.shape[1]
    embed_width = col_width * lax.axis_size("col")
    offset = lax.axis_index("batch") * vocab_rows
    col_slot = lax.axis_index("col")
    quarter = row_count // lax.axis_size("col")
    low_width = math.gcd(vocab_rows, 128)
    high_width = vocab_rows // low_width

    def owned(id_values):
        local_ids = id_values - offset
        return jnp.where((local_ids >= 0) & (local_ids < vocab_rows), local_ids, vocab_rows)

    def bag_counts(id_block):
        local_ids = owned(id_block)
        high_hot = (
            local_ids[:, :, None] // low_width == jnp.arange(high_width)[None, None, :]
        ).astype(jnp.bfloat16)
        low_hot = (
            local_ids[:, :, None] % low_width == jnp.arange(low_width)[None, None, :]
        ).astype(jnp.bfloat16)
        counted = jnp.einsum("rbh,rbl->rhl", high_hot, low_hot, preferred_element_type=jnp.bfloat16)
        return counted.reshape(id_block.shape[0], vocab_rows)

    def single_hot(id_block):
        return (owned(id_block)[:, None] == jnp.arange(vocab_rows)[None, :]).astype(jnp.bfloat16)

    zero_col = jnp.zeros((col_width, 1), jnp.bfloat16)
    padded_out = jnp.concatenate([out_table, zero_col], axis=1)
    all_watch, all_search, all_pos = (
        lax.all_gather(watch_ids, "batch", axis=0, tiled=True),
        lax.all_gather(search_ids, "batch", axis=0, tiled=True),
        lax.all_gather(pos_ids, "batch", axis=0, tiled=True),
    )
    total_rows = all_watch.shape[0]
    block_rows = min(1024, total_rows)
    block_count = total_rows // block_rows
    neg_local = owned(neg_ids)
    neg_part = jnp.take(padded_out, neg_local, axis=1).astype(jnp.float32)

    def flatten_blocks(stacked):
        return stacked.transpose(1, 0, 2).reshape(col_width, total_rows)

    def bag_block(inputs_block):
        watch_block, search_block, pos_block = inputs_block
        watch_part = contract_cols(watch_table, bag_counts(watch_block))
        search_part = contract_cols(search_table, bag_counts(search_block))
        pos_part = contract_cols(out_table, single_hot(pos_block))
        return (watch_part, search_part, pos_part)

    id_blocks = (
        all_watch.reshape(block_count, block_rows, bag_size),
        all_search.reshape(block_count, block_rows, bag_size),
        all_pos.reshape(block_count, block_rows),
    )
    watch_parts, search_parts, pos_parts = lax.map(bag_block, id_blocks)
    watch_sum, search_sum, pos_rows = (
        lax.psum_scatter(flatten_blocks(watch_parts), "batch", scatter_dimension=1, tiled=True),
        lax.psum_scatter(flatten_blocks(search_parts), "batch", scatter_dimension=1, tiled=True),
        lax.psum_scatter(flatten_blocks(pos_parts), "batch", scatter_dimension=1, tiled=True),
    )
    neg_rows, valid_total = lax.psum((neg_part, jnp.sum(valid_counts).astype(jnp.float32)), "batch")
    pooled_watch = (watch_sum / bag_size).astype(jnp.bfloat16)
    pooled_search = (search_sum / bag_size).astype(jnp.bfloat16)
    pos_bf = pos_rows.astype(jnp.bfloat16)
    neg_bf = neg_rows.astype(jnp.bfloat16)
    count_here = valid_counts[0]
    full_watch, full_search, full_pos, full_neg = (
        lax.all_gather(pooled_watch, "col", axis=0, tiled=True),
        lax.all_gather(pooled_search, "col", axis=0, tiled=True),
        lax.all_gather(pos_bf, "col", axis=0, tiled=True),
        lax.all_gather(neg_bf, "col", axis=0, tiled=True),
    )
    watch_rows = full_watch.T
    search_rows = full_search.T
    pos_full = full_pos.T
    live_rows = jnp.arange(row_count) < count_here
    weight = jnp.where(live_rows, 1.0 / valid_total, 0.0)
    buckets = demo_table.shape[0]
    bucket_counts = jnp.sum(
        (demo_ids[:, :, None] == jnp.arange(buckets)[None, None, :]).astype(jnp.float32), axis=1
    ).astype(jnp.bfloat16)
    demo_vec = jnp.dot(bucket_counts, demo_table, preferred_element_type=jnp.float32)
    joined = jnp.concatenate([watch_rows, search_rows, demo_vec.astype(jnp.bfloat16)], axis=1)
    pre_first = jnp.dot(joined, w_first, preferred_element_type=jnp.float32) + b_first
    act_first = jax.nn.gelu(pre_first).astype(jnp.bfloat16)
    pre_second = jnp.dot(act_first, w_second, preferred_element_type=jnp.float32) + b_second
    act_second = jax.nn.gelu(pre_second).astype(jnp.bfloat16)
    user_block = (
        jnp.dot(act_second, w_third, preferred_element_type=jnp.float32) + b_third
    ).astype(jnp.bfloat16)
    neg_logits = jnp.dot(user_block, full_neg, preferred_element_type=jnp.float32)
    pos_logit = jnp.sum(user_block.astype(jnp.float32) * pos_full.astype(jnp.float32), axis=1)
    row_peak = jnp.maximum(jnp.max(neg_logits, axis=1), pos_logit)
    exp_neg = jnp.exp(neg_logits - row_peak[:, None])
    exp_pos = jnp.exp(pos_logit - row_peak)
    row_total = jnp.sum(exp_neg, axis=1) + exp_pos
    lse = row_peak + jnp.log(row_total)
    loss_here = jnp.sum(weight * (lse - pos_logit))
    grad_neg = (weight[:, None] * exp_neg / row_total[:, None]).astype(jnp.bfloat16)
    grad_pos = (weight * (exp_pos / row_total - 1.0)).astype(jnp.bfloat16)
    grad_user = (
        contract_cols(grad_neg, full_neg)
        + grad_pos.astype(jnp.float32)[:, None] * pos_full.astype(jnp.float32)
    ).astype(jnp.bfloat16)
    neg_row_grad = contract_rows(user_block, grad_neg)
    pos_row_grad = (grad_pos.astype(jnp.float32)[:, None] * user_block.astype(jnp.float32)).astype(
        jnp.bfloat16
    )
    grad_w_third = contract_rows(act_second, grad_user)
    grad_b_third = jnp.sum(grad_user.astype(jnp.float32), axis=0)
    grad_pre_second = gelu_back(pre_second, contract_cols(grad_user, w_third)).astype(jnp.bfloat16)
    grad_w_second = contract_rows(act_first, grad_pre_second)
    grad_b_second = jnp.sum(grad_pre_second.astype(jnp.float32), axis=0)
    grad_pre_first = gelu_back(pre_first, contract_cols(grad_pre_second, w_second)).astype(
        jnp.bfloat16
    )
    grad_w_first = contract_rows(joined, grad_pre_first)
    grad_b_first = jnp.sum(grad_pre_first.astype(jnp.float32), axis=0)
    grad_joined = contract_cols(grad_pre_first, w_first).astype(jnp.bfloat16)
    grad_pw = grad_joined[:, :embed_width]
    grad_ps = grad_joined[:, embed_width : 2 * embed_width]
    grad_demo = contract_rows(bucket_counts, grad_joined[:, 2 * embed_width :])
    col_start = col_slot * col_width
    own_pw = lax.dynamic_slice_in_dim(grad_pw, col_start, col_width, 1).T
    own_ps = lax.dynamic_slice_in_dim(grad_ps, col_start, col_width, 1).T
    own_pos = lax.dynamic_slice_in_dim(pos_row_grad, col_start, col_width, 1).T
    user_vecs = lax.dynamic_slice_in_dim(user_block, col_slot * quarter, quarter, 0)
    all_pw, all_ps, all_dpos = (
        lax.all_gather(own_pw, "batch", axis=1, tiled=True),
        lax.all_gather(own_ps, "batch", axis=1, tiled=True),
        lax.all_gather(own_pos, "batch", axis=1, tiled=True),
    )
    neg_own = lax.dynamic_slice_in_dim(neg_row_grad, col_slot * col_width, col_width, 0)
    sums_out = lax.psum(
        (
            grad_w_first,
            grad_b_first,
            grad_w_second,
            grad_b_second,
            grad_w_third,
            grad_b_third,
            grad_demo,
            neg_own,
            loss_here,
        ),
        "batch",
    )
    neg_sum_own = sums_out[7]

    def split_blocks(columns):
        return columns.reshape(col_width, block_count, block_rows).transpose(1, 0, 2)

    def grad_block(running, inputs_block):
        watch_block, search_block, pos_block, block_pw, block_ps, block_pos = inputs_block
        new_watch = running[0] + jnp.dot(
            block_pw, bag_counts(watch_block), preferred_element_type=jnp.float32
        )
        new_search = running[1] + jnp.dot(
            block_ps, bag_counts(search_block), preferred_element_type=jnp.float32
        )
        new_out = running[2] + jnp.dot(
            block_pos, single_hot(pos_block), preferred_element_type=jnp.float32
        )
        return ((new_watch, new_search, new_out), None)

    zeros_table = jnp.zeros((col_width, vocab_rows), jnp.float32)
    (table_watch, table_search, table_out), _ = lax.scan(
        grad_block,
        (zeros_table, zeros_table, zeros_table),
        id_blocks + (split_blocks(all_pw), split_blocks(all_ps), split_blocks(all_dpos)),
    )
    neg_added = (
        jnp.zeros((col_width, vocab_rows + 1), jnp.float32).at[:, neg_local].add(neg_sum_own)
    )
    table_out = table_out + neg_added[:, :vocab_rows]
    return (
        user_vecs,
        sums_out[8],
        table_watch / bag_size,
        table_search / bag_size,
        table_out,
        sums_out[6],
        sums_out[0],
        sums_out[1],
        sums_out[2],
        sums_out[3],
        sums_out[4],
        sums_out[5],
    )


def solution(mesh):
    in_specs = (
        P("batch", None),
        P("batch", None),
        P("batch", None),
        P("batch"),
        P(),
        P("batch"),
        P("col", "batch"),
        P("col", "batch"),
        P(),
        P("col", "batch"),
        P(),
        P(),
        P(),
        P(),
        P(),
        P(),
    )
    out_specs = (
        P(("batch", "col"), None),
        P(),
        P("col", "batch"),
        P("col", "batch"),
        P("col", "batch"),
        P(),
        P(),
        P(),
        P(),
        P(),
        P(),
        P(),
    )
    return jax.shard_map(
        per_device, mesh=mesh, in_specs=in_specs, out_specs=out_specs, check_vma=False
    )
```

profile of v0, /device:TPU:1, one launch (start us, length us, event | category | flops | bytes accessed | tf_op | source)
XLA Modules:
  0.0 642.7 jit_solution(16935257819675166655)
XLA Ops:
  8.1 18.1 %all-gather = s32[8,1,128]{2,1,0:T(1,128)S(1)} all-gather(s32[1,1,128]{2,1,0:T(1,128)} %bitcast.85), channel_id=1, replica_groups=mesh['batch'=8,'col'=4] {'batch'}, dimensions={0}, use_global_device_ids=true | all-gather | bytes 4608 | tf_op jit(solution)/shard_map/all_gather | solution.py:77
  26.2 8.9 %fusion.32 = f32[64,1024]{1,0:T(8,128)} fusion(bf16[64,8192]{1,0:T(8,128)(2,1)} %param.25, s32[1024]{0:T(1024)S(1)} %and_select_fusion.2), kind=kOutput, calls=%fused_computation.39 | convolution fusion | flops 1082130432 | bytes 1314816 | tf_op jit(solution)/shard_map/while/body/eval_jaxpr/dot_general | solution.py:16
  35.1 24.5 %all_gather.32 = s32[1024,50]{0,1:T(8,128)S(1)} all-gather(s32[128,50]{0,1:T(8,128)S(1)} %copy-done.9), channel_id=1, replica_groups=mesh['batch'=8,'col'=4] {'batch'}, dimensions={0}, use_global_device_ids=true | all-gather | bytes 230400 | tf_op jit(solution)/shard_map/all_gather | solution.py:76
  59.6 24.8 %all_gather.30 = s32[1024,50]{0,1:T(8,128)S(1)} all-gather(s32[128,50]{0,1:T(8,128)S(1)} %copy-done.10), channel_id=1, replica_groups=mesh['batch'=8,'col'=4] {'batch'}, dimensions={0}, use_global_device_ids=true | all-gather | bytes 230400 | tf_op jit(solution)/shard_map/all_gather | solution.py:75
  85.3 39.7 %fusion.3 = bf16[1024,64,128]{2,1,0:T(8,128)(2,1)} fusion(s32[1024,50]{1,0:T(8,128)S(1)} %copy.59, s32[1024,50]{1,0:T(8,128)S(1)} %copy.58), kind=kOutput, calls=%fused_computation.10 | convolution fusion | flops 848691200 | bytes 17186816 | tf_op jit(solution)/shard_map/while/body/eval_jaxpr/rbh,rbl->rhl/dot_general | solution.py:66
  125.0 13.7 %fusion.36 = f32[64,1024]{1,0:T(8,128)} fusion(bf16[64,8192]{1,0:T(8,128)(2,1)S(1)} %copy-done.14, bf16[128,8,64,128]{3,2,1,0:T(8,128)(2,1)} %bitcast.86), kind=kOutput, calls=%fused_computation.41 | convolution fusion | flops 1073741824 | bytes 18087936 | tf_op jit(solution)/shard_map/while/body/eval_jaxpr/dot_general | solution.py:16
  139.3 39.7 %fusion.2 = bf16[1024,64,128]{2,1,0:T(8,128)(2,1)} fusion(s32[1024,50]{1,0:T(8,128)S(1)} %copy.57, s32[1024,50]{1,0:T(8,128)S(1)} %copy.56), kind=kOutput, calls=%fused_computation.9 | convolution fusion | flops 848691200 | bytes 17186816 | tf_op jit(solution)/shard_map/while/body/eval_jaxpr/rbh,rbl->rhl/dot_general | solution.py:66
  179.0 13.8 %fusion.33 = f32[64,1024]{1,0:T(8,128)} fusion(bf16[64,8192]{1,0:T(8,128)(2,1)S(1)} %copy-done.15, bf16[128,8,64,128]{3,2,1,0:T(8,128)(2,1)} %bitcast.88), kind=kOutput, calls=%fused_computation.40 | convolution fusion | flops 1073741824 | bytes 18087936 | tf_op jit(solution)/shard_map/while/body/eval_jaxpr/dot_general | solution.py:16
  193.1 1.8 copy.60
  194.9 1.8 concatenate.7
  196.7 18.8 %gather_fusion = bf16[5120,64]{1,0:T(8,128)(2,1)} fusion(bf16[64,8193]{0,1:T(8,128)(2,1)S(1)} %concatenate.7, s32[5120]{0:T(1024)S(1)} %broadcast_clamp_fusion), kind=kCustom, calls=%fused_computation | custom fusion | bytes 1331200 | tf_op jit(solution)/shard_map/jit(_take)/gather | solution.py:83
  217.9 63.6 %all-reduce.8 = (f32[]{:T(128)}, bf16[64,5120]{1,0:T(8,128)(2,1)}) all-reduce(f32[]{:T(128)S(6)} %convert_element_type.117, f32[64,5120]{1,0:T(8,128)S(1)} %convert_bitcast_fusion), channel_id=1, replica_groups=mesh['batch'=8,'col'=4] {'batch'}, use_global_device_ids=true, to_apply=%region_3.4 | all-reduce | flops 327681 | bytes 1966088 | tf_op jit(solution)/shard_map/psum | solution.py:106
  283.4 34.1 %all_gather.36 = bf16[256,128]{1,0:T(8,128)(2,1)S(1)} all-gather(bf16[64,128]{1,0:T(8,128)(2,1)S(1)} %convert_element_type.121), channel_id=1, replica_groups=mesh['batch'=8,'col'=4] {'col'}, dimensions={0}, use_global_device_ids=true | all-gather | bytes 81920 | tf_op jit(solution)/shard_map/all_gather | solution.py:115
  318.4 5.6 all_gather.33
  324.8 5.5 all_gather.31
  330.8 1.6 convolution_add_fusion.1
  332.7 3.0 all-gather.3.cloned.1.call-done
  335.7 2.3 fusion.73
  344.0 1.9 fusion.59
  345.9 1.8 fusion.69
  351.4 19.4 %all-reduce.1 = (f32[]{:T(128)}, f32[1024]{0:T(1024)}, f32[512]{0:T(512)}, f32[256]{0:T(256)}) all-reduce(f32[]{:T(128)} %get-tuple-element.104, f32[1024]{0:T(1024)S(1)} %get-tuple-element.91, f32[512]{0:T(512)S(1)} %get-tuple-element.89, f32[256]{0:T(256)S(1)} %get-tuple-element.109), channel_id=1, replica_groups=mesh['batch'=8,'col'=4] {'batch'}, use_global_device_ids=true, to_apply=%region_10.11 | all-reduce | flops 1793 | bytes 14344 | tf_op jit(solution)/shard_map/psum | solution.py:179
  370.9 25.2 %all_gather.37 = bf16[64,1024]{1,0:T(8,128)(2,1)S(1)} all-gather(bf16[64,128]{1,0:T(8,128)(2,1)S(1)} %dynamic-slice_bitcast_fusion.1), channel_id=1, replica_groups=mesh['batch'=8,'col'=4] {'batch'}, dimensions={1}, use_global_device_ids=true | all-gather | bytes 147456 | tf_op jit(solution)/shard_map/all_gather | solution.py:174
  396.0 24.6 %all_gather.38 = bf16[64,1024]{1,0:T(8,128)(2,1)S(1)} all-gather(bf16[64,128]{1,0:T(8,128)(2,1)S(1)} %dynamic-slice_bitcast_fusion), channel_id=1, replica_groups=mesh['batch'=8,'col'=4] {'batch'}, dimensions={1}, use_global_device_ids=true | all-gather | bytes 147456 | tf_op jit(solution)/shard_map/all_gather | solution.py:175
  420.7 26.2 %all_gather.39 = bf16[64,1024]{0,1:T(8,128)(2,1)S(1)} all-gather(bf16[64,128]{0,1:T(8,128)(2,1)S(1)} %fusion.60), channel_id=1, replica_groups=mesh['batch'=8,'col'=4] {'batch'}, dimensions={1}, use_global_device_ids=true | all-gather | bytes 147456 | tf_op jit(solution)/shard_map/all_gather | solution.py:176
  447.0 18.9 %fusion.22 = f32[64,8192]{1,0:T(8,128)} fusion(bf16[64,1024]{1,0:T(8,128)(2,1)S(1)} %all_gather.37, bf16[128,8,64,128]{3,2,1,0:T(8,128)(2,1)} %bitcast.89), kind=kOutput, calls=%fused_computation.29 | convolution fusion | flops 1074266112 | bytes 19005440 | tf_op jit(solution)/shard_map/while/body/eval_jaxpr/dot_general | solution.py:200
  465.9 19.1 %fusion.25 = f32[64,8192]{1,0:T(8,128)} fusion(bf16[64,1024]{1,0:T(8,128)(2,1)S(1)} %all_gather.38, bf16[128,8,64,128]{3,2,1,0:T(8,128)(2,1)} %bitcast.87), kind=kOutput, calls=%fused_computation.30 | convolution fusion | flops 1074266112 | bytes 19005440 | tf_op jit(solution)/shard_map/while/body/eval_jaxpr/dot_general | solution.py:203
  484.9 93.6 %all-reduce.7.cloned.1.call-done = (f32[64,5120]{1,0:T(8,128)}, f32[256,88]{0,1:T(8,128)}, f32[600,1024]{1,0:T(8,128)}, f32[1024,512]{1,0:T(8,128)}, f32[512,256]{1,0:T(8,128)}) async-done(((f32[64,5120]{1,0:T(8,128)}, f32[256,88]{0,1:T(8,128)}, f32[600,1024]{1,0:T(8,128)}, f32[1024,512]{1,0:T(8,128)}, f32[512,256]{1,0:T(8,128)}), (f32[64,5120]{1,0:T(8,128)}, f32[256,88]{0,1:T(8,128)}, ...) | async-done | bytes 6479888 | tf_op jit(solution)/shard_map/psum | solution.py:179
  578.5 3.0 copy.63
  581.5 34.0 %scatter_custom_fusion = f32[64,8193]{0,1:T(8,128)} fusion(s32[5120]{0:T(1024)S(1)} %get-tuple-element.96, f32[5120,64]{1,0:T(8,128)} %copy.63, f32[]{:T(128)} %constant.147.clone.1), kind=kCustom, calls=%fused_computation.35 | custom fusion | flops 327680 | bytes 2097920 | tf_op jit(solution)/shard_map/scatter-add | solution.py:218
  615.6 4.4 slice.20
  620.0 3.0 copy.65
  623.1 8.0 %fusion.28 = f32[64,8192]{1,0:T(8,128)} fusion(f32[64,8192]{1,0:T(8,128)S(1)} %copy.65, bf16[64,1024]{0,1:T(8,128)(2,1)S(1)} %all_gather.39, s32[1024]{0:T(1024)S(1)} %and_select_fusion.2), kind=kOutput, calls=%fused_computation.31 | convolution fusion | flops 1082654720 | bytes 4329472 | tf_op jit(solution)/shard_map/while/body/eval_jaxpr/dot_general | solution.py:206
  (95 shorter events, 21.2 us)
Async XLA Ops:
  8.0 322.3 %copy-start = (bf16[600,1024]{1,0:T(8,128)(2,1)S(1)}, bf16[600,1024]{1,0:T(8,128)(2,1)}, u32[]{:S(2)}) copy-start(bf16[600,1024]{1,0:T(8,128)(2,1)} %param.26) | copy-start | bytes 3686404
  8.0 274.6 %reduce-scatter.8.cloned.1.call-start = ((), (), s32[]{:S(2)}) async-start(), calls=%async_computation.6 | async-start | bytes 294912 | tf_op jit(solution)/shard_map/reduce_scatter | solution.py:104
  26.2 9.0 %copy-start.9 = (s32[128,50]{0,1:T(8,128)S(1)}, s32[128,50]{0,1:T(8,128)}, u32[]{:S(2)}) copy-start(s32[128,50]{0,1:T(8,128)} %param.17) | copy-start | bytes 76804
  26.2 33.5 %copy-start.10 = (s32[128,50]{0,1:T(8,128)S(1)}, s32[128,50]{0,1:T(8,128)}, u32[]{:S(2)}) copy-start(s32[128,50]{0,1:T(8,128)} %param.16) | copy-start | bytes 76804
  35.1 282.6 %reduce-scatter.6.cloned.1.call-start = ((), (), s32[]{:S(2)}) async-start(), calls=%async_computation.4 | async-start | bytes 294912 | tf_op jit(solution)/shard_map/reduce_scatter | solution.py:103
  85.3 39.7 %copy-start.14 = (bf16[64,8192]{1,0:T(8,128)(2,1)S(1)}, bf16[64,8192]{1,0:T(8,128)(2,1)}, u32[]{:S(2)}) copy-start(bf16[64,8192]{1,0:T(8,128)(2,1)} %param.23) | copy-start | bytes 3145732
  138.8 185.2 %reduce-scatter.4.cloned.1.call-start = ((), (), s32[]{:S(2)}) async-start(), calls=%async_computation.3 | async-start | bytes 294912 | tf_op jit(solution)/shard_map/reduce_scatter | solution.py:102
  139.3 39.7 %copy-start.15 = (bf16[64,8192]{1,0:T(8,128)(2,1)S(1)}, bf16[64,8192]{1,0:T(8,128)(2,1)}, u32[]{:S(2)}) copy-start(bf16[64,8192]{1,0:T(8,128)(2,1)} %param.22) | copy-start | bytes 3145732
  179.0 14.2 %copy-start.5 = (bf16[64,8192]{1,0:T(8,128)(2,1)S(1)}, bf16[64,8192]{1,0:T(8,128)(2,1)}, u32[]{:S(2)}) copy-start(bf16[64,8192]{1,0:T(8,128)(2,1)} %param.25) | copy-start | bytes 3145732
  192.8 2.1 copy-start.11
  192.8 142.9 %all-gather.3.cloned.1.call-start = ((), (), s32[]{:S(2)}) async-start(), calls=%async_computation.5 | async-start | bytes 3276800 | tf_op jit(solution)/shard_map/all_gather | solution.py:116
  215.5 66.8 %copy-start.13 = (s32[128,4]{0,1:T(4,128)S(1)}, s32[128,4]{0,1:T(4,128)}, u32[]{:S(2)}) copy-start(s32[128,4]{0,1:T(4,128)} %param.18) | copy-start | bytes 6148
  215.5 66.9 %copy-start.8 = (bf16[256,88]{0,1:T(8,128)(2,1)S(1)}, bf16[256,88]{0,1:T(8,128)(2,1)}, u32[]{:S(2)}) copy-start(bf16[256,88]{0,1:T(8,128)(2,1)} %param.24) | copy-start | bytes 135172
  217.1 113.2 %copy-start.12 = (f32[1024]{0:T(1024)S(1)}, f32[1024]{0:T(1024)}, u32[]{:S(2)}) copy-start(f32[1024]{0:T(1024)} %param.27) | copy-start | bytes 12292
  217.2 113.6 %copy-start.18 = (f32[512]{0:T(512)S(1)}, f32[512]{0:T(512)}, u32[]{:S(2)}) copy-start(f32[512]{0:T(512)} %param.29) | copy-start | bytes 6148
  281.5 50.9 %copy-start.17 = (bf16[512,256]{1,0:T(8,128)(2,1)S(1)}, bf16[512,256]{1,0:T(8,128)(2,1)}, u32[]{:S(2)}) copy-start(bf16[512,256]{1,0:T(8,128)(2,1)} %param.30) | copy-start | bytes 786436
  281.5 50.9 %copy-start.19 = (f32[256]{0:T(256)S(1)}, f32[256]{0:T(256)}, u32[]{:S(2)}) copy-start(f32[256]{0:T(256)} %param.31) | copy-start | bytes 3076
  281.5 297.0 %all-reduce.7.cloned.1.call-start = ((), (), s32[]{:S(2)}) async-start(), calls=%async_computation.7 | async-start | bytes 12959744 | tf_op jit(solution)/shard_map/psum | solution.py:179
  339.8 1.7 copy-start.2
  341.5 1.4 copy-start.16
  623.0 8.0 %copy-start.7 = (f32[256,88]{0,1:T(8,128)S(1)}, f32[256,88]{0,1:T(8,128)}, u32[]{:S(2)}) copy-start(f32[256,88]{0,1:T(8,128)} %get-tuple-element.118) | copy-start | bytes 270340
  623.0 8.7 %copy-start.3 = (f32[600,1024]{1,0:T(8,128)S(1)}, f32[600,1024]{1,0:T(8,128)}, u32[]{:S(2)}) copy-start(f32[600,1024]{1,0:T(8,128)} %get-tuple-element.119) | copy-start | bytes 7372804
  631.1 2.1 copy-start.4
  631.7 3.6 copy-start.1
  633.2 1.4 copy-start.6
Sparse Core Ops, SparseCore 0:
  35.2 61.0 reduce-scatter.7
  138.9 73.3 reduce-scatter.5
  216.1 62.4 reduce-scatter.3
  350.9 227.5 all-reduce.6
Sparse Core Ops, SparseCore 1:
  281.6 54.0 all-gather.2
where the time goes:
time: 651 us; the launch traced here: 643 us
  blocking collectives  272 us (42%)
  matrix products  176 us (27%)
  waiting for transfers between devices  96.7 us (15%)
  local copies, waits for them, and re-layouts  42.4 us (7%)
  other arithmetic  38.9 us (6%)
  between operations  17.2 us (3%)
    psum x1, waiting for transfers between devices, per_device(): lax.psum((grad_w_first, grad_b_first, grad_w_second, grad_b_second, grad_...  93.6 us
    dot_general x2, matrix products, bag_counts(): jnp.einsum('rbh,rbl->rhl', high_hot, low_hot, preferred_element_type=jnp....  79.4 us
    psum x1, blocking collectives, per_device(): lax.psum((neg_part, jnp.sum(valid_counts).astype(jnp.float32)), 'batch')  63.6 us
    dot_general x7, matrix products, contract_cols(): lax.dot_general(left, right, (((1,), (1,)), ((), ())), preferred_element_...  38.9 us
    all_gather x1, blocking collectives, per_device(): lax.all_gather(pos_bf, 'col', axis=0, tiled=True)  34.1 us
    scatter-add x1, other arithmetic, per_device(): jnp.zeros((col_width, vocab_rows + 1), jnp.float32).at[:, neg_local]  34 us
    all_gather x1, blocking collectives, per_device(): lax.all_gather(own_pos, 'batch', axis=1, tiled=True)  26.2 us
    all_gather x1, blocking collectives, per_device(): lax.all_gather(own_pw, 'batch', axis=1, tiled=True)  25.2 us
  transfers between devices with their start and end apart: 5, of which 2 were waited for; matrix products, arithmetic and copies ran while one was open for 27% of the time, Pallas kernels for 0%

commit v1 on v0

--- a/solution.py
+++ b/solution.py
@@ -1,8 +1,11 @@
+import functools
 import math
 
 import jax
 import jax.numpy as jnp
 from jax import lax
+from jax.experimental import pallas as pl
+from jax.experimental.pallas import tpu as pltpu
 from jax.sharding import PartitionSpec as P
 
 
@@ -234,6 +237,833 @@
     )
 
 
+F32, BF16, FP8, I32 = jnp.float32, jnp.bfloat16, jnp.float8_e4m3fn, jnp.int32
+MESH = pl.DeviceIdType.MESH
+LOW = 256
+ROWS_IN_GROUP = 4
+BAG_PAD = 64
+CHUNK = 256
+NEG_FLOOR = -1e30
+
+
+def dot_as(left, right, left_dim, right_dim):
+    return lax.dot_general(
+        left, right, (((left_dim,), (right_dim,)), ((), ())), preferred_element_type=F32
+    )
+
+
+def iota(shape, dim):
+    return lax.broadcasted_iota(I32, shape, dim)
+
+
+def one_where(mask, kind):
+    return jnp.where(mask, jnp.ones((), BF16), jnp.zeros((), BF16)).astype(kind)
+
+
+def slot_cap(neg_count, batch):
+    mean = neg_count / batch
+    return int(math.ceil((mean + 4.5 * math.sqrt(mean)) / 128.0)) * 128
+
+
+def gelu_and_slope(pre):
+    inner_scale = math.sqrt(2.0 / math.pi)
+    square = pre * pre
+    bent = jnp.tanh(inner_scale * (pre + 0.044715 * (square * pre)))
+    value = 0.5 * pre * (1.0 + bent)
+    slope = 0.5 * (1.0 + bent) + 0.5 * pre * (1.0 - bent * bent) * (
+        inner_scale * (1.0 + 3.0 * 0.044715 * square)
+    )
+    return value, slope
+
+
+def spread_matrix(rows):
+    shape = (rows, 4 * rows)
+    r, m = iota(shape, 0), iota(shape, 1)
+    groups = rows // ROWS_IN_GROUP
+    return one_where((r % groups == m // 16) & (r // groups == m % ROWS_IN_GROUP), BF16)
+
+
+class Sizes:
+    def __init__(self, batch, col, rows, bag, width, vocab, negs, embed):
+        self.batch, self.col, self.rows, self.bag = batch, col, rows, bag
+        self.width, self.vocab, self.negs, self.embed = width, vocab, negs, embed
+        self.total = batch * rows
+        self.quarter = rows // col
+        self.users = batch * self.quarter
+        self.groups = rows // ROWS_IN_GROUP
+        self.high = vocab // LOW
+        self.high_parts = self.high // 4
+        self.cap = slot_cap(negs, batch)
+        self.neg_rows = -(-negs // CHUNK)
+        self.neg_pad = -(-self.neg_rows // 16) * 16
+
+
+def front_kernel(
+    sz,
+    watch_ids, search_ids, extra, neg_ids, demo_table, b_first, b_second, b_third, w_demo,
+    watch_table, search_table, out_table, w_first, w_second, w_third,
+    watch_counts, search_counts, x_out, act1_out, slope1_out, act2_out, slope2_out, gu_out,
+    buckets_out, neg_rows_out, pos_rows_out, slots_out, pos_out, user_out, small_out,
+    tabs, mix, w1, w2, w3, ids, neg_dest, neg_digits, counts, sums, pieces, x, acts1, slopes1,
+    acts2, slopes2, users, buckets, neg_own, neg_all, pos_own, pos_all, e_cols, e_rows, probs,
+    stats, g_send, g_recv, gu, rg_send, rg_recv, loss_all,
+    local_sem, out_sem, count_sem, ids_s, ids_r, rs_s, rs_r, ag_s, ag_r, xx_s, xx_r, co_s, co_r,
+    ne_s, ne_r, pe_s, pe_r, st_s, st_r, gs_s, gs_r, ga_s, ga_r, gx_s, gx_r, gc_s, gc_r,
+    rg_s, rg_r, lo_s, lo_r,
+):
+    b, c = lax.axis_index("batch"), lax.axis_index("col")
+    nb, nc = sz.batch, sz.col
+    offset = b * sz.vocab
+    cap, width, embed = sz.cap, sz.width, sz.embed
+    cx = lax.rem(c + 2, nc)
+    ck = c + 1 - 2 * lax.rem(c, 2)
+
+    def batch_peer(i):
+        return lax.rem(b + i, nb)
+
+    def batch_from(i):
+        return lax.rem(b + nb - i, nb)
+
+    def col_peer(i):
+        return lax.rem(c + i, nc)
+
+    def col_from(i):
+        return lax.rem(c + nc - i, nc)
+
+    def send(src, dst, ssem, rsem, to):
+        return pltpu.make_async_remote_copy(
+            src_ref=src, dst_ref=dst, send_sem=ssem, recv_sem=rsem,
+            device_id=to, device_id_type=MESH,
+        )
+
+    barrier = pltpu.get_barrier_semaphore()
+    for i in range(1, nb):
+        pl.semaphore_signal(barrier, inc=1, device_id=(batch_peer(i), c), device_id_type=MESH)
+    for i in range(1, nc):
+        pl.semaphore_signal(barrier, inc=1, device_id=(b, col_peer(i)), device_id_type=MESH)
+
+    loads = [
+        (out_table, tabs.at[2]), (watch_table, tabs.at[0]), (search_table, tabs.at[1]),
+        (w_second, w2), (w_third, w3), (w_demo, w1.at[pl.ds(nc * 128, 128)]),
+    ]
+    for i in range(nc):
+        loads.append((w_first.at[pl.ds(i * width, width)], w1.at[pl.ds(i * 128, width)]))
+        loads.append((w_first.at[pl.ds(embed + i * width, width)], w1.at[pl.ds(i * 128 + width, width)]))
+    loads = [pltpu.make_async_copy(s, d, local_sem.at[i]) for i, (s, d) in enumerate(loads)]
+    for load in loads:
+        load.start()
+
+    packed = (watch_ids[...] & 0xFFFF) | (search_ids[...] << 16)
+    zero_ids = jnp.zeros((sz.groups + 8, CHUNK), I32)
+    ids[b] = zero_ids
+    for r4 in range(ROWS_IN_GROUP):
+        ids[b, 0 : sz.groups, r4 * BAG_PAD : r4 * BAG_PAD + sz.bag] = packed[
+            r4 * sz.groups : (r4 + 1) * sz.groups, :
+        ]
+    ids[b, sz.groups : sz.groups + 8, 0:128] = extra[...]
+
+    pl.semaphore_wait(barrier, nb - 1 + nc - 1)
+    ids_sends = []
+    for i in range(1, nb):
+        copy = send(ids.at[b], ids.at[b], ids_s.at[i - 1], ids_r.at[i - 1], (batch_peer(i), c))
+        copy.start()
+        ids_sends.append(copy)
+
+    negs = neg_ids[...]
+    neg_local = negs - offset
+    own = (neg_local >= 0) & (neg_local < sz.vocab)
+    own_bf = one_where(own, BF16)
+    pads = sz.neg_pad
+    upper = one_where(iota((CHUNK, CHUNK), 0) < iota((CHUNK, CHUNK), 1), BF16)
+    before = dot_as(own_bf, upper, 1, 0)
+    in_row = dot_as(own_bf, jnp.ones((CHUNK, CHUNK), BF16), 1, 0)
+    lower = one_where(iota((pads, pads), 1) < iota((pads, pads), 0), BF16)
+    rows_before = dot_as(lower, in_row.astype(BF16), 1, 0)
+    neg_dest[...] = jnp.where(own, before + rows_before, -1.0)
+    owned_count = dot_as(jnp.ones((8, pads), BF16), in_row.astype(BF16), 1, 0)
+    most = jnp.zeros((1, 1), F32)
+    for shard in range(nb):
+        part = negs - shard * sz.vocab
+        hits = jnp.where((part >= 0) & (part < sz.vocab), 1.0, 0.0)
+        most = jnp.maximum(most, jnp.sum(jnp.sum(hits, axis=1, keepdims=True), axis=0, keepdims=True))
+    for digit in range(4):
+        neg_digits[digit] = ((neg_local >> (4 * digit)) & 15).astype(F32)
+
+    def compact(k, total):
+        place = neg_dest[pl.ds(k, 1), :]
+        hot = one_where(place == iota((cap, CHUNK), 0).astype(F32), FP8)
+        line = iota((32, CHUNK), 0)
+        value = jnp.where(line == 4, 1.0, 0.0)
+        for digit in range(4):
+            value = jnp.where(line == digit, neg_digits[digit, pl.ds(k, 1), :], value)
+        return total + dot_as(value.astype(FP8), hot, 1, 1)
+
+    slot = lax.fori_loop(0, sz.neg_rows, compact, jnp.zeros((32, cap), F32))
+    neg_low = slot[0:1] + 16.0 * slot[1:2]
+    neg_high = jnp.where(slot[4:5] > 0.5, slot[2:3] + 16.0 * slot[3:4], -1.0)
+
+    def pick_columns(high_row, low_row, count):
+        low_hot = one_where(low_row.astype(BF16) == iota((LOW, count), 0).astype(BF16), BF16)
+
+        def part(hq, total):
+            base = pl.multiple_of(hq * 4 * LOW, 4 * LOW)
+            left = jnp.concatenate(
+                [tabs[2, :, pl.ds(base + i * LOW, LOW)] for i in range(4)], axis=0
+            )
+            got = dot_as(left, low_hot, 1, 0)
+            for i in range(4):
+                at = (hq * 4 + i).astype(F32)
+                total = total + jnp.where(high_row == at, got[i * width : (i + 1) * width], 0.0)
+            return total
+
+        return lax.fori_loop(0, sz.high_parts, part, jnp.zeros((width, count), F32)).astype(BF16)
+
+    loads[0].wait()
+    neg_own[...] = pick_columns(neg_high, neg_low, cap)
+    neg_all[c] = neg_own[...]
+    e_sends = []
+    for i in range(1, nc):
+        copy = send(neg_own, neg_all.at[c], ne_s.at[i - 1], ne_r.at[i - 1], (b, col_peer(i)))
+        copy.start()
+        e_sends.append(copy)
+
+    for t in range(2):
+        loads[1 + t].wait()
+
+        def turn(hh, _):
+            base = pl.multiple_of(hh * 4 * LOW, 4 * LOW)
+            tall = jnp.concatenate([tabs[t, :, pl.ds(base + i * LOW, LOW)] for i in range(4)], axis=0)
+            mix[t, pl.ds(pl.multiple_of(hh * LOW, LOW), LOW), :] = tall.T
+            return 0
+
+        lax.fori_loop(0, sz.high_parts, turn, 0)
+
+    for i in range(1, nb):
+        src = batch_from(i)
+        send(ids.at[src], ids.at[src], ids_s.at[i - 1], ids_r.at[i - 1], (b, c)).wait_recv()
+
+    pos_ids = jnp.concatenate([ids[j, sz.groups : sz.groups + 1, 0:128] for j in range(nb)], axis=0)
+    valid = jnp.concatenate([ids[j, sz.groups + 1 : sz.groups + 2, 0:128] for j in range(nb)], axis=0)
+    pos_local = pos_ids - offset
+    pos_owned = (pos_local >= 0) & (pos_local < sz.vocab)
+    pos_pair = jnp.concatenate(
+        [
+            jnp.where(pos_owned, pos_local >> 8, 255).astype(F32),
+            (pos_local & 255).astype(F32),
+        ],
+        axis=0,
+    ).astype(BF16)
+    shape = (128, sz.total)
+    lane = iota(shape, 1)
+    pick = one_where(
+        iota(shape, 0) == (lane // sz.users) * sz.quarter + lane % sz.quarter, BF16
+    )
+    pos_wide = dot_as(pos_pair, pick, 1, 0)
+    shape = (nb, sz.total)
+    at_block = (iota(shape, 1) // sz.quarter) % nb == iota(shape, 0)
+    pos_high = jnp.sum(jnp.where(at_block, pos_wide[0:nb], 0.0), axis=0, keepdims=True)
+    pos_low = jnp.sum(jnp.where(at_block, pos_wide[nb : 2 * nb], 0.0), axis=0, keepdims=True)
+    pos_high = jnp.where(pos_high > 254.0, -1.0, pos_high)
+
+    slots_out[...] = jnp.concatenate([neg_high, neg_low, jnp.zeros((6, cap), F32)], axis=0)
+    pos_out[...] = jnp.concatenate([pos_high, pos_low, jnp.zeros((6, sz.total), F32)], axis=0)
+
+    for quarter in range(nc):
+        lanes = slice(quarter * sz.users, (quarter + 1) * sz.users)
+        pos_own[quarter] = pick_columns(pos_high[:, lanes], pos_low[:, lanes], sz.users)
+    pos_all[c] = pos_own[c]
+    for i in range(1, nc):
+        to = col_peer(i)
+        copy = send(pos_own.at[to], pos_all.at[c], pe_s.at[i - 1], pe_r.at[i - 1], (b, to))
+        copy.start()
+        e_sends.append(copy)
+
+    shape = (nb, sz.users)
+    user_block = iota(shape, 1) // sz.quarter == iota(shape, 0)
+    valid_wide = jnp.concatenate([valid] * (sz.users // 128), axis=1).astype(F32)
+    live_count = jnp.sum(jnp.where(user_block, valid_wide, 0.0), axis=0, keepdims=True)
+    valid_total = jnp.sum(valid_wide, axis=0, keepdims=True)
+    user_place = c * sz.quarter + iota((1, sz.users), 1) % sz.quarter
+    weight = jnp.where(user_place.astype(F32) < live_count, 1.0 / valid_total, 0.0)
+
+    bucket_total = jnp.zeros((demo_table.shape[0], sz.total), BF16)
+    bucket_line = iota((demo_table.shape[0], sz.total), 0).astype(BF16)
+    for field in range(4):
+        row = sz.groups + 2 + field
+        line = jnp.concatenate([ids[j, row : row + 1, 0:128] for j in range(nb)], axis=1)
+        bucket_total = bucket_total + one_where(line.astype(F32).astype(BF16) == bucket_line, BF16)
+    buckets[...] = bucket_total
+    x[:, nc * 128 :] = dot_as(bucket_total, demo_table[...], 0, 0).astype(BF16)
+    buckets_copy = pltpu.make_async_copy(buckets, buckets_out, out_sem.at[0])
+    buckets_copy.start()
+
+    for load in loads[3:]:
+        load.wait()
+
+    spread = spread_matrix(sz.rows)
+    piece = sz.rows // nb
+    block_lines = 4 * sz.rows
+    lane_mod = iota((16, CHUNK), 1) % BAG_PAD
+    lane_r4 = iota((16, CHUNK), 1) // BAG_PAD
+
+    def count_copy(t, table, slot_at):
+        out = (watch_counts, search_counts)[table]
+        return pltpu.make_async_copy(counts.at[table, slot_at], out.at[t], count_sem.at[table, slot_at])
+
+    def bag_block(t):
+        slot_at = lax.rem(t, 2)
+        results = []
+        for table in range(2):
+
+            @pl.when(t >= 2)
+            def _():
+                count_copy(t - 2, table, slot_at).wait()
+
+            code_line = iota((4 * sz.high, CHUNK), 0).astype(BF16)
+            low_line = iota((LOW, CHUNK), 0).astype(BF16)
+
+            def groups_of(q, _):
+                word = ids[t, pl.ds(pl.multiple_of(q * 16, 16), 16), :]
+                value = (word & 0xFFFF) if table == 0 else lax.shift_right_logical(word, 16)
+                local = value - offset
+                mine = (local >= 0) & (local < sz.vocab) & (lane_mod < sz.bag)
+                code = jnp.where(mine, (local >> 8) * 4 + lane_r4, -1).astype(F32).astype(BF16)
+                low = (local & 255).astype(F32).astype(BF16)
+                for g in range(16):
+                    left = one_where(code[g : g + 1, :] == code_line, FP8)
+                    right = one_where(low[g : g + 1, :] == low_line, FP8)
+                    found = dot_as(left, right, 1, 1).astype(BF16)
+                    line = pl.ds(pl.multiple_of(q * 256 + g * 16, 16), 16)
+                    for hh in range(sz.high_parts):
+                        counts[table, slot_at, line, hh * LOW : (hh + 1) * LOW] = found[
+                            hh * 16 : (hh + 1) * 16, :
+                        ]
+                return 0
+
+            lax.fori_loop(0, sz.groups // 16, groups_of, 0)
+            count_copy(t, table, slot_at).start()
+            total = dot_as(counts[table, slot_at], mix[table], 1, 0)
+            shape = (block_lines, 4 * width)
+            total = jnp.where((iota(shape, 0) // 4) % 4 == iota(shape, 1) // width, total, 0.0)
+            half = total[:, :128] + total[:, 128:]
+            half = half + pltpu.roll(half, width, 1)
+            top = half.astype(BF16)
+            rest = (half - top.astype(F32)).astype(BF16)
+            both = jnp.where(iota((block_lines, 128), 1) < width, top, rest)
+            found = dot_as(spread, both, 1, 0)
+            results.append(found + pltpu.roll(found, width, 1))
+        joined = jnp.where(iota((sz.rows, 128), 1) < width, results[0], results[1])
+        sums[t] = joined.astype(BF16)
+        for i in range(1, nb):
+            to = batch_peer(i)
+            send(
+                sums.at[t, pl.ds(pl.multiple_of(to * piece, piece), piece)], pieces.at[t, i - 1],
+                rs_s.at[t, i - 1], rs_r.at[t], (to, c),
+            ).start()
+
+    def x_at(t, col):
+        return x.at[
+            pl.ds(pl.multiple_of(t * sz.rows, sz.rows), sz.rows),
+            pl.ds(pl.multiple_of(col * 128, 128), 128),
+        ]
+
+    def x_piece(t, owner):
+        return x.at[
+            pl.ds(pl.multiple_of(t * sz.rows + owner * piece, piece), piece),
+            pl.ds(pl.multiple_of(c * 128, 128), 128),
+        ]
+
+    def reduce_block(t):
+        send(pieces.at[t], pieces.at[t], rs_s.at[t, 0], rs_r.at[t], (b, c)).wait_recv()
+        total = sums[t, pl.ds(pl.multiple_of(b * piece, piece), piece), :].astype(F32)
+        for i in range(nb - 1):
+            total = total + pieces[t, i].astype(F32)
+        x[
+            pl.ds(pl.multiple_of(t * sz.rows + b * piece, piece), piece),
+            pl.ds(pl.multiple_of(c * 128, 128), 128),
+        ] = (total / sz.bag).astype(BF16)
+        for i in range(1, nb):
+            send(x_piece(t, b), x_piece(t, b), ag_s.at[t, i - 1], ag_r.at[t], (batch_peer(i), c)).start()
+
+    def cross_block(t):
+        send(pieces.at[t], pieces.at[t], ag_s.at[t, 0], ag_r.at[t], (b, c)).wait_recv()
+        send(x_at(t, c), x_at(t, c), xx_s.at[t], xx_r.at[t], (b, cx)).start()
+
+    def core_block(t):
+        send(x_at(t, cx), x_at(t, cx), xx_s.at[t], xx_r.at[t], (b, cx)).wait_recv()
+        send(x_at(t, c), x_at(t, c), co_s.at[t, 0], co_r.at[t, 0], (b, ck)).start()
+        send(x_at(t, cx), x_at(t, cx), co_s.at[t, 1], co_r.at[t, 1], (b, ck)).start()
+
+    def full_block(t):
+        ckx = lax.rem(ck + 2, nc)
+        send(x_at(t, ck), x_at(t, ck), co_s.at[t, 0], co_r.at[t, 0], (b, ck)).wait_recv()
+        send(x_at(t, ckx), x_at(t, ckx), co_s.at[t, 1], co_r.at[t, 1], (b, ck)).wait_recv()
+
+    tower_rows = sz.total // 4
+
+    def tower(k):
+        at = pl.ds(pl.multiple_of(k * tower_rows, tower_rows), tower_rows)
+        pre = dot_as(x[at, :], w1[...], 1, 0) + b_first[...]
+        value, slope = gelu_and_slope(pre)
+        value = value.astype(BF16)
+        acts1[at, :] = value
+        slopes1[at, :] = slope.astype(BF16)
+        pre = dot_as(value, w2[...], 1, 0) + b_second[...]
+        value, slope = gelu_and_slope(pre)
+        value = value.astype(BF16)
+        acts2[at, :] = value
+        slopes2[at, :] = slope.astype(BF16)
+        users[at, :] = (dot_as(value, w3[...], 1, 0) + b_third[...]).astype(BF16)
+
+    def step(t, _):
+        @pl.when(t < nb)
+        def _():
+            bag_block(t)
+
+        @pl.when((t >= 1) & (t < nb + 1))
+        def _():
+            reduce_block(t - 1)
+
+        @pl.when((t >= 2) & (t < nb + 2))
+        def _():
+            cross_block(t - 2)
+
+        @pl.when((t >= 3) & (t < nb + 3))
+        def _():
+            core_block(t - 3)
+
+        @pl.when(t >= 4)
+        def _():
+            full_block(t - 4)
+
+        @pl.when(t >= nb)
+        def _():
+            tower(t - nb)
+
+        return 0
+
+    lax.fori_loop(0, nb + 4, step, 0)
+
+    out_copies = [(x, x_out), (acts1, act1_out), (slopes1, slope1_out), (acts2, act2_out), (slopes2, slope2_out)]
+    out_copies = [pltpu.make_async_copy(s, d, out_sem.at[1 + i]) for i, (s, d) in enumerate(out_copies)]
+    for copy in out_copies:
+        copy.start()
+    user_out[...] = users[pl.ds(pl.multiple_of(b * sz.rows + c * sz.quarter, sz.quarter), sz.quarter), :]
+
+    for i in range(1, nc):
+        src = col_from(i)
+        send(neg_all.at[src], neg_all.at[src], ne_s.at[i - 1], ne_r.at[i - 1], (b, c)).wait_recv()
+        send(pos_all.at[src], pos_all.at[src], pe_s.at[i - 1], pe_r.at[i - 1], (b, c)).wait_recv()
+    for i in range(nc):
+        e_cols[i * width : (i + 1) * width, 0:cap] = neg_all[i]
+        e_cols[i * width : (i + 1) * width, cap:] = pos_all[i]
+    e_rows[...] = e_cols[...].T
+
+    quarter_users = jnp.concatenate(
+        [
+            users[pl.ds(pl.multiple_of(j * sz.rows + c * sz.quarter, sz.quarter), sz.quarter), :]
+            for j in range(nb)
+        ],
+        axis=0,
+    )
+    logits = dot_as(e_rows[...], quarter_users, 1, 1)
+    neg_logits, pos_logits = logits[0:cap], logits[cap:]
+    slot_ok = iota((cap, sz.users), 0).astype(F32) < owned_count[0:1, : sz.users]
+    pos_here = jnp.zeros((1, sz.users), F32)
+    for quarter in range(nc):
+        pos_here = jnp.where(c == quarter, pos_high[:, quarter * sz.users : (quarter + 1) * sz.users], pos_here)
+    pos_ok = (iota((sz.users, sz.users), 0) == iota((sz.users, sz.users), 1)) & (pos_here >= 0.0)
+    neg_logits = jnp.where(slot_ok, neg_logits, NEG_FLOOR)
+    pos_masked = jnp.where(pos_ok, pos_logits, NEG_FLOOR)
+    peak = jnp.maximum(
+        jnp.max(neg_logits, axis=0, keepdims=True), jnp.max(pos_masked, axis=0, keepdims=True)
+    )
+    mass = jnp.sum(jnp.where(slot_ok, jnp.exp(neg_logits - peak), 0.0), axis=0, keepdims=True) + jnp.sum(
+        jnp.where(pos_ok, jnp.exp(pos_masked - peak), 0.0), axis=0, keepdims=True
+    )
+    pos_value = jnp.sum(jnp.where(pos_ok, pos_logits, 0.0), axis=0, keepdims=True)
+    stats[b] = jnp.concatenate([peak, mass, pos_value, jnp.zeros((5, sz.users), F32)], axis=0)
+    st_sends = []
+    for i in range(1, nb):
+        copy = send(stats.at[b], stats.at[b], st_s.at[i - 1], st_r.at[i - 1], (batch_peer(i), c))
+        copy.start()
+        st_sends.append(copy)
+    for i in range(1, nb):
+        src = batch_from(i)
+        send(stats.at[src], stats.at[src], st_s.at[i - 1], st_r.at[i - 1], (b, c)).wait_recv()
+    peaks = [stats[j, 0:1, :] for j in range(nb)]
+    top = peaks[0]
+    for j in range(1, nb):
+        top = jnp.maximum(top, peaks[j])
+    full_mass = jnp.zeros((1, sz.users), F32)
+    pos_logit = jnp.zeros((1, sz.users), F32)
+    for j in range(nb):
+        full_mass = full_mass + stats[j, 1:2, :] * jnp.exp(peaks[j] - top)
+        pos_logit = pos_logit + stats[j, 2:3, :]
+    lse = top + jnp.log(full_mass)
+    loss_part = jnp.sum(weight * (lse - pos_logit), axis=1, keepdims=True)
+    scale = weight / full_mass
+    neg_grad = jnp.where(slot_ok, jnp.exp(neg_logits - top) * scale, 0.0).astype(BF16)
+    pos_grad = jnp.where(
+        pos_ok, weight * (jnp.exp(pos_logit - top) / full_mass - 1.0), 0.0
+    ).astype(BF16)
+    probs[0:cap] = neg_grad
+    probs[cap:] = pos_grad
+    grad_user = dot_as(probs[...], e_rows[...], 0, 0)
+    for j in range(nb):
+        g_send[j] = grad_user[j * sz.quarter : (j + 1) * sz.quarter].astype(BF16)
+    gs_sends = []
+    for i in range(1, nb):
+        to = batch_peer(i)
+        copy = send(g_send.at[to], g_recv.at[i - 1], gs_s.at[i - 1], gs_r.at[i - 1], (to, c))
+        copy.start()
+        gs_sends.append(copy)
+    loss_all[c] = jnp.broadcast_to(loss_part, (8, 128))
+    for i in range(1, nc):
+        copy = send(loss_all.at[c], loss_all.at[c], lo_s.at[i - 1], lo_r.at[i - 1], (b, col_peer(i)))
+        copy.start()
+        gs_sends.append(copy)
+    rows_grad = dot_as(probs[...], quarter_users, 1, 0)
+    rows_grad = rows_grad.T.astype(BF16)
+    for i in range(nc):
+        rg_send[i] = rows_grad[i * width : (i + 1) * width]
+    for i in range(1, nb):
+        send(g_send.at[0], g_recv.at[i - 1], gs_s.at[i - 1], gs_r.at[i - 1], (b, c)).wait_recv()
+    total = g_send[b].astype(F32)
+    for i in range(nb - 1):
+        total = total + g_recv[i].astype(F32)
+    mine_rows = pl.ds(pl.multiple_of(c * sz.quarter, sz.quarter), sz.quarter)
+    gu[b, mine_rows, :] = total.astype(BF16)
+    for i in range(1, nb):
+        place = gu.at[b, mine_rows]
+        copy = send(place, place, ga_s.at[i - 1], ga_r.at[i - 1], (batch_peer(i), c))
+        copy.start()
+        gs_sends.append(copy)
+    for i in range(1, nc):
+        to = col_peer(i)
+        copy = send(rg_send.at[to], rg_recv.at[c], rg_s.at[i - 1], rg_r.at[i - 1], (b, to))
+        copy.start()
+        gs_sends.append(copy)
+    rg_recv[c] = rg_send[c]
+    for i in range(1, nb):
+        place = gu.at[batch_from(i), mine_rows]
+        send(place, place, ga_s.at[i - 1], ga_r.at[i - 1], (b, c)).wait_recv()
+
+    def gu_at(col):
+        return gu.at[:, pl.ds(pl.multiple_of(col * sz.quarter, sz.quarter), sz.quarter), :]
+
+    copy = send(gu_at(c), gu_at(c), gx_s, gx_r, (b, cx))
+    copy.start()
+    gs_sends.append(copy)
+    send(gu_at(cx), gu_at(cx), gx_s, gx_r, (b, cx)).wait_recv()
+    for i, col in enumerate((c, cx)):
+        copy = send(gu_at(col), gu_at(col), gc_s.at[i], gc_r.at[i], (b, ck))
+        copy.start()
+        gs_sends.append(copy)
+    for i, col in enumerate((ck, lax.rem(ck + 2, nc))):
+        send(gu_at(col), gu_at(col), gc_s.at[i], gc_r.at[i], (b, ck)).wait_recv()
+    gu_copy = pltpu.make_async_copy(gu, gu_out, out_sem.at[6])
+    gu_copy.start()
+
+    loss = loss_all[c] * 1.0
+    for i in range(1, nc):
+        src = col_from(i)
+        send(loss_all.at[src], loss_all.at[src], lo_s.at[i - 1], lo_r.at[i - 1], (b, c)).wait_recv()
+        send(rg_recv.at[src], rg_recv.at[src], rg_s.at[i - 1], rg_r.at[i - 1], (b, c)).wait_recv()
+    loss = loss_all[0]
+    neg_total = rg_recv[0, :, 0:cap].astype(F32)
+    for i in range(1, nc):
+        loss = loss + loss_all[i]
+        neg_total = neg_total + rg_recv[i, :, 0:cap].astype(F32)
+    neg_rows_out[...] = neg_total.astype(BF16)
+    for i in range(nc):
+        pos_rows_out[:, i * sz.users : (i + 1) * sz.users] = rg_recv[i, :, cap:]
+    fits = jnp.where(most <= float(cap), 1.0, 0.0)
+    line = iota((8, 128), 0)
+    small_out[...] = jnp.where(line == 0, loss, jnp.broadcast_to(fits, (8, 128)))
+
+    for copy in ids_sends + e_sends + st_sends + gs_sends:
+        copy.wait_send()
+
+    def drain(t, _):
+        for i in range(1, nb):
+            send(sums.at[t, pl.ds(0, piece)], pieces.at[t, 0], rs_s.at[t, i - 1], rs_r.at[t], (b, c)).wait_send()
+            send(x_piece(t, b), x_piece(t, b), ag_s.at[t, i - 1], ag_r.at[t], (b, c)).wait_send()
+        send(x_at(t, c), x_at(t, c), xx_s.at[t], xx_r.at[t], (b, cx)).wait_send()
+        send(x_at(t, c), x_at(t, c), co_s.at[t, 0], co_r.at[t, 0], (b, ck)).wait_send()
+        send(x_at(t, cx), x_at(t, cx), co_s.at[t, 1], co_r.at[t, 1], (b, ck)).wait_send()
+        return 0
+
+    lax.fori_loop(0, nb, drain, 0)
+    for table in range(2):
+        count_copy(nb - 2, table, nb % 2).wait()
+        count_copy(nb - 1, table, (nb - 1) % 2).wait()
+    buckets_copy.wait()
+    gu_copy.wait()
+    for copy in out_copies:
+        copy.wait()
+
+
+def front(sz, args):
+    nb, nc, total = sz.batch, sz.col, sz.total
+    width, embed, cap, users = sz.width, sz.embed, sz.cap, sz.users
+    slots = cap + users
+    first, second = args["w_second"].shape
+    buckets = args["demo_table"].shape[0]
+    x_width = nc * 128 + 128
+    lines = 4 * sz.rows
+    vmem = pl.BlockSpec(memory_space=pltpu.VMEM)
+    hbm = pl.BlockSpec(memory_space=pl.ANY)
+    dma = pltpu.SemaphoreType.DMA
+    count_shape = jax.ShapeDtypeStruct((nb, lines, sz.high_parts * LOW), BF16)
+
+    def shape(dims, kind=BF16):
+        return jax.ShapeDtypeStruct(dims, kind)
+
+    outs = [
+        (count_shape, hbm), (count_shape, hbm), (shape((total, x_width)), hbm),
+        (shape((total, first)), hbm), (shape((total, first)), hbm),
+        (shape((total, second)), hbm), (shape((total, second)), hbm),
+        (shape((nb, sz.rows, embed)), hbm), (shape((buckets, total)), hbm),
+        (shape((width, cap)), vmem), (shape((width, total)), vmem),
+        (shape((8, cap), F32), vmem), (shape((8, total), F32), vmem),
+        (shape((sz.quarter, embed)), vmem), (shape((8, 128), F32), vmem),
+    ]
+    scratch = [
+        pltpu.VMEM((3, width, sz.vocab), BF16),
+        pltpu.VMEM((2, sz.high_parts * LOW, 4 * width), BF16),
+        pltpu.VMEM((x_width, first), BF16),
+        pltpu.VMEM((first, second), BF16),
+        pltpu.VMEM((second, embed), BF16),
+        pltpu.VMEM((nb, sz.groups + 8, CHUNK), I32),
+        pltpu.VMEM((sz.neg_pad, CHUNK), F32),
+        pltpu.VMEM((4, sz.neg_pad, CHUNK), F32),
+        pltpu.VMEM((2, 2, lines, sz.high_parts * LOW), BF16),
+        pltpu.VMEM((nb, sz.rows, 128), BF16),
+        pltpu.VMEM((nb, nb - 1, sz.rows // nb, 128), BF16),
+        pltpu.VMEM((total, x_width), BF16),
+        pltpu.VMEM((total, first), BF16),
+        pltpu.VMEM((total, first), BF16),
+        pltpu.VMEM((total, second), BF16),
+        pltpu.VMEM((total, second), BF16),
+        pltpu.VMEM((total, embed), BF16),
+        pltpu.VMEM((buckets, total), BF16),
+        pltpu.VMEM((width, cap), BF16),
+        pltpu.VMEM((nc, width, cap), BF16),
+        pltpu.VMEM((nc, width, users), BF16),
+        pltpu.VMEM((nc, width, users), BF16),
+        pltpu.VMEM((embed, slots), BF16),
+        pltpu.VMEM((slots, embed), BF16),
+        pltpu.VMEM((slots, users), BF16),
+        pltpu.VMEM((nb, 8, users), F32),
+        pltpu.VMEM((nb, sz.quarter, embed), BF16),
+        pltpu.VMEM((nb - 1, sz.quarter, embed), BF16),
+        pltpu.VMEM((nb, sz.rows, embed), BF16),
+        pltpu.VMEM((nc, width, slots), BF16),
+        pltpu.VMEM((nc, width, slots), BF16),
+        pltpu.VMEM((nc, 8, 128), F32),
+        dma((6 + 2 * nc,)), dma((7,)), dma((2, 2)),
+        dma((nb - 1,)), dma((nb - 1,)),
+        dma((nb, nb - 1)), dma((nb,)), dma((nb, nb - 1)), dma((nb,)),
+        dma((nb,)), dma((nb,)), dma((nb, 2)), dma((nb, 2)),
+        dma((nc - 1,)), dma((nc - 1,)), dma((nc - 1,)), dma((nc - 1,)),
+        dma((nb - 1,)), dma((nb - 1,)), dma((nb - 1,)), dma((nb - 1,)),
+        dma((nb - 1,)), dma((nb - 1,)), dma, dma, dma((2,)), dma((2,)),
+        dma((nc - 1,)), dma((nc - 1,)), dma((nc - 1,)), dma((nc - 1,)),
+    ]
+    rows = args["watch_ids"].shape[0]
+    extra = jnp.concatenate(
+        [
+            args["pos_ids"][None, :],
+            jnp.broadcast_to(args["valid_counts"][:, None], (1, rows)),
+            args["demo_ids"].T,
+            jnp.zeros((8 - 2 - args["demo_ids"].shape[1], rows), I32),
+        ],
+        axis=0,
+    )
+    pad = sz.neg_pad * CHUNK - sz.negs
+    negs = jnp.concatenate([args["neg_ids"], jnp.full((pad,), -1, I32)]).reshape(sz.neg_pad, CHUNK)
+    demo_width = args["demo_table"].shape[1]
+    demo = jnp.pad(args["demo_table"], ((0, 0), (0, 128 - demo_width)))
+    w_demo = jnp.pad(args["w_first"][2 * embed :], ((0, 128 - demo_width), (0, 0)))
+    operands = [
+        (args["watch_ids"], vmem), (args["search_ids"], vmem), (extra, vmem), (negs, vmem), (demo, vmem),
+        (args["b_first"][None, :], vmem), (args["b_second"][None, :], vmem), (args["b_third"][None, :], vmem),
+        (w_demo, hbm), (args["watch_table"], hbm), (args["search_table"], hbm), (args["out_table"], hbm),
+        (args["w_first"], hbm), (args["w_second"], hbm), (args["w_third"], hbm),
+    ]
+    return pl.pallas_call(
+        functools.partial(front_kernel, sz),
+        out_shape=[o for o, _ in outs],
+        in_specs=[s for _, s in operands],
+        out_specs=[s for _, s in outs],
+        scratch_shapes=scratch,
+        compiler_params=pltpu.CompilerParams(
+            collective_id=0, has_side_effects=True, vmem_limit_bytes=60 * 2**20
+        ),
+        name="front",
+    )(*[o for o, _ in operands])
+
+
+def back_kernel(
+    sz, grads, neg_rows, pos_rows, slots, pos, watch_counts, search_counts,
+    watch_out, search_out, table_out, spread_grads, chunk, lines, in_sem, out_sem,
+):
+    width, cap, total = sz.width, sz.cap, sz.total
+    parts, nb = sz.high_parts, sz.batch
+    outs = (watch_out, search_out)
+    ins = (watch_counts, search_counts)
+    depth = 3
+
+    def load(n):
+        table, hh = n // parts, n % parts
+        source = ins[table].at[:, :, pl.ds(hh * LOW, LOW)]
+        return pltpu.make_async_copy(source, chunk.at[n % depth], in_sem.at[n % depth])
+
+    def store(n):
+        out = outs[n // parts] if n < 2 * parts else table_out
+        hh = n % parts
+        return pltpu.make_async_copy(
+            lines.at[n % 2], out.at[:, pl.ds(hh * 4 * LOW, 4 * LOW)], out_sem.at[n % 2]
+        )
+
+    for n in range(depth):
+        load(n).start()
+
+    spread = spread_matrix(sz.rows)
+    shape = (4 * width, 4 * sz.rows)
+    mask = iota(shape, 0) // width == (iota(shape, 1) // 4) % 4
+    for table in range(2):
+        for t in range(nb):
+            part = grads[t * sz.rows : (t + 1) * sz.rows, table * width : (table + 1) * width]
+            wide = jnp.concatenate([part] * 4, axis=1)
+            laid = dot_as(wide, spread, 0, 0)
+            spread_grads[table, :, t * 4 * sz.rows : (t + 1) * 4 * sz.rows] = jnp.where(
+                mask, laid, 0.0
+            ).astype(BF16)
+
+    def put(n, found, factor):
+        if n >= 2:
+            store(n - 2).wait()
+        for i in range(4):
+            lines[n % 2, :, i * LOW : (i + 1) * LOW] = found[i * width : (i + 1) * width] * factor
+        store(n).start()
+
+    for n in range(2 * parts):
+        table = n // parts
+        load(n).wait()
+        stacked = chunk[n % depth].reshape(nb * 4 * sz.rows, LOW)
+        found = dot_as(spread_grads[table], stacked, 1, 0)
+        if n + depth < 2 * parts:
+            load(n + depth).start()
+        put(n, found, 1.0 / sz.bag)
+
+    high = jnp.concatenate([slots[0:1, :], pos[0:1, :]], axis=1)
+    low = jnp.concatenate([slots[1:2, :], pos[1:2, :]], axis=1)
+    values = jnp.concatenate([neg_rows[...], pos_rows[...]], axis=1)
+    low_hot = one_where(low.astype(BF16) == iota((LOW, cap + total), 0).astype(BF16), BF16)
+    for hh in range(parts):
+        left = jnp.concatenate(
+            [jnp.where(high == float(hh * 4 + i), values, jnp.zeros((), BF16)) for i in range(4)], axis=0
+        )
+        put(2 * parts + hh, dot_as(left, low_hot, 1, 1), 1.0)
+    store(3 * parts - 2).wait()
+    store(3 * parts - 1).wait()
+
+
+def back(sz, grads, neg_rows, pos_rows, slots, pos, watch_counts, search_counts):
+    vmem = pl.BlockSpec(memory_space=pltpu.VMEM)
+    hbm = pl.BlockSpec(memory_space=pl.ANY)
+    table = jax.ShapeDtypeStruct((sz.width, sz.vocab), F32)
+    lines = 4 * sz.rows
+    return pl.pallas_call(
+        functools.partial(back_kernel, sz),
+        out_shape=[table] * 3,
+        in_specs=[vmem] * 5 + [hbm] * 2,
+        out_specs=[hbm] * 3,
+        scratch_shapes=[
+            pltpu.VMEM((2, 4 * sz.width, sz.batch * lines), BF16),
+            pltpu.VMEM((3, sz.batch, lines, LOW), BF16),
+            pltpu.VMEM((2, sz.width, 4 * LOW), F32),
+            pltpu.SemaphoreType.DMA((3,)),
+            pltpu.SemaphoreType.DMA((2,)),
+        ],
+        compiler_params=pltpu.CompilerParams(vmem_limit_bytes=56 * 2**20),
+        name="back",
+    )(grads, neg_rows, pos_rows, slots, pos, watch_counts, search_counts)
+
+
+def fast_device(sz, *inputs):
+    names = (
+        "watch_ids", "search_ids", "demo_ids", "pos_ids", "neg_ids", "valid_counts", "watch_table",
+        "search_table", "demo_table", "out_table", "w_first", "b_first", "w_second", "b_second",
+        "w_third", "b_third",
+    )
+    args = dict(zip(names, inputs))
+    (
+        watch_counts, search_counts, x, act1, slope1, act2, slope2, gu, buckets,
+        neg_rows, pos_rows, slots, pos, user_vecs, small,
+    ) = front(sz, args)
+
+    def finish(*operands):
+        nc, width, embed, total = sz.col, sz.width, sz.embed, sz.total
+        w_first, w_second, w_third = args["w_first"], args["w_second"], args["w_third"]
+        demo_width = args["demo_table"].shape[1]
+        start = lax.axis_index("col") * width
+        gu_rows = gu.reshape(total, embed)
+        grad_second = (contract_cols(gu_rows, w_third) * slope2.astype(F32)).astype(BF16)
+        grad_first = (contract_cols(grad_second, w_second) * slope1.astype(F32)).astype(BF16)
+        picked = jnp.concatenate(
+            [
+                lax.dynamic_slice_in_dim(w_first, start, width, 0),
+                lax.dynamic_slice_in_dim(w_first, embed + start, width, 0),
+                w_first[2 * embed :],
+            ],
+            axis=0,
+        )
+        grad_x = contract_cols(grad_first, picked).astype(BF16)
+        tables = back(
+            sz, grad_x[:, : 2 * width], neg_rows, pos_rows, slots, pos, watch_counts, search_counts
+        )
+        pairs = x[:, : nc * 128].reshape(total, nc, 2, width).transpose(0, 2, 1, 3)
+        joined = jnp.concatenate(
+            [pairs.reshape(total, 2 * embed), x[:, nc * 128 : nc * 128 + demo_width]], axis=1
+        )
+        grad_demo = jnp.dot(buckets, grad_x[:, 2 * width :], preferred_element_type=F32)
+        return (
+            user_vecs,
+            small[0, 0],
+            tables[0],
+            tables[1],
+            tables[2],
+            grad_demo,
+            contract_rows(joined, grad_first),
+            jnp.sum(grad_first.astype(F32), axis=0),
+            contract_rows(act1, grad_second),
+            jnp.sum(grad_second.astype(F32), axis=0),
+            contract_rows(act2, gu_rows),
+            jnp.sum(gu_rows.astype(F32), axis=0),
+        )
+
+    def general(*operands):
+        return per_device(*operands)
+
+    return lax.cond(small[1, 0] > 0.5, finish, general, *inputs)
+
+
+def fast_sizes(mesh, shapes):
+    watch, demo, negs, table, first = shapes
+    batch, col = mesh.shape["batch"], mesh.shape["col"]
+    rows, width, vocab = watch[0] // batch, table[0] // col, table[1] // batch
+    sz = Sizes(batch, col, rows, watch[1], width, vocab, negs[0], table[0])
+    good = (
+        batch == 8 and col == 4 and rows == 128 and watch[1] <= BAG_PAD and width == 64
+        and vocab == 32 * LOW and table[1] <= 65536 and demo[1] <= 4 and first[0] <= 2 * table[0] + 128
+        and negs[0] <= 256 * CHUNK
+    )
+    return sz if good else None
+
+
 def solution(mesh):
     in_specs = (
         P("batch", None),
@@ -267,6 +1097,13 @@
         P(),
         P(),
     )
-    return jax.shard_map(
-        per_device, mesh=mesh, in_specs=in_specs, out_specs=out_specs, check_vma=False
-    )
+
+    def whole(*inputs):
+        shapes = [inputs[i].shape for i in (0, 2, 4, 6, 10)]
+        sz = fast_sizes(mesh, shapes)
+        body = per_device if sz is None else functools.partial(fast_device, sz)
+        return jax.shard_map(
+            body, mesh=mesh, in_specs=in_specs, out_specs=out_specs, check_vma=False
+        )(*inputs)
+
+    return whole

time: 651 us -> 179 us (0.27); the launches traced: 643 us -> 178 us
  blocking collectives: 272 us -> 0 us
  matrix products: 176 us -> 16.6 us
  Pallas kernels: 0 us -> 121 us
  waiting for transfers between devices: 96.7 us -> 0 us
  other arithmetic: 38.9 us -> 1.5 us
  local copies, waits for them, and re-layouts: 42.4 us -> 22.3 us
    all_gather x9 -> x0, blocking collectives: 189 us -> none  [the longest x1 34.1 us: per_device(): lax.all_gather(pos_bf, 'col', axis=0, tiled=True)]
    dot_general x10 -> x1, matrix products: 130 us -> 0.93 us  [finish(): jnp.dot(buckets, grad_x[:, 2 * width:], preferred_element_type=F32)]
    pallas_call x0 -> x2, Pallas kernels: none -> 121 us  [the longest x1 92.5 us: front(): pl.pallas_call(functools.partial(front_kernel, sz), out_shape=[o for o, _...]
    psum x1 -> x0, waiting for transfers between devices: 93.6 us -> none  [per_device(): lax.psum((grad_w_first, grad_b_first, grad_w_second, grad_b_second, grad_...]
    psum x2 -> x0, blocking collectives: 83 us -> none  [the longest x1 63.6 us: per_device(): lax.psum((neg_part, jnp.sum(valid_counts).astype(jnp.float32)), 'batch')]
    scatter-add x1 -> x0, other arithmetic: 34 us -> none  [per_device(): jnp.zeros((col_width, vocab_rows + 1), jnp.float32).at[:, neg_local]]
    dot_general x7 -> x3, matrix products: 38.9 us -> 8.94 us  [contract_cols(): lax.dot_general(left, right, (((1,), (1,)), ((), ())), preferred_element_...]
    gather x2 -> x0, local copies, waits for them, and re-layouts: 20.3 us -> none  [per_device(): neg_part = jnp.take(padded_out, neg_local, axis=1).astype(jnp.float32)]
  transfers between devices with their start and end apart: 5 -> 0, of which waited for: 2 -> 0; matrix products, arithmetic and copies ran while one was open for 27% -> 0% of each run, Pallas kernels for 0% -> 0%
where the time goes in v1:
time: 179 us; the launch traced here: 178 us
  Pallas kernels  121 us (68%)
  local copies, waits for them, and re-layouts  22.3 us (12%)
  matrix products  16.6 us (9%)
  between operations  15.5 us (9%)
    pallas_call x1, Pallas kernels, front(): pl.pallas_call(functools.partial(front_kernel, sz), out_shape=[o for o, _...  92.5 us
    pallas_call x1, Pallas kernels, back(): pl.pallas_call(functools.partial(back_kernel, sz), out_shape=[table] * 3,...  28.9 us
    unnamed x32, local copies, waits for them, and re-layouts  12.5 us
    dot_general x3, matrix products, contract_cols(): lax.dot_general(left, right, (((1,), (1,)), ((), ())), preferred_element_...  8.94 us
    dot_general x3, matrix products, contract_rows(): lax.dot_general(left, right, (((0,), (0,)), ((), ())), preferred_element_...  6.69 us

profile of v1, /device:TPU:1, one launch (start us, length us, event | category | flops | bytes accessed | tf_op | source)
XLA Modules:
  0.0 177.9 jit_solution(360522156567861849)
XLA Ops:
  7.2 1.5 copy.119.watch_ids
  8.7 1.5 copy.120.search_ids
  10.9 1.3 add_add_fusion.extra
  12.3 0.7 concatenate.19
  13.0 0.6 reshape.243.neg_ids
  13.6 0.9 copy.118
  14.5 0.7 pad.10.demo_table
  15.2 0.9 slice.36
  16.1 0.7 pad.11.w_demo
  16.9 92.5 %front.1 = (bf16[8,512,2048]{2,1,0:T(8,128)(2,1)}, bf16[8,512,2048]{2,1,0:T(8,128)(2,1)}, bf16[1024,640]{1,0:T(8,128)(2,1)}, bf16[1024,1024]{1,0:T(8,128)(2,1)},...) custom-call(s32[128,50]{1,0:T(8,128)} %copy.119.watch_ids, ...), custom_call_target="tpu_custom_call" | custom-call | tf_op jit(solution)/shard_map/front/pallas_call | solution.py:895
  109.4 0.5 slice.37
  110.6 51.7 %conditional.1 = (bf16[32,256]{1,0:T(8,128)(2,1)}, f32[]{:T(128)}, f32[64,8192]{1,0:T(8,128)}, f32[64,8192]{1,0:T(8,128)}, f32[64,8192]{1,0:T(8,128)}, /*index=5...) conditional(s32[]{:T(128)} %bitcast.27, ...), branch_computations={%region_0.24_spmd, %region_24.28_spmd} | conditional | flops 10171484160 | bytes 394216288 | solution.py:1051
  110.9 0.5 slice.28
  111.4 1.9 %convert_reduce_fusion.1 = (f32[512]{0:T(512)S(1)}, bf16[1024,512]{1,0:T(8,128)(2,1)S(1)}) fusion(bf16[1024,512]{1,0:T(8,128)(2,1)} %get-tuple-element.136, bf16[1024,256]{1,0:T(8,128)(2,1)} %bitcast.105, bf16[512,256]{1,0:T(8,128)(2,1)} %get-tuple-element.135), kind=kOutput, calls=%fused_computation.4 | convolution fusion | flops 271056384 | bytes 2885632 | tf_op jit(solution)/shard_map/cond/branch_1_fun/dot_general | solution.py:19
  113.3 4.6 %convert_reduce_fusion = (f32[1024]{0:T(1024)S(1)}, bf16[1024,1024]{1,0:T(8,128)(2,1)}) fusion(bf16[1024,1024]{1,0:T(8,128)(2,1)} %get-tuple-element.156, bf16[1024,512]{1,0:T(8,128)(2,1)S(1)} %get-tuple-element.461, bf16[1024,512]{1,0:T(8,128)(2,1)S(1)} %copy-done.12), kind=kOutput, calls=%fused_computation.2 | convolution fusion | flops 1078983680 | bytes 6295552 | tf_op jit(solution)/shard_map/cond/branch_1_fun/dot_general | solution.py:19
  118.0 2.4 %convolution_convert_fusion = bf16[1024,216]{1,0:T(8,128)(2,1)S(1)} fusion(bf16[1024,1024]{1,0:T(8,128)(2,1)} %get-tuple-element.459, bf16[88,1024]{1,0:T(8,128)(2,1)S(1)} %slice.29, bf16[64,1024]{1,0:T(8,128)(2,1)S(1)} %get-tuple-element.457, bf16[64,1024]{1,0:T(8,128)(2,1)S(1)} %get-tuple-element.456), kind=kOutput, calls=%fused_computation.7 | convolution fusion | flops 454533120 | bytes 2981888 | tf_op jit(solution)/shard_map/cond/branch_1_fun/dot_general | solution.py:19
  120.4 0.7 slice.40.grads
  121.2 28.9 %back.1 = (f32[64,8192]{1,0:T(8,128)}, f32[64,8192]{1,0:T(8,128)}, f32[64,8192]{1,0:T(8,128)}) custom-call(bf16[1024,128]{1,0:T(8,128)(2,1)} %slice.40.grads, bf16[64,768]{1,0:T(8,128)(2,1)S(1)} %copy-done.22, bf16[64,1024]{1,0:T(8,128)(2,1)S(1)} %copy-done.19, f32[8,768]{1,0:T(8,128)S(1)} %copy-done.25, f32[8,1024]{1,0:T(8,128)S(1)} %copy-done.24, ...), custom_call_target="tpu_custom_call" | custom-call | tf_op jit(solution)/shard_map/cond/branch_1_fun/back/pallas_call | solution.py:979
  150.1 0.9 convolution_bitcast_fusion.1
  151.1 0.6 copy.125
  151.8 0.1 copy.112
  151.9 1.4 copy-done.38
  153.3 2.9 %fusion = f32[600,1024]{1,0:T(8,128)} fusion(bf16[1024,1024]{1,0:T(8,128)(2,1)S(1)} %copy-done.38, bf16[1024,88]{0,1:T(8,128)(2,1)S(1)} %slice.43, bf16[1024,512]{0,1:T(8,128)(2,1)S(1)} %bitcast.108), kind=kOutput, calls=%fused_computation.8 | convolution fusion | flops 1260748800 | bytes 5783552 | tf_op jit(solution)/shard_map/cond/branch_1_fun/dot_general | solution.py:13
  156.2 1.3 convolution_bitcast_fusion
  157.5 1.9 %copy.113 = f32[1024,512]{1,0:T(8,128)} copy(f32[1024,512]{0,1:T(8,128)S(1)} %convolution_bitcast_fusion) | data formatting | bytes 4194304 | tf_op jit(solution)/shard_map/cond
  159.4 2.5 %fusion.86 = f32[512,256]{1,0:T(8,128)} fusion(bf16[1024,512]{1,0:T(8,128)(2,1)} %get-tuple-element.170, bf16[1024,256]{1,0:T(8,128)(2,1)S(1)} %bitcast.106), kind=kOutput, calls=%fused_computation.149 | convolution fusion | flops 268435456 | bytes 2097152 | tf_op jit(solution)/shard_map/cond/branch_1_fun/dot_general | solution.py:13
  161.9 0.2 convert_reduce_fusion.2
  162.4 1.3 copy.190
  163.7 1.5 copy.191
  165.2 3.6 %copy.192 = f32[600,1024]{1,0:T(8,128)} copy(f32[600,1024]{1,0:T(8,128)} %get-tuple-element.520) | data formatting | bytes 4915200
  168.9 1.3 copy.193
  170.2 0.8 copy.194
  (54 shorter events, 0.4 us)
Async XLA Ops:
  16.9 93.7 %copy-start = (bf16[600,1024]{1,0:T(8,128)(2,1)S(1)}, bf16[600,1024]{1,0:T(8,128)(2,1)}, u32[]{:S(2)}) copy-start(bf16[600,1024]{1,0:T(8,128)(2,1)} %w_first.1) | copy-start | bytes 3686404
  16.9 93.7 %copy-start.2 = (bf16[64,8192]{1,0:T(8,128)(2,1)S(1)}, bf16[64,8192]{1,0:T(8,128)(2,1)}, u32[]{:S(2)}) copy-start(bf16[64,8192]{1,0:T(8,128)(2,1)} %out_table.1) | copy-start | bytes 3145732
  16.9 93.7 %copy-start.18 = (bf16[256,88]{0,1:T(8,128)(2,1)S(1)}, bf16[256,88]{0,1:T(8,128)(2,1)}, u32[]{:S(2)}) copy-start(bf16[256,88]{0,1:T(8,128)(2,1)} %param.26) | copy-start | bytes 135172
  16.9 93.7 %copy-start.20 = (s32[128,50]{0,1:T(8,128)S(1)}, s32[128,50]{0,1:T(8,128)}, u32[]{:S(2)}) copy-start(s32[128,50]{0,1:T(8,128)} %param.18) | copy-start | bytes 76804
  16.9 93.7 %copy-start.21 = (s32[128,50]{0,1:T(8,128)S(1)}, s32[128,50]{0,1:T(8,128)}, u32[]{:S(2)}) copy-start(s32[128,50]{0,1:T(8,128)} %param.19) | copy-start | bytes 76804
  16.9 93.7 %copy-start.23 = (s32[5120]{0:T(1024)S(1)}, s32[5120]{0:T(1024)}, u32[]{:S(2)}) copy-start(s32[5120]{0:T(1024)} %param.22) | copy-start | bytes 61444
  16.9 93.7 %copy-start.31 = (s32[128]{0:T(128)S(1)}, s32[128]{0:T(128)}, u32[]{:S(2)}) copy-start(s32[128]{0:T(128)} %param.21) | copy-start | bytes 1540
  110.8 2.5 %copy-start.12 = (bf16[1024,512]{1,0:T(8,128)(2,1)S(1)}, bf16[1024,512]{1,0:T(8,128)(2,1)}, u32[]{:S(2)}) copy-start(bf16[1024,512]{1,0:T(8,128)(2,1)} %get-tuple-element.137) | copy-start | bytes 3145732 | tf_op jit(solution)/shard_map/cond
  113.3 4.6 %copy-start.3 = (bf16[1024,512]{1,0:T(8,128)(2,1)}, bf16[1024,512]{1,0:T(8,128)(2,1)S(1)}, u32[]{:S(2)}) copy-start(bf16[1024,512]{1,0:T(8,128)(2,1)S(1)} %get-tuple-element.461) | copy-start | bytes 3145732 | tf_op jit(solution)/shard_map/cond
  118.0 3.2 %copy-start.19 = (bf16[64,1024]{1,0:T(8,128)(2,1)S(1)}, bf16[64,1024]{1,0:T(8,128)(2,1)}, u32[]{:S(2)}) copy-start(bf16[64,1024]{1,0:T(8,128)(2,1)} %get-tuple-element.159.pos_rows) | copy-start | bytes 393220 | tf_op jit(solution)/shard_map/cond
  118.0 3.2 %copy-start.22 = (bf16[64,768]{1,0:T(8,128)(2,1)S(1)}, bf16[64,768]{1,0:T(8,128)(2,1)}, u32[]{:S(2)}) copy-start(bf16[64,768]{1,0:T(8,128)(2,1)} %get-tuple-element.158.neg_rows) | copy-start | bytes 294916 | tf_op jit(solution)/shard_map/cond
  118.0 3.1 %copy-start.24 = (f32[8,1024]{1,0:T(8,128)S(1)}, f32[8,1024]{1,0:T(8,128)}, u32[]{:S(2)}) copy-start(f32[8,1024]{1,0:T(8,128)} %get-tuple-element.161.pos) | copy-start | bytes 98308 | tf_op jit(solution)/shard_map/cond
  118.0 3.1 %copy-start.25 = (f32[8,768]{1,0:T(8,128)S(1)}, f32[8,768]{1,0:T(8,128)}, u32[]{:S(2)}) copy-start(f32[8,768]{1,0:T(8,128)} %get-tuple-element.160.slots) | copy-start | bytes 73732 | tf_op jit(solution)/shard_map/cond
  121.2 28.9 %copy-start.14 = (bf16[256,1024]{1,0:T(8,128)(2,1)S(1)}, bf16[256,1024]{1,0:T(8,128)(2,1)}, u32[]{:S(2)}) copy-start(bf16[256,1024]{1,0:T(8,128)(2,1)} %get-tuple-element.167) | copy-start | bytes 1572868 | tf_op jit(solution)/shard_map/cond
  121.2 29.9 %copy-start.8 = (bf16[1024,640]{1,0:T(8,128)(2,1)S(1)}, bf16[1024,640]{1,0:T(8,128)(2,1)}, u32[]{:S(2)}) copy-start(bf16[1024,640]{1,0:T(8,128)(2,1)} %get-tuple-element.433) | copy-start | bytes 3932164 | tf_op jit(solution)/shard_map/cond
  151.7 1.6 copy-start.38
  153.3 2.9 %copy-start.4 = (bf16[1024,512]{1,0:T(8,128)(2,1)S(1)}, bf16[1024,512]{1,0:T(8,128)(2,1)}, u32[]{:S(2)}) copy-start(bf16[1024,512]{1,0:T(8,128)(2,1)} %copy-done.3) | copy-start | bytes 3145732 | tf_op jit(solution)/shard_map/cond
  153.3 2.9 %copy-start.6 = (bf16[1024,1024]{1,0:T(8,128)(2,1)S(1)}, bf16[1024,1024]{1,0:T(8,128)(2,1)}, u32[]{:S(2)}) copy-start(bf16[1024,1024]{1,0:T(8,128)(2,1)} %get-tuple-element.169) | copy-start | bytes 6291460 | tf_op jit(solution)/shard_map/cond
  157.5 1.9 %copy-start.5 = (bf16[8,128,256]{2,1,0:T(8,128)(2,1)S(1)}, bf16[8,128,256]{2,1,0:T(8,128)(2,1)}, u32[]{:S(2)}) copy-start(bf16[8,128,256]{2,1,0:T(8,128)(2,1)} %get-tuple-element.134) | copy-start | bytes 1572868 | tf_op jit(solution)/shard_map/cond
  162.3 6.5 %copy-start.33 = (f32[1024]{0:T(1024)}, f32[1024]{0:T(1024)S(1)}, u32[]{:S(2)}) copy-start(f32[1024]{0:T(1024)S(1)} %get-tuple-element.521) | copy-start | bytes 12292
  162.4 6.5 %copy-start.34 = (f32[512]{0:T(512)}, f32[512]{0:T(512)S(1)}, u32[]{:S(2)}) copy-start(f32[512]{0:T(512)S(1)} %get-tuple-element.523) | copy-start | bytes 6148
  162.4 6.5 %copy-start.35 = (f32[256]{0:T(256)}, f32[256]{0:T(256)S(1)}, u32[]{:S(2)}) copy-start(f32[256]{0:T(256)S(1)} %get-tuple-element.525) | copy-start | bytes 3076
  165.2 3.6 %copy-start.7 = (f32[1024,512]{1,0:T(8,128)S(1)}, f32[1024,512]{1,0:T(8,128)}, u32[]{:S(2)}) copy-start(f32[1024,512]{1,0:T(8,128)} %get-tuple-element.522) | copy-start | bytes 6291460
  168.9 1.4 copy-start.15

commit v2 on v0

--- a/solution.py
+++ b/solution.py
@@ -1,8 +1,11 @@
+import functools
 import math
 
 import jax
 import jax.numpy as jnp
 from jax import lax
+from jax.experimental import pallas as pl
+from jax.experimental.pallas import tpu as pltpu
 from jax.sharding import PartitionSpec as P
 
 
@@ -22,7 +25,59 @@
     return jax.vjp(jax.nn.gelu, pre_value)[1](grad_value)[0]
 
 
+class Collectives:
+    def gather(self, value, name, axis):
+        return lax.all_gather(value, name, axis=axis, tiled=True)
+
+    def scatter_sum(self, value, name, axis):
+        return lax.psum_scatter(value, name, scatter_dimension=axis, tiled=True)
+
+    def total(self, values, name):
+        return lax.psum(values, name)
+
+
+class RingCollectives:
+    def shift(self, value, name):
+        size = lax.axis_size(name)
+        return lax.ppermute(value, name, [(i, (i + 1) % size) for i in range(size)])
+
+    def stack(self, value, name):
+        size, me = lax.axis_size(name), lax.axis_index(name)
+        held = [value]
+        for _ in range(size - 1):
+            held.append(self.shift(held[-1], name))
+        return jnp.take(jnp.stack(held), (me - jnp.arange(size)) % size, axis=0)
+
+    def gather(self, value, name, axis):
+        parts = self.stack(value, name)
+        return jnp.concatenate([parts[i] for i in range(parts.shape[0])], axis=axis)
+
+    def ring_sum(self, parts, name):
+        size, me = lax.axis_size(name), lax.axis_index(name)
+        held = jnp.take(parts, (me - 1) % size, axis=0)
+        for step in range(1, size):
+            held = self.shift(held, name) + jnp.take(parts, (me - 1 - step) % size, axis=0)
+        return held
+
+    def scatter_sum(self, value, name, axis):
+        size = lax.axis_size(name)
+        return self.ring_sum(jnp.stack(jnp.split(value, size, axis=axis)), name)
+
+    def total(self, values, name):
+        size = lax.axis_size(name)
+        flat = jnp.concatenate([v.reshape(-1) for v in values])
+        length = -(-flat.shape[0] // (size * 128)) * 128
+        parts = jnp.pad(flat, (0, size * length - flat.shape[0])).reshape(size, length)
+        whole = self.stack(self.ring_sum(parts, name), name).reshape(-1)
+        out, at = [], 0
+        for v in values:
+            out.append(whole[at : at + v.size].reshape(v.shape))
+            at += v.size
+        return tuple(out)
+
+
 def per_device(
+    comm,
     watch_ids,
     search_ids,
     demo_ids,
@@ -72,9 +127,9 @@
     zero_col = jnp.zeros((col_width, 1), jnp.bfloat16)
     padded_out = jnp.concatenate([out_table, zero_col], axis=1)
     all_watch, all_search, all_pos = (
-        lax.all_gather(watch_ids, "batch", axis=0, tiled=True),
-        lax.all_gather(search_ids, "batch", axis=0, tiled=True),
-        lax.all_gather(pos_ids, "batch", axis=0, tiled=True),
+        comm.gather(watch_ids, "batch", 0),
+        comm.gather(search_ids, "batch", 0),
+        comm.gather(pos_ids, "batch", 0),
     )
     total_rows = all_watch.shape[0]
     block_rows = min(1024, total_rows)
@@ -99,21 +154,23 @@
     )
     watch_parts, search_parts, pos_parts = lax.map(bag_block, id_blocks)
     watch_sum, search_sum, pos_rows = (
-        lax.psum_scatter(flatten_blocks(watch_parts), "batch", scatter_dimension=1, tiled=True),
-        lax.psum_scatter(flatten_blocks(search_parts), "batch", scatter_dimension=1, tiled=True),
-        lax.psum_scatter(flatten_blocks(pos_parts), "batch", scatter_dimension=1, tiled=True),
-    )
-    neg_rows, valid_total = lax.psum((neg_part, jnp.sum(valid_counts).astype(jnp.float32)), "batch")
+        comm.scatter_sum(flatten_blocks(watch_parts), "batch", 1),
+        comm.scatter_sum(flatten_blocks(search_parts), "batch", 1),
+        comm.scatter_sum(flatten_blocks(pos_parts), "batch", 1),
+    )
+    neg_rows, valid_total = comm.total(
+        (neg_part, jnp.sum(valid_counts).astype(jnp.float32)), "batch"
+    )
     pooled_watch = (watch_sum / bag_size).astype(jnp.bfloat16)
     pooled_search = (search_sum / bag_size).astype(jnp.bfloat16)
     pos_bf = pos_rows.astype(jnp.bfloat16)
     neg_bf = neg_rows.astype(jnp.bfloat16)
     count_here = valid_counts[0]
     full_watch, full_search, full_pos, full_neg = (
-        lax.all_gather(pooled_watch, "col", axis=0, tiled=True),
-        lax.all_gather(pooled_search, "col", axis=0, tiled=True),
-        lax.all_gather(pos_bf, "col", axis=0, tiled=True),
-        lax.all_gather(neg_bf, "col", axis=0, tiled=True),
+        comm.gather(pooled_watch, "col", 0),
+        comm.gather(pooled_search, "col", 0),
+        comm.gather(pos_bf, "col", 0),
+        comm.gather(neg_bf, "col", 0),
     )
     watch_rows = full_watch.T
     search_rows = full_search.T
@@ -171,12 +228,12 @@
     own_pos = lax.dynamic_slice_in_dim(pos_row_grad, col_start, col_width, 1).T
     user_vecs = lax.dynamic_slice_in_dim(user_block, col_slot * quarter, quarter, 0)
     all_pw, all_ps, all_dpos = (
-        lax.all_gather(own_pw, "batch", axis=1, tiled=True),
-        lax.all_gather(own_ps, "batch", axis=1, tiled=True),
-        lax.all_gather(own_pos, "batch", axis=1, tiled=True),
+        comm.gather(own_pw, "batch", 1),
+        comm.gather(own_ps, "batch", 1),
+        comm.gather(own_pos, "batch", 1),
     )
     neg_own = lax.dynamic_slice_in_dim(neg_row_grad, col_slot * col_width, col_width, 0)
-    sums_out = lax.psum(
+    sums_out = comm.total(
         (
             grad_w_first,
             grad_b_first,
@@ -234,6 +291,951 @@
     )
 
 
+F32, BF16, FP8, I32 = jnp.float32, jnp.bfloat16, jnp.float8_e4m3fn, jnp.int32
+MESH = pl.DeviceIdType.MESH
+LOW = 256
+ROWS_IN_GROUP = 4
+BAG_PAD = 64
+CHUNK = 256
+NEG_FLOOR = -1e30
+
+
+def dot_as(left, right, left_dim, right_dim):
+    return lax.dot_general(
+        left, right, (((left_dim,), (right_dim,)), ((), ())), preferred_element_type=F32
+    )
+
+
+def iota(shape, dim):
+    return lax.broadcasted_iota(I32, shape, dim)
+
+
+def one_where(mask, kind):
+    return jnp.where(mask, jnp.ones((), BF16), jnp.zeros((), BF16)).astype(kind)
+
+
+def slot_cap(neg_count, batch):
+    mean = neg_count / batch
+    return int(math.ceil((mean + 4.5 * math.sqrt(mean)) / CHUNK)) * CHUNK
+
+
+def gelu(pre):
+    bent = jnp.tanh(math.sqrt(2.0 / math.pi) * (pre + 0.044715 * (pre * pre * pre)))
+    return 0.5 * pre * (1.0 + bent)
+
+
+def gelu_slope(pre):
+    inner_scale = math.sqrt(2.0 / math.pi)
+    square = pre * pre
+    bent = jnp.tanh(inner_scale * (pre + 0.044715 * (square * pre)))
+    return 0.5 * (1.0 + bent) + 0.5 * pre * (1.0 - bent * bent) * (
+        inner_scale * (1.0 + 3.0 * 0.044715 * square)
+    )
+
+
+def spread_matrix(rows):
+    shape = (rows, 4 * rows)
+    r, m = iota(shape, 0), iota(shape, 1)
+    groups = rows // ROWS_IN_GROUP
+    return one_where((r % groups == m // 16) & (r // groups == m % ROWS_IN_GROUP), BF16)
+
+
+class Sizes:
+    def __init__(self, batch, col, rows, bag, width, vocab, negs, embed, demo_width):
+        self.batch, self.col, self.rows, self.bag = batch, col, rows, bag
+        self.width, self.vocab, self.negs, self.embed = width, vocab, negs, embed
+        self.demo_width = demo_width
+        self.total = batch * rows
+        self.quarter = rows // col
+        self.users = batch * self.quarter
+        self.groups = rows // ROWS_IN_GROUP
+        self.high = vocab // LOW
+        self.high_parts = self.high // 4
+        self.cap = slot_cap(negs, batch)
+        self.cap_tiles = self.cap // CHUNK
+        self.tiles = self.cap_tiles + col
+        self.neg_lines = -(-negs // (CHUNK * 8)) * 8
+        self.steps = 4
+        self.span = self.total // self.steps
+        self.x_width = col * 128 + 128
+
+
+def front_kernel(
+    sz,
+    watch_ids, search_ids, demo_ids, pos_ids, neg_ids, demo_table, b_first, b_second, b_third, valid_count,
+    watch_table, search_table, out_table, w_first, w_second, w_third,
+    counts_out, x_out, act1_out, slope1_out, act2_out, slope2_out, gu_out, buckets_out,
+    neg_rows_out, pos_rows_out, slots_out, user_out, loss_out, fits_out,
+    tabs, tall, mix, w1_raw, w1, w2, w3, turned, ids, neg_dest, neg_digits, counts, found_sums, sums, pieces, x,
+    pre1, pre2, acts1, slopes1, acts2, slopes2, users, buckets, slots, picked, neg_all, pos_all, e_cols,
+    e_rows, probs, stats, g_send, g_recv, gu, rg_send, rg_recv, gp_all, loss_all,
+    local_sem, out_sem, count_sem, ids_s, ids_r, rs_s, rs_r, ag_s, ag_r, xx_s, xx_r, co_s, co_r,
+    ne_s, ne_r, pe_s, pe_r, st_s, st_r, gs_s, gs_r, ga_s, ga_r, gx_s, gx_r, gc_s, gc_r,
+    rg_s, rg_r, gp_s, gp_r, lo_s, lo_r,
+):
+    b, c = lax.axis_index("batch"), lax.axis_index("col")
+    nb, nc = sz.batch, sz.col
+    offset = b * sz.vocab
+    cap, width, embed = sz.cap, sz.width, sz.embed
+    cx = lax.rem(c + 2, nc)
+    ck = c + 1 - 2 * lax.rem(c, 2)
+    ckx = lax.rem(ck + 2, nc)
+
+    def batch_peer(i):
+        return lax.rem(b + i, nb)
+
+    def batch_from(i):
+        return lax.rem(b + nb - i, nb)
+
+    def col_peer(i):
+        return lax.rem(c + i, nc)
+
+    def col_from(i):
+        return lax.rem(c + nc - i, nc)
+
+    def send(src, dst, ssem, rsem, to):
+        return pltpu.make_async_remote_copy(
+            src_ref=src, dst_ref=dst, send_sem=ssem, recv_sem=rsem,
+            device_id=to, device_id_type=MESH,
+        )
+
+    barrier = pltpu.get_barrier_semaphore()
+    for i in range(1, nb):
+        pl.semaphore_signal(barrier, inc=1, device_id=(batch_peer(i), c), device_id_type=MESH)
+    for i in range(1, nc):
+        pl.semaphore_signal(barrier, inc=1, device_id=(b, col_peer(i)), device_id_type=MESH)
+
+    loads = [
+        (watch_table, tabs.at[0]), (search_table, tabs.at[1]), (out_table, tabs.at[2]),
+        (w_first, w1_raw), (w_second, w2), (w_third, w3),
+    ]
+    loads = [pltpu.make_async_copy(s, d, local_sem.at[i]) for i, (s, d) in enumerate(loads)]
+    for load in loads:
+        load.start()
+
+    turned[...] = jnp.zeros((BAG_PAD, 128), I32)
+    turned[0 : sz.bag, :] = (watch_ids[...] & 0xFFFF) | (search_ids[...] << 16)
+    packed = turned[...].T
+    for r4 in range(ROWS_IN_GROUP):
+        ids[b, 0 : sz.groups, r4 * BAG_PAD : (r4 + 1) * BAG_PAD] = packed[
+            r4 * sz.groups : (r4 + 1) * sz.groups, :
+        ]
+    ids[b, sz.groups : sz.groups + 8, :] = jnp.zeros((8, CHUNK), I32)
+    ids[b, sz.groups : sz.groups + 1, 0:128] = pos_ids[...]
+    ids[b, sz.groups + 1 : sz.groups + 2, 0:128] = jnp.full((1, 128), valid_count[0], I32)
+    ids[b, sz.groups + 2 : sz.groups + 2 + demo_ids.shape[0], 0:128] = demo_ids[...]
+
+    negs = neg_ids[...]
+    lines = sz.neg_lines
+    missing = 2 * lines - negs.shape[0]
+    second = jnp.concatenate([negs[lines:], jnp.full((missing, 128), -1, I32)], axis=0)
+    negs = jnp.concatenate([negs[:lines], second], axis=1)
+    neg_local = negs - offset
+    own = (neg_local >= 0) & (neg_local < sz.vocab)
+    own_bf = one_where(own, BF16)
+    upper = one_where(iota((CHUNK, CHUNK), 0) < iota((CHUNK, CHUNK), 1), BF16)
+    before = dot_as(own_bf, upper, 1, 0)
+    in_row = dot_as(own_bf, jnp.ones((CHUNK, CHUNK), BF16), 1, 0)
+    lower = one_where(iota((lines, lines), 1) < iota((lines, lines), 0), BF16)
+    rows_before = dot_as(lower, in_row.astype(BF16), 1, 0)
+    neg_dest[...] = jnp.where(own, before + rows_before, -1.0)
+    owned_count = dot_as(jnp.ones((8, lines), BF16), in_row.astype(BF16), 1, 0)
+    most = jnp.zeros((1, 1), F32)
+    for shard in range(nb):
+        part = negs - shard * sz.vocab
+        hits = jnp.where((part >= 0) & (part < sz.vocab), 1.0, 0.0)
+        most = jnp.maximum(most, jnp.sum(jnp.sum(hits, axis=1, keepdims=True), axis=0, keepdims=True))
+    fits_out[...] = jnp.where(most <= float(cap), 1, 0)
+    for digit in range(4):
+        neg_digits[digit] = ((neg_local >> (4 * digit)) & 15).astype(F32)
+
+    def compact(k, total):
+        place = neg_dest[pl.ds(k, 1), :]
+        hot = one_where(place == iota((cap, CHUNK), 0).astype(F32), FP8)
+        line = iota((32, CHUNK), 0)
+        value = jnp.where(line == 4, 1.0, 0.0)
+        for digit in range(4):
+            value = jnp.where(line == digit, neg_digits[digit, pl.ds(k, 1), :], value)
+        return total + dot_as(value.astype(FP8), hot, 1, 1)
+
+    slot = lax.fori_loop(0, lines, compact, jnp.zeros((32, cap), F32))
+    neg_low = slot[0:1] + 16.0 * slot[1:2]
+    neg_high = jnp.where(slot[4:5] > 0.5, slot[2:3] + 16.0 * slot[3:4], -1.0)
+    slots[...] = jnp.zeros((sz.tiles, 8, CHUNK), F32)
+    for k in range(sz.cap_tiles):
+        slots[k, 0:1, :] = neg_high[:, k * CHUNK : (k + 1) * CHUNK]
+        slots[k, 1:2, :] = neg_low[:, k * CHUNK : (k + 1) * CHUNK]
+
+    for t in range(2):
+        loads[t].wait()
+
+    def turn(n, _):
+        t, hh = n // sz.high_parts, n % sz.high_parts
+        base = pl.multiple_of(hh * 4 * LOW, 4 * LOW)
+        stack = jnp.concatenate([tabs[t, :, pl.ds(base + i * LOW, LOW)] for i in range(4)], axis=0)
+        mix[t, pl.ds(pl.multiple_of(hh * LOW, LOW), LOW), :] = stack.T
+        return 0
+
+    lax.fori_loop(0, 2 * sz.high_parts, turn, 0)
+
+    pl.semaphore_wait(barrier, nb - 1 + nc - 1)
+    last_sends = []
+    for i in range(1, nb):
+        copy = send(ids.at[b], ids.at[b], ids_s.at[i - 1], ids_r.at[i - 1], (batch_peer(i), c))
+        copy.start()
+        last_sends.append(copy)
+
+    loads[2].wait()
+
+    def stack_up(hh, _):
+        for i in range(4):
+            tall[pl.ds(pl.multiple_of((hh * 4 + i) * width, width), width), :] = tabs[
+                2, :, pl.ds(pl.multiple_of((hh * 4 + i) * LOW, LOW), LOW)
+            ]
+        return 0
+
+    lax.fori_loop(0, sz.high_parts, stack_up, 0)
+
+    def pick_tile(k, _):
+        high, low = slots[k, 0:1, :], slots[k, 1:2, :]
+        low_hot = one_where(low.astype(BF16) == iota((LOW, CHUNK), 0).astype(BF16), BF16)
+        total = jnp.zeros((width, CHUNK), F32)
+        for part in range(4):
+            tall_rows = width * sz.high // 4
+            got = dot_as(tall[part * tall_rows : (part + 1) * tall_rows, :], low_hot, 1, 0)
+            for i in range(sz.high // 4):
+                at = float(part * (sz.high // 4) + i)
+                total = total + jnp.where(high == at, got[i * width : (i + 1) * width], 0.0)
+        picked[k] = total.astype(BF16)
+        return 0
+
+    lax.fori_loop(0, sz.cap_tiles, pick_tile, 0)
+    neg_part = picked.at[pl.ds(0, sz.cap_tiles)]
+    for i in range(1, nc):
+        copy = send(neg_part, neg_all.at[c], ne_s.at[i - 1], ne_r.at[i - 1], (b, col_peer(i)))
+        copy.start()
+        last_sends.append(copy)
+    for k in range(sz.cap_tiles):
+        neg_all[c, k] = picked[k]
+
+    loads[3].wait()
+    w1[nc * 128 :, :] = jnp.zeros((128, w1.shape[1]), BF16)
+    for i in range(nc):
+        w1[i * 128 : i * 128 + width, :] = w1_raw[i * width : (i + 1) * width, :]
+        w1[i * 128 + width : (i + 1) * 128, :] = w1_raw[embed + i * width : embed + (i + 1) * width, :]
+    w1[nc * 128 : nc * 128 + sz.demo_width, :] = w1_raw[2 * embed :, :]
+    loads[4].wait()
+    loads[5].wait()
+
+    for i in range(1, nb):
+        src = batch_from(i)
+        send(ids.at[src], ids.at[src], ids_s.at[i - 1], ids_r.at[i - 1], (b, c)).wait_recv()
+
+    all_pos = jnp.concatenate([ids[j, sz.groups : sz.groups + 1, 0:128] for j in range(nb)], axis=0)
+    valid = jnp.concatenate([ids[j, sz.groups + 1 : sz.groups + 2, 0:128] for j in range(nb)], axis=0)
+    pos_local = all_pos - offset
+    pos_owned = (pos_local >= 0) & (pos_local < sz.vocab)
+    pos_pair = jnp.concatenate(
+        [
+            jnp.where(pos_owned, pos_local >> 8, 255).astype(F32),
+            (pos_local & 255).astype(F32),
+        ],
+        axis=0,
+    ).astype(BF16)
+    shape = (nb, CHUNK)
+    at_block = iota(shape, 1) // sz.quarter == iota(shape, 0)
+    for quarter in range(nc):
+        shape = (128, CHUNK)
+        pick = one_where(iota(shape, 0) == quarter * sz.quarter + iota(shape, 1) % sz.quarter, BF16)
+        wide = dot_as(pos_pair, pick, 1, 0)
+        high = jnp.sum(jnp.where(at_block, wide[0:nb], 0.0), axis=0, keepdims=True)
+        low = jnp.sum(jnp.where(at_block, wide[nb : 2 * nb], 0.0), axis=0, keepdims=True)
+        slots[sz.cap_tiles + quarter, 0:1, :] = jnp.where(high > 254.0, -1.0, high)
+        slots[sz.cap_tiles + quarter, 1:2, :] = low
+    slots_out[...] = slots[...]
+    lax.fori_loop(sz.cap_tiles, sz.tiles, pick_tile, 0)
+    pos_all[c] = picked[sz.cap_tiles + c]
+    for i in range(1, nc):
+        to = col_peer(i)
+        copy = send(picked.at[sz.cap_tiles + to], pos_all.at[c], pe_s.at[i - 1], pe_r.at[i - 1], (b, to))
+        copy.start()
+        last_sends.append(copy)
+
+    valid_wide = jnp.concatenate([valid] * (sz.users // 128), axis=1).astype(F32)
+    live_count = jnp.sum(jnp.where(at_block, valid_wide, 0.0), axis=0, keepdims=True)
+    valid_total = jnp.sum(valid_wide, axis=0, keepdims=True)
+    user_place = c * sz.quarter + iota((1, sz.users), 1) % sz.quarter
+    weight = jnp.where(user_place.astype(F32) < live_count, 1.0 / valid_total, 0.0)
+
+    bucket_total = jnp.zeros((buckets.shape[0], sz.total), BF16)
+    bucket_line = iota((buckets.shape[0], sz.total), 0).astype(BF16)
+    for field in range(demo_ids.shape[0]):
+        row = sz.groups + 2 + field
+        line = jnp.concatenate([ids[j, row : row + 1, 0:128] for j in range(nb)], axis=1)
+        bucket_total = bucket_total + one_where(line.astype(F32).astype(BF16) == bucket_line, BF16)
+    buckets[...] = bucket_total
+    demo_rows = demo_table[...].astype(F32).T.astype(BF16)
+    x[:, nc * 128 :] = jnp.zeros((sz.total, 128), BF16)
+    x[:, nc * 128 : nc * 128 + sz.demo_width] = dot_as(bucket_total, demo_rows, 0, 0).astype(BF16)
+    buckets_copy = pltpu.make_async_copy(buckets, buckets_out, out_sem.at[0])
+    buckets_copy.start()
+
+    spread = spread_matrix(sz.rows)
+    span = sz.span
+    piece = span // nb
+    span_lines = 4 * span
+    lane_mod = iota((16, CHUNK), 1) % BAG_PAD
+    lane_r4 = iota((16, CHUNK), 1) // BAG_PAD
+    blocks = span // sz.rows
+    parts_in_block = sz.groups // 16
+
+    def count_copy(t, table, slot_at):
+        rows = pl.ds(pl.multiple_of(t * span_lines, span_lines), span_lines)
+        return pltpu.make_async_copy(
+            counts.at[table, slot_at], counts_out.at[table, :, rows], count_sem.at[table, slot_at]
+        )
+
+    def bag_table(t, table):
+        slot_at = lax.rem(t, 2)
+
+        @pl.when(t >= 2)
+        def _():
+            count_copy(t - 2, table, slot_at).wait()
+
+        code_line = iota((4 * sz.high, CHUNK), 0).astype(BF16)
+        low_line = iota((LOW, CHUNK), 0).astype(BF16)
+
+        def groups_of(q, _):
+            block = t * blocks + q // parts_in_block
+            word = ids[block, pl.ds(pl.multiple_of((q % parts_in_block) * 16, 16), 16), :]
+            value = lax.shift_right_logical(word, 16 * table) & 0xFFFF
+            local = value - offset
+            mine = (local >= 0) & (local < sz.vocab) & (lane_mod < sz.bag)
+            code = jnp.where(mine, (local >> 8) * 4 + lane_r4, -1).astype(F32).astype(BF16)
+            low = (local & 255).astype(F32).astype(BF16)
+            for g in range(16):
+                left = one_where(code[g : g + 1, :] == code_line, FP8)
+                right = one_where(low[g : g + 1, :] == low_line, FP8)
+                found = dot_as(left, right, 1, 1).astype(BF16)
+                line = pl.ds(pl.multiple_of(q * 256 + g * 16, 16), 16)
+                for hh in range(sz.high_parts):
+                    counts[table, slot_at, hh, line, :] = found[hh * 16 : (hh + 1) * 16, :]
+            return 0
+
+        lax.fori_loop(0, blocks * parts_in_block, groups_of, 0)
+        count_copy(t, table, slot_at).start()
+        left = jnp.concatenate([counts[table, slot_at, hh] for hh in range(sz.high_parts)], axis=1)
+        total = dot_as(left, mix[table], 1, 0)
+        shape = (span_lines, 4 * width)
+        total = jnp.where((iota(shape, 0) // 4) % 4 == iota(shape, 1) // width, total, 0.0)
+        half = (total[:, :128] + total[:, 128:]).astype(BF16)
+        for k in range(blocks):
+            found = dot_as(spread, half[k * 4 * sz.rows : (k + 1) * 4 * sz.rows], 1, 0)
+            found_sums[table, k * sz.rows : (k + 1) * sz.rows, :] = found + pltpu.roll(found, width, 1)
+
+    def bag_step(t):
+        def one_table(table, _):
+            bag_table(t, table)
+            return 0
+
+        lax.fori_loop(0, 2, one_table, 0)
+        joined = jnp.where(iota((span, 128), 1) < width, found_sums[0], found_sums[1])
+        sums[t] = joined.astype(BF16)
+        for i in range(1, nb):
+            to = batch_peer(i)
+            send(
+                sums.at[t, pl.ds(pl.multiple_of(to * piece, piece), piece)], pieces.at[t, i - 1],
+                rs_s.at[t, i - 1], rs_r.at[t], (to, c),
+            ).start()
+
+    def x_at(t, col):
+        return x.at[
+            pl.ds(pl.multiple_of(t * span, span), span), pl.ds(pl.multiple_of(col * 128, 128), 128)
+        ]
+
+    def x_piece(t, owner):
+        return x.at[
+            pl.ds(pl.multiple_of(t * span + owner * piece, piece), piece),
+            pl.ds(pl.multiple_of(c * 128, 128), 128),
+        ]
+
+    def reduce_step(t):
+        send(pieces.at[t], pieces.at[t], rs_s.at[t, 0], rs_r.at[t], (b, c)).wait_recv()
+        total = sums[t, pl.ds(pl.multiple_of(b * piece, piece), piece), :].astype(F32)
+        for i in range(nb - 1):
+            total = total + pieces[t, i].astype(F32)
+        x[
+            pl.ds(pl.multiple_of(t * span + b * piece, piece), piece),
+            pl.ds(pl.multiple_of(c * 128, 128), 128),
+        ] = (total / sz.bag).astype(BF16)
+        for i in range(1, nb):
+            send(x_piece(t, b), x_piece(t, b), ag_s.at[t, i - 1], ag_r.at[t], (batch_peer(i), c)).start()
+
+    def cross_step(t):
+        send(pieces.at[t], pieces.at[t], ag_s.at[t, 0], ag_r.at[t], (b, c)).wait_recv()
+        send(x_at(t, c), x_at(t, c), xx_s.at[t], xx_r.at[t], (b, cx)).start()
+
+    def core_step(t):
+        send(x_at(t, cx), x_at(t, cx), xx_s.at[t], xx_r.at[t], (b, cx)).wait_recv()
+        send(x_at(t, c), x_at(t, c), co_s.at[t, 0], co_r.at[t, 0], (b, ck)).start()
+        send(x_at(t, cx), x_at(t, cx), co_s.at[t, 1], co_r.at[t, 1], (b, ck)).start()
+
+    def full_step(t):
+        send(x_at(t, ck), x_at(t, ck), co_s.at[t, 0], co_r.at[t, 0], (b, ck)).wait_recv()
+        send(x_at(t, ckx), x_at(t, ckx), co_s.at[t, 1], co_r.at[t, 1], (b, ck)).wait_recv()
+
+    def tower(k):
+        at = pl.ds(pl.multiple_of(k * span, span), span)
+        pre = dot_as(x[at, :], w1[...], 1, 0) + b_first[...]
+        pre1[at, :] = pre
+        value = gelu(pre).astype(BF16)
+        acts1[at, :] = value
+        pre = dot_as(value, w2[...], 1, 0) + b_second[...]
+        pre2[at, :] = pre
+        value = gelu(pre).astype(BF16)
+        acts2[at, :] = value
+        users[at, :] = (dot_as(value, w3[...], 1, 0) + b_third[...]).astype(BF16)
+
+    def slopes(k):
+        at = pl.ds(pl.multiple_of(k * span, span), span)
+        slopes1[at, :] = gelu_slope(pre1[at, :]).astype(BF16)
+        slopes2[at, :] = gelu_slope(pre2[at, :]).astype(BF16)
+
+    def step(t, _):
+        @pl.when(t < sz.steps)
+        def _():
+            bag_step(t)
+
+        @pl.when((t >= 1) & (t < sz.steps + 1))
+        def _():
+            reduce_step(t - 1)
+
+        @pl.when((t >= 2) & (t < sz.steps + 2))
+        def _():
+            cross_step(t - 2)
+
+        @pl.when((t >= 3) & (t < sz.steps + 3))
+        def _():
+            core_step(t - 3)
+
+        @pl.when(t >= 4)
+        def _():
+            full_step(t - 4)
+
+        @pl.when(t >= sz.steps)
+        def _():
+            tower(t - sz.steps)
+
+        return 0
+
+    lax.fori_loop(0, sz.steps + 4, step, 0)
+
+    out_copies = [(x, x_out), (acts1, act1_out), (acts2, act2_out), (slopes1, slope1_out), (slopes2, slope2_out)]
+    out_copies = [pltpu.make_async_copy(s, d, out_sem.at[1 + i]) for i, (s, d) in enumerate(out_copies)]
+    for copy in out_copies[:3]:
+        copy.start()
+    user_out[...] = users[pl.ds(pl.multiple_of(b * sz.rows + c * sz.quarter, sz.quarter), sz.quarter), :]
+
+    for i in range(1, nc):
+        src = col_from(i)
+        send(neg_all.at[src], neg_all.at[src], ne_s.at[i - 1], ne_r.at[i - 1], (b, c)).wait_recv()
+        send(pos_all.at[src], pos_all.at[src], pe_s.at[i - 1], pe_r.at[i - 1], (b, c)).wait_recv()
+    for i in range(nc):
+        for k in range(sz.cap_tiles):
+            e_cols[i * width : (i + 1) * width, k * CHUNK : (k + 1) * CHUNK] = neg_all[i, k]
+        e_cols[i * width : (i + 1) * width, cap:] = pos_all[i]
+    e_rows[...] = e_cols[...].T
+
+    def users_of(quarter):
+        return jnp.concatenate(
+            [
+                users[pl.ds(pl.multiple_of(j * sz.rows + quarter * sz.quarter, sz.quarter), sz.quarter), :]
+                for j in range(nb)
+            ],
+            axis=0,
+        )
+
+    quarter_users = users_of(c)
+    logits = dot_as(e_rows[...], quarter_users, 1, 1)
+    neg_logits, pos_logits = logits[0:cap], logits[cap:]
+    slot_ok = iota((cap, sz.users), 0).astype(F32) < owned_count[0:1, : sz.users]
+    pos_here = slots[sz.cap_tiles + c, 0:1, :]
+    pos_ok = (iota((sz.users, sz.users), 0) == iota((sz.users, sz.users), 1)) & (pos_here >= 0.0)
+    neg_logits = jnp.where(slot_ok, neg_logits, NEG_FLOOR)
+    pos_masked = jnp.where(pos_ok, pos_logits, NEG_FLOOR)
+    peak = jnp.maximum(
+        jnp.max(neg_logits, axis=0, keepdims=True), jnp.max(pos_masked, axis=0, keepdims=True)
+    )
+    mass = jnp.sum(jnp.where(slot_ok, jnp.exp(neg_logits - peak), 0.0), axis=0, keepdims=True) + jnp.sum(
+        jnp.where(pos_ok, jnp.exp(pos_masked - peak), 0.0), axis=0, keepdims=True
+    )
+    pos_value = jnp.sum(jnp.where(pos_ok, pos_logits, 0.0), axis=0, keepdims=True)
+    stats[b] = jnp.concatenate([peak, mass, pos_value, jnp.zeros((5, sz.users), F32)], axis=0)
+    for i in range(1, nb):
+        copy = send(stats.at[b], stats.at[b], st_s.at[i - 1], st_r.at[i - 1], (batch_peer(i), c))
+        copy.start()
+        last_sends.append(copy)
+
+    def some_slopes(k, _):
+        slopes(k)
+        return 0
+
+    lax.fori_loop(0, sz.steps // 2, some_slopes, 0)
+    for i in range(1, nb):
+        src = batch_from(i)
+        send(stats.at[src], stats.at[src], st_s.at[i - 1], st_r.at[i - 1], (b, c)).wait_recv()
+    peaks = [stats[j, 0:1, :] for j in range(nb)]
+    top = peaks[0]
+    for j in range(1, nb):
+        top = jnp.maximum(top, peaks[j])
+    full_mass = jnp.zeros((1, sz.users), F32)
+    pos_logit = jnp.zeros((1, sz.users), F32)
+    for j in range(nb):
+        full_mass = full_mass + stats[j, 1:2, :] * jnp.exp(peaks[j] - top)
+        pos_logit = pos_logit + stats[j, 2:3, :]
+    lse = top + jnp.log(full_mass)
+    loss_part = jnp.sum(weight * (lse - pos_logit), axis=1, keepdims=True)
+    scale = weight / full_mass
+    probs[0:cap] = jnp.where(slot_ok, jnp.exp(neg_logits - top) * scale, 0.0).astype(BF16)
+    pos_grad = weight * (jnp.exp(pos_logit - top) / full_mass - 1.0)
+    probs[cap:] = jnp.where(pos_ok, pos_grad, 0.0).astype(BF16)
+    grad_user = dot_as(probs[...], e_rows[...], 0, 0)
+    for j in range(nb):
+        g_send[j] = grad_user[j * sz.quarter : (j + 1) * sz.quarter].astype(BF16)
+    for i in range(1, nb):
+        to = batch_peer(i)
+        copy = send(g_send.at[to], g_recv.at[i - 1], gs_s.at[i - 1], gs_r.at[i - 1], (to, c))
+        copy.start()
+        last_sends.append(copy)
+    rows_grad = dot_as(probs[0:cap, :], quarter_users, 1, 0)
+    rows_grad = rows_grad.T.astype(BF16)
+    for i in range(nc):
+        rg_send[i] = rows_grad[i * width : (i + 1) * width]
+    gp_all[c] = jnp.broadcast_to(jnp.where(pos_here >= 0.0, pos_grad, 0.0), (8, sz.users))
+    loss_all[c] = jnp.broadcast_to(loss_part, (8, 128))
+    for i in range(1, nc):
+        to = col_peer(i)
+        for copy in (
+            send(rg_send.at[to], rg_recv.at[c], rg_s.at[i - 1], rg_r.at[i - 1], (b, to)),
+            send(gp_all.at[c], gp_all.at[c], gp_s.at[i - 1], gp_r.at[i - 1], (b, to)),
+            send(loss_all.at[c], loss_all.at[c], lo_s.at[i - 1], lo_r.at[i - 1], (b, to)),
+        ):
+            copy.start()
+            last_sends.append(copy)
+    rg_recv[c] = rg_send[c]
+    lax.fori_loop(sz.steps // 2, sz.steps, some_slopes, 0)
+    for copy in out_copies[3:]:
+        copy.start()
+    for i in range(1, nb):
+        send(g_send.at[0], g_recv.at[i - 1], gs_s.at[i - 1], gs_r.at[i - 1], (b, c)).wait_recv()
+    total = g_send[b].astype(F32)
+    for i in range(nb - 1):
+        total = total + g_recv[i].astype(F32)
+
+    def gu_at(block, col):
+        return gu.at[block, pl.ds(pl.multiple_of(col * sz.quarter, sz.quarter), sz.quarter), :]
+
+    def gu_all(col):
+        return gu.at[:, pl.ds(pl.multiple_of(col * sz.quarter, sz.quarter), sz.quarter), :]
+
+    gu[b, pl.ds(pl.multiple_of(c * sz.quarter, sz.quarter), sz.quarter), :] = total.astype(BF16)
+    for i in range(1, nb):
+        copy = send(gu_at(b, c), gu_at(b, c), ga_s.at[i - 1], ga_r.at[i - 1], (batch_peer(i), c))
+        copy.start()
+        last_sends.append(copy)
+    for i in range(nb):
+        src = batch_from(i)
+        if i > 0:
+            send(gu_at(src, c), gu_at(src, c), ga_s.at[i - 1], ga_r.at[i - 1], (b, c)).wait_recv()
+        copy = send(gu_at(src, c), gu_at(src, c), gx_s.at[i], gx_r.at[i], (b, cx))
+        copy.start()
+        last_sends.append(copy)
+    copy = send(gu_all(c), gu_all(c), gc_s.at[0], gc_r.at[0], (b, ck))
+    copy.start()
+    last_sends.append(copy)
+
+    pick_own = one_where(iota((width, embed), 1) == c * width + iota((width, embed), 0), BF16)
+    for i in range(1, nc):
+        src = col_from(i)
+        send(gp_all.at[src], gp_all.at[src], gp_s.at[i - 1], gp_r.at[i - 1], (b, c)).wait_recv()
+    for quarter in range(nc):
+        own_part = dot_as(pick_own, users_of(quarter), 1, 1)
+        grad = gp_all[quarter, 0:1, :].astype(BF16).astype(F32)
+        mine = slots[sz.cap_tiles + quarter, 0:1, :] >= 0.0
+        pos_rows_out[:, quarter * sz.users : (quarter + 1) * sz.users] = jnp.where(
+            mine, grad * own_part, 0.0
+        ).astype(BF16)
+
+    for i in range(nb):
+        src = batch_from(i)
+        send(gu_at(src, cx), gu_at(src, cx), gx_s.at[i], gx_r.at[i], (b, cx)).wait_recv()
+    copy = send(gu_all(cx), gu_all(cx), gc_s.at[1], gc_r.at[1], (b, ck))
+    copy.start()
+    last_sends.append(copy)
+
+    for i in range(1, nc):
+        src = col_from(i)
+        send(loss_all.at[src], loss_all.at[src], lo_s.at[i - 1], lo_r.at[i - 1], (b, c)).wait_recv()
+        send(rg_recv.at[src], rg_recv.at[src], rg_s.at[i - 1], rg_r.at[i - 1], (b, c)).wait_recv()
+    loss = loss_all[0]
+    neg_total = rg_recv[0].astype(F32)
+    for i in range(1, nc):
+        loss = loss + loss_all[i]
+        neg_total = neg_total + rg_recv[i].astype(F32)
+    neg_rows_out[...] = neg_total.astype(BF16)
+    loss_out[...] = loss[0:1, 0:1]
+
+    for i, col in enumerate((ck, ckx)):
+        send(gu_all(col), gu_all(col), gc_s.at[i], gc_r.at[i], (b, ck)).wait_recv()
+    gu_copy = pltpu.make_async_copy(gu, gu_out, out_sem.at[6])
+    gu_copy.start()
+
+    for copy in last_sends:
+        copy.wait_send()
+
+    def drain(t, _):
+        for i in range(1, nb):
+            send(sums.at[t, pl.ds(0, piece)], pieces.at[t, 0], rs_s.at[t, i - 1], rs_r.at[t], (b, c)).wait_send()
+            send(x_piece(t, b), x_piece(t, b), ag_s.at[t, i - 1], ag_r.at[t], (b, c)).wait_send()
+        send(x_at(t, c), x_at(t, c), xx_s.at[t], xx_r.at[t], (b, cx)).wait_send()
+        send(x_at(t, c), x_at(t, c), co_s.at[t, 0], co_r.at[t, 0], (b, ck)).wait_send()
+        send(x_at(t, cx), x_at(t, cx), co_s.at[t, 1], co_r.at[t, 1], (b, ck)).wait_send()
+        return 0
+
+    lax.fori_loop(0, sz.steps, drain, 0)
+    for table in range(2):
+        for t in (sz.steps - 2, sz.steps - 1):
+            count_copy(t, table, t % 2).wait()
+    buckets_copy.wait()
+    gu_copy.wait()
+    for copy in out_copies:
+        copy.wait()
+
+
+def front(sz, args):
+    nb, nc, total = sz.batch, sz.col, sz.total
+    width, embed, cap, users = sz.width, sz.embed, sz.cap, sz.users
+    slots = cap + users
+    first, second = args["w_second"].shape
+    buckets = args["demo_table"].shape[0]
+    x_width = sz.x_width
+    span_lines = 4 * sz.span
+    vmem = pl.BlockSpec(memory_space=pltpu.VMEM)
+    smem = pl.BlockSpec(memory_space=pltpu.SMEM)
+    hbm = pl.BlockSpec(memory_space=pl.ANY)
+    dma = pltpu.SemaphoreType.DMA
+
+    def shape(dims, kind=BF16):
+        return jax.ShapeDtypeStruct(dims, kind)
+
+    outs = [
+        (shape((2, sz.high_parts, 4 * total, LOW)), hbm), (shape((total, x_width)), hbm),
+        (shape((total, first)), hbm), (shape((total, first)), hbm),
+        (shape((total, second)), hbm), (shape((total, second)), hbm),
+        (shape((nb, sz.rows, embed)), hbm), (shape((buckets, total)), hbm),
+        (shape((width, cap)), vmem), (shape((width, total)), vmem),
+        (shape((sz.tiles, 8, CHUNK), F32), vmem),
+        (shape((sz.quarter, embed)), vmem), (shape((1, 1), F32), vmem), (shape((1, 1), I32), vmem),
+    ]
+    scratch = [
+        pltpu.VMEM((3, width, sz.vocab), BF16),
+        pltpu.VMEM((sz.high * width, LOW), BF16),
+        pltpu.VMEM((2, sz.high_parts * LOW, 4 * width), BF16),
+        pltpu.VMEM(args["w_first"].shape, BF16),
+        pltpu.VMEM((x_width, first), BF16),
+        pltpu.VMEM((first, second), BF16),
+        pltpu.VMEM((second, embed), BF16),
+        pltpu.VMEM((BAG_PAD, 128), I32),
+        pltpu.VMEM((nb, sz.groups + 8, CHUNK), I32),
+        pltpu.VMEM((sz.neg_lines, CHUNK), F32),
+        pltpu.VMEM((4, sz.neg_lines, CHUNK), F32),
+        pltpu.VMEM((2, 2, sz.high_parts, span_lines, LOW), BF16),
+        pltpu.VMEM((2, sz.span, 128), F32),
+        pltpu.VMEM((sz.steps, sz.span, 128), BF16),
+        pltpu.VMEM((sz.steps, nb - 1, sz.span // nb, 128), BF16),
+        pltpu.VMEM((total, x_width), BF16),
+        pltpu.VMEM((total, first), F32),
+        pltpu.VMEM((total, second), F32),
+        pltpu.VMEM((total, first), BF16),
+        pltpu.VMEM((total, first), BF16),
+        pltpu.VMEM((total, second), BF16),
+        pltpu.VMEM((total, second), BF16),
+        pltpu.VMEM((total, embed), BF16),
+        pltpu.VMEM((buckets, total), BF16),
+        pltpu.VMEM((sz.tiles, 8, CHUNK), F32),
+        pltpu.VMEM((sz.tiles, width, CHUNK), BF16),
+        pltpu.VMEM((nc, sz.cap_tiles, width, CHUNK), BF16),
+        pltpu.VMEM((nc, width, users), BF16),
+        pltpu.VMEM((embed, slots), BF16),
+        pltpu.VMEM((slots, embed), BF16),
+        pltpu.VMEM((slots, users), BF16),
+        pltpu.VMEM((nb, 8, users), F32),
+        pltpu.VMEM((nb, sz.quarter, embed), BF16),
+        pltpu.VMEM((nb - 1, sz.quarter, embed), BF16),
+        pltpu.VMEM((nb, sz.rows, embed), BF16),
+        pltpu.VMEM((nc, width, cap), BF16),
+        pltpu.VMEM((nc, width, cap), BF16),
+        pltpu.VMEM((nc, 8, users), F32),
+        pltpu.VMEM((nc, 8, 128), F32),
+        dma((6,)), dma((7,)), dma((2, 2)),
+        dma((nb - 1,)), dma((nb - 1,)),
+        dma((sz.steps, nb - 1)), dma((sz.steps,)), dma((sz.steps, nb - 1)), dma((sz.steps,)),
+        dma((sz.steps,)), dma((sz.steps,)), dma((sz.steps, 2)), dma((sz.steps, 2)),
+        dma((nc - 1,)), dma((nc - 1,)), dma((nc - 1,)), dma((nc - 1,)),
+        dma((nb - 1,)), dma((nb - 1,)), dma((nb - 1,)), dma((nb - 1,)),
+        dma((nb - 1,)), dma((nb - 1,)), dma((nb,)), dma((nb,)), dma((2,)), dma((2,)),
+        dma((nc - 1,)), dma((nc - 1,)), dma((nc - 1,)), dma((nc - 1,)), dma((nc - 1,)), dma((nc - 1,)),
+    ]
+    operands = [
+        (args["watch_ids"].T, vmem), (args["search_ids"].T, vmem), (args["demo_ids"].T, vmem),
+        (args["pos_ids"].reshape(1, -1), vmem), (args["neg_ids"].reshape(-1, 128), vmem),
+        (args["demo_table"].T, vmem), (args["b_first"].reshape(1, -1), vmem),
+        (args["b_second"].reshape(1, -1), vmem), (args["b_third"].reshape(1, -1), vmem),
+        (args["valid_counts"], smem),
+        (args["watch_table"], hbm), (args["search_table"], hbm), (args["out_table"], hbm),
+        (args["w_first"], hbm), (args["w_second"], hbm), (args["w_third"], hbm),
+    ]
+    return pl.pallas_call(
+        functools.partial(front_kernel, sz),
+        out_shape=[o for o, _ in outs],
+        in_specs=[s for _, s in operands],
+        out_specs=[s for _, s in outs],
+        scratch_shapes=scratch,
+        compiler_params=pltpu.CompilerParams(
+            collective_id=0, has_side_effects=True, vmem_limit_bytes=63 * 2**20
+        ),
+        name="front",
+    )(*[o for o, _ in operands])
+
+
+def back_kernel(
+    sz, neg_rows, pos_rows, slots, counts, x_in, act1_in, slope1_in, act2_in, slope2_in, gu_in,
+    buckets_in, w_first, w_second, w_third,
+    watch_out, search_out, table_out, gw1_out, gw2_out, gw3_out, demo_out, gb1_out, gb2_out, gb3_out,
+    x, act1, slope1, act2, slope2, gu, buckets, w1, w1_own, w2, w3, gps, gpf, gx, spread_grads, ring,
+    lines, low_rows, gw1, gw2, gw3, in_sem, ring_sem, line_sem, out_sem,
+):
+    width, cap, total, nb = sz.width, sz.cap, sz.total, sz.batch
+    parts, nc, embed = sz.high_parts, sz.col, sz.embed
+    c = lax.axis_index("col")
+    depth = ring.shape[0]
+    names = [
+        (gu_in, gu), (w_third, w3), (slope2_in, slope2), (w_second, w2), (slope1_in, slope1),
+        (w_first, w1), (act2_in, act2), (act1_in, act1), (x_in, x), (buckets_in, buckets),
+    ]
+    loads = [pltpu.make_async_copy(s, d, in_sem.at[i]) for i, (s, d) in enumerate(names)]
+    for load in loads:
+        load.start()
+
+    def ring_load(n):
+        return pltpu.make_async_copy(
+            counts.at[lax.rem(n, 2), n // 2], ring.at[lax.rem(n, depth)], ring_sem.at[lax.rem(n, depth)]
+        )
+
+    for n in range(depth):
+        ring_load(n).start()
+
+    loads[5].wait()
+    w1_own[...] = jnp.zeros(w1_own.shape, BF16)
+    w1_own[0:width, :] = w1[pl.ds(pl.multiple_of(c * width, width), width), :]
+    w1_own[width : 2 * width, :] = w1[pl.ds(pl.multiple_of(embed + c * width, width), width), :]
+    w1_own[2 * width : 2 * width + sz.demo_width, :] = w1[2 * embed :, :]
+    for load in loads[:5]:
+        load.wait()
+    half_blocks = nb // 2
+    half = half_blocks * sz.rows
+
+    def down(k, _):
+        at = pl.ds(pl.multiple_of(k * half, half), half)
+        top = gu[pl.ds(k * half_blocks, half_blocks)].reshape(half, embed)
+        second = (dot_as(top, w3[...], 1, 1) * slope2[at, :].astype(F32)).astype(BF16)
+        gps[at, :] = second
+        first = (dot_as(second, w2[...], 1, 1) * slope1[at, :].astype(F32)).astype(BF16)
+        gpf[at, :] = first
+        gx[at, :] = dot_as(first, w1_own[...], 1, 1).astype(BF16)
+        return 0
+
+    lax.fori_loop(0, 2, down, 0)
+
+    spread = spread_matrix(sz.rows)
+    shape = (4 * width, 4 * sz.rows)
+    mask = iota(shape, 0) // width == (iota(shape, 1) // 4) % 4
+
+    def lay(t, _):
+        rows = gx[pl.ds(pl.multiple_of(t * sz.rows, sz.rows), sz.rows), 0:128]
+        at = pl.ds(pl.multiple_of(t * 4 * sz.rows, 4 * sz.rows), 4 * sz.rows)
+        for table in range(2):
+            part = rows[:, table * width : (table + 1) * width]
+            wide = jnp.concatenate([part] * 4, axis=1)
+            laid = dot_as(wide, spread, 0, 0)
+            spread_grads[table, :, at] = jnp.where(mask, laid, 0.0).astype(BF16)
+        return 0
+
+    lax.fori_loop(0, nb, lay, 0)
+
+    for load in loads[6:]:
+        load.wait()
+    gu_rows = gu[...].reshape(total, embed)
+    gw3[...] = dot_as(act2[...], gu_rows, 0, 0)
+    gw2[...] = dot_as(act1[...], gps[...], 0, 0)
+    gw1[...] = dot_as(x[...], gpf[...], 0, 0)
+    stores = [(gw3, gw3_out), (gw2, gw2_out)]
+    for i in range(nc):
+        stores.append((gw1.at[pl.ds(i * 128, width)], gw1_out.at[pl.ds(i * width, width)]))
+        stores.append((gw1.at[pl.ds(i * 128 + width, width)], gw1_out.at[pl.ds(embed + i * width, width)]))
+    stores.append((gw1.at[pl.ds(nc * 128, sz.demo_width)], gw1_out.at[pl.ds(2 * embed, sz.demo_width)]))
+    stores = [pltpu.make_async_copy(s, d, out_sem.at[i]) for i, (s, d) in enumerate(stores)]
+    for store in stores:
+        store.start()
+    demo = dot_as(buckets[...], gx[:, 128:256], 1, 0)
+    demo_out[...] = demo.T[0 : sz.demo_width, :]
+    gb1_out[...] = jnp.sum(gpf[...].astype(F32), axis=0, keepdims=True)
+    gb2_out[...] = jnp.sum(gps[...].astype(F32), axis=0, keepdims=True)
+    gb3_out[...] = jnp.sum(gu_rows.astype(F32), axis=0, keepdims=True)
+
+    def line_store(out, slot, hh):
+        at = pl.ds(pl.multiple_of(hh * 4 * LOW, 4 * LOW), 4 * LOW)
+        return pltpu.make_async_copy(lines.at[slot], out.at[:, at], line_sem.at[slot])
+
+    def put(slot, found, factor):
+        for i in range(4):
+            lines[slot, :, i * LOW : (i + 1) * LOW] = found[i * width : (i + 1) * width] * factor
+
+    def bags(hh, _):
+        for table, out in enumerate((watch_out, search_out)):
+            n = hh * 2 + table
+            slot = table * 2 + lax.rem(hh, 2)
+            ring_load(n).wait()
+            found = dot_as(spread_grads[table], ring[lax.rem(n, depth)], 1, 0)
+
+            @pl.when(n + depth < 2 * parts)
+            def _():
+                ring_load(n + depth).start()
+
+            @pl.when(hh >= 2)
+            def _():
+                line_store(out, slot, hh - 2).wait()
+
+            put(slot, found, 1.0 / sz.bag)
+            line_store(out, slot, hh).start()
+        return 0
+
+    lax.fori_loop(0, parts, bags, 0)
+
+    for k in range(sz.tiles):
+        low = slots[k, 1:2, :].astype(BF16)
+        hot = one_where(low == iota((LOW, CHUNK), 0).astype(BF16), BF16)
+        low_rows[k * CHUNK : (k + 1) * CHUNK, :] = hot.T
+    high = jnp.concatenate([slots[k, 0:1, :] for k in range(sz.tiles)], axis=1).astype(BF16)
+    values = jnp.concatenate([neg_rows[...], pos_rows[...]], axis=1)
+
+    def scatter(n, _):
+        left = []
+        for i in range(8):
+            at = (n * 8 + i).astype(F32).astype(BF16)
+            left.append(jnp.where(high == at, values, jnp.zeros((), BF16)))
+        found = dot_as(jnp.concatenate(left, axis=0), low_rows[...], 1, 0)
+        for j in range(2):
+
+            @pl.when(n >= 1)
+            def _():
+                line_store(table_out, 4 + j, (n - 1) * 2 + j).wait()
+
+            put(4 + j, found[j * 4 * width : (j + 1) * 4 * width], 1.0)
+            line_store(table_out, 4 + j, n * 2 + j).start()
+        return 0
+
+    lax.fori_loop(0, parts // 2, scatter, 0)
+    for table, out in enumerate((watch_out, search_out)):
+        for hh in (parts - 2, parts - 1):
+            line_store(out, table * 2 + hh % 2, hh).wait()
+    for j in range(2):
+        line_store(table_out, 4 + j, parts - 2 + j).wait()
+    for store in stores:
+        store.wait()
+
+
+def back(sz, args, kept):
+    vmem = pl.BlockSpec(memory_space=pltpu.VMEM)
+    hbm = pl.BlockSpec(memory_space=pl.ANY)
+    total, nb = sz.total, sz.batch
+    first, second = args["w_second"].shape
+    embed, buckets = sz.embed, args["demo_table"].shape[0]
+    dma = pltpu.SemaphoreType.DMA
+
+    def shape(dims, kind=F32):
+        return jax.ShapeDtypeStruct(dims, kind)
+
+    table = shape((sz.width, sz.vocab))
+    outs = [(table, hbm)] * 3 + [
+        (shape((args["w_first"].shape)), hbm), (shape((first, second)), hbm), (shape((second, embed)), hbm),
+        (shape((sz.demo_width, buckets)), vmem), (shape((1, first)), vmem), (shape((1, second)), vmem),
+        (shape((1, embed)), vmem),
+    ]
+    slots = sz.tiles * CHUNK
+    return pl.pallas_call(
+        functools.partial(back_kernel, sz),
+        out_shape=[o for o, _ in outs],
+        in_specs=[vmem] * 3 + [hbm] * 11,
+        out_specs=[s for _, s in outs],
+        scratch_shapes=[
+            pltpu.VMEM((total, sz.x_width), BF16), pltpu.VMEM((total, first), BF16),
+            pltpu.VMEM((total, first), BF16), pltpu.VMEM((total, second), BF16),
+            pltpu.VMEM((total, second), BF16), pltpu.VMEM((nb, sz.rows, embed), BF16),
+            pltpu.VMEM((buckets, total), BF16), pltpu.VMEM(args["w_first"].shape, BF16),
+            pltpu.VMEM((256, first), BF16), pltpu.VMEM((first, second), BF16),
+            pltpu.VMEM((second, embed), BF16), pltpu.VMEM((total, second), BF16),
+            pltpu.VMEM((total, first), BF16), pltpu.VMEM((total, 256), BF16),
+            pltpu.VMEM((2, 4 * sz.width, 4 * total), BF16), pltpu.VMEM((4, 4 * total, LOW), BF16),
+            pltpu.VMEM((6, sz.width, 4 * LOW), F32), pltpu.VMEM((slots, LOW), BF16),
+            pltpu.VMEM((sz.x_width, first), F32), pltpu.VMEM((first, second), F32),
+            pltpu.VMEM((second, embed), F32),
+            dma((10,)), dma((4,)), dma((6,)), dma((3 + 2 * sz.col,)),
+        ],
+        compiler_params=pltpu.CompilerParams(vmem_limit_bytes=62 * 2**20),
+        name="back",
+    )(*kept, args["w_first"], args["w_second"], args["w_third"])
+
+
+def fast_device(sz, *inputs):
+    names = (
+        "watch_ids", "search_ids", "demo_ids", "pos_ids", "neg_ids", "valid_counts", "watch_table",
+        "search_table", "demo_table", "out_table", "w_first", "b_first", "w_second", "b_second",
+        "w_third", "b_third",
+    )
+    args = dict(zip(names, inputs))
+    (
+        counts, x, act1, slope1, act2, slope2, gu, buckets, neg_rows, pos_rows, slots, user_vecs, loss, fits,
+    ) = front(sz, args)
+
+    def finish(*operands):
+        kept = (neg_rows, pos_rows, slots, counts, x, act1, slope1, act2, slope2, gu, buckets)
+        watch, search, table, gw1, gw2, gw3, demo, gb1, gb2, gb3 = back(sz, args, kept)
+        return (
+            user_vecs, loss.reshape(()), watch, search, table, demo.T, gw1, gb1.reshape(-1),
+            gw2, gb2.reshape(-1), gw3, gb3.reshape(-1),
+        )
+
+    def general(*operands):
+        return per_device(RingCollectives(), *operands)
+
+    return lax.cond(fits.reshape(()) > 0, finish, general, *inputs)
+
+
+def fast_sizes(mesh, shapes):
+    watch, demo, negs, table, first = shapes
+    batch, col = mesh.shape["batch"], mesh.shape["col"]
+    rows, width, vocab = watch[0] // batch, table[0] // col, table[1] // batch
+    demo_width = first[0] - 2 * table[0]
+    sz = Sizes(batch, col, rows, watch[1], width, vocab, negs[0], table[0], demo_width)
+    good = (
+        batch == 8 and col == 4 and rows == 128 and watch[1] <= BAG_PAD and width == 64
+        and vocab == 32 * LOW and table[1] <= 65536 and demo[1] <= 4 and demo_width <= 128
+        and negs[0] % 128 == 0 and negs[0] <= 256 * CHUNK
+    )
+    return sz if good else None
+
+
 def solution(mesh):
     in_specs = (
         P("batch", None),
@@ -267,6 +1269,15 @@
         P(),
         P(),
     )
-    return jax.shard_map(
-        per_device, mesh=mesh, in_specs=in_specs, out_specs=out_specs, check_vma=False
-    )
+    def whole(*inputs):
+        shapes = [inputs[i].shape for i in (0, 2, 4, 6, 10)]
+        sz = fast_sizes(mesh, shapes)
+        if sz is None:
+            body = functools.partial(per_device, Collectives())
+        else:
+            body = functools.partial(fast_device, sz)
+        return jax.shard_map(
+            body, mesh=mesh, in_specs=in_specs, out_specs=out_specs, check_vma=False
+        )(*inputs)
+
+    return whole

time: 651 us -> 128 us (0.20); the launches traced: 643 us -> 127 us
  blocking collectives: 272 us -> 0 us
  matrix products: 176 us -> 0 us
  Pallas kernels: 0 us -> 122 us
  waiting for transfers between devices: 96.7 us -> 0 us
  local copies, waits for them, and re-layouts: 42.4 us -> 1.35 us
  other arithmetic: 38.9 us -> 0 us
  between operations: 17.2 us -> 3.77 us
    all_gather x9 -> x0, blocking collectives: 189 us -> none  [the longest x1 34.1 us: per_device(): lax.all_gather(pos_bf, 'col', axis=0, tiled=True)]
    dot_general x22 -> x0, matrix products: 176 us -> none  [the longest x2 79.4 us: bag_counts(): jnp.einsum('rbh,rbl->rhl', high_hot, low_hot, preferred_element_type=jnp....]
    pallas_call x0 -> x2, Pallas kernels: none -> 122 us  [the longest x1 84.3 us: front(): pl.pallas_call(functools.partial(front_kernel, sz), out_shape=[o for o, _...]
    psum x1 -> x0, waiting for transfers between devices: 93.6 us -> none  [per_device(): lax.psum((grad_w_first, grad_b_first, grad_w_second, grad_b_second, grad_...]
    psum x2 -> x0, blocking collectives: 83 us -> none  [the longest x1 63.6 us: per_device(): lax.psum((neg_part, jnp.sum(valid_counts).astype(jnp.float32)), 'batch')]
    scatter-add x1 -> x0, other arithmetic: 34 us -> none  [per_device(): jnp.zeros((col_width, vocab_rows + 1), jnp.float32).at[:, neg_local]]
    gather x2 -> x0, local copies, waits for them, and re-layouts: 20.3 us -> none  [per_device(): neg_part = jnp.take(padded_out, neg_local, axis=1).astype(jnp.float32)]
    unnamed x46 -> x11, local copies, waits for them, and re-layouts: 10 us -> 1.35 us
  transfers between devices with their start and end apart: 5 -> 0, of which waited for: 2 -> 0; matrix products, arithmetic and copies ran while one was open for 27% -> 0% of each run, Pallas kernels for 0% -> 0%
where the time goes in v2:
time: 128 us; the launch traced here: 127 us
  Pallas kernels  122 us (95%)
  between operations  3.77 us (3%)
  local copies, waits for them, and re-layouts  1.35 us (1%)
    pallas_call x1, Pallas kernels, front(): pl.pallas_call(functools.partial(front_kernel, sz), out_shape=[o for o, _...  84.3 us
    pallas_call x1, Pallas kernels, back(): pl.pallas_call(functools.partial(back_kernel, sz), out_shape=[o for o, _...  37.8 us

profile of v2, /device:TPU:1, one launch (start us, length us, event | category | flops | bytes accessed | tf_op | source)
XLA Modules:
  0.0 127.4 jit_solution(10253493435498750815)
XLA Ops:
  1.3 0.0 copy-start.29
  1.3 0.0 copy-start.35
  1.3 0.0 copy-start.38
  1.3 0.0 copy-start.48
  1.3 84.3 %front.1 = (bf16[2,8,4096,256]{3,2,1,0:T(8,128)(2,1)}, bf16[1024,640]{1,0:T(8,128)(2,1)}, bf16[1024,1024]{1,0:T(8,128)(2,1)}, bf16[1024,1024]{1,0:T(8,128)(2,1)}...) custom-call(s32[50,128]{1,0:T(8,128)} %bitcast.214.watch_ids, ...), custom_call_target="tpu_custom_call" | custom-call | tf_op jit(solution)/shard_map/front/pallas_call | solution.py:998
  86.2 0.0 copy-done.29
  86.2 0.0 copy-done.35
  86.3 0.0 copy-done.38
  86.3 0.0 copy-done.48
  86.3 38.1 %conditional.1 = (bf16[32,256]{1,0:T(8,128)(2,1)}, f32[]{:T(128)}, f32[64,8192]{1,0:T(8,128)}, f32[64,8192]{1,0:T(8,128)}, f32[64,8192]{1,0:T(8,128)}, /*index=5...) conditional(s32[]{:T(128)} %bitcast.223, ...), branch_computations={%region_0.16_spmd, %region_10.17_spmd} | conditional | flops 10206007296 | bytes 622236800 | solution.py:1222
  86.5 37.8 %back.1 = (f32[64,8192]{1,0:T(8,128)}, f32[64,8192]{1,0:T(8,128)}, f32[64,8192]{1,0:T(8,128)}, f32[600,1024]{1,0:T(8,128)}, f32[1024,512]{1,0:T(8,128)}, /*index...) custom-call(bf16[64,768]{1,0:T(8,128)(2,1)} %get-tuple-element.154.neg_rows, ...), custom_call_target="tpu_custom_call" | custom-call | tf_op jit(solution)/shard_map/cond/branch_1_fun/back/pallas_call | solution.py:1176
  124.3 0.0 copy-start.45
  124.4 1.3 %copy.312 = bf16[32,256]{1,0:T(8,128)(2,1)} copy(bf16[32,256]{1,0:T(8,128)(2,1)} %get-tuple-element.580) | data formatting | bytes 32768
  126.3 0.0 copy-done.45
Async XLA Ops:
  1.3 84.9 %copy-start.29 = (s32[5120]{0:T(1024)S(1)}, s32[5120]{0:T(1024)}, u32[]{:S(2)}) copy-start(s32[5120]{0:T(1024)} %param.34) | copy-start | bytes 61444
  1.3 84.9 %copy-start.35 = (f32[1024]{0:T(1024)S(1)}, f32[1024]{0:T(1024)}, u32[]{:S(2)}) copy-start(f32[1024]{0:T(1024)} %param.41) | copy-start | bytes 12292
  1.3 84.9 %copy-start.38 = (s32[128,4]{0,1:T(4,128)S(1)}, s32[128,4]{0,1:T(4,128)}, u32[]{:S(2)}) copy-start(s32[128,4]{0,1:T(4,128)} %param.32) | copy-start | bytes 6148
  1.3 84.9 %copy-start.48 = (s32[128]{0:T(128)S(1)}, s32[128]{0:T(128)}, u32[]{:S(2)}) copy-start(s32[128]{0:T(128)} %param.33) | copy-start | bytes 1540
  124.3 2.0 %copy-start.45 = (f32[1024]{0:T(1024)}, f32[1024]{0:T(1024)S(1)}, u32[]{:S(2)}) copy-start(f32[1024]{0:T(1024)S(1)} %get-tuple-element.587) | copy-start | bytes 12292

commit v3 on v2

--- a/solution.py
+++ b/solution.py
@@ -333,13 +333,6 @@
     )
 
 
-def spread_matrix(rows):
-    shape = (rows, 4 * rows)
-    r, m = iota(shape, 0), iota(shape, 1)
-    groups = rows // ROWS_IN_GROUP
-    return one_where((r % groups == m // 16) & (r // groups == m % ROWS_IN_GROUP), BF16)
-
-
 class Sizes:
     def __init__(self, batch, col, rows, bag, width, vocab, negs, embed, demo_width):
         self.batch, self.col, self.rows, self.bag = batch, col, rows, bag
@@ -364,12 +357,12 @@
     sz,
     watch_ids, search_ids, demo_ids, pos_ids, neg_ids, demo_table, b_first, b_second, b_third, valid_count,
     watch_table, search_table, out_table, w_first, w_second, w_third,
-    counts_out, x_out, act1_out, slope1_out, act2_out, slope2_out, gu_out, buckets_out,
+    counts_out, x_out, act1_out, act2_out, gu_out, gps_out, gpf_out, gx_out, buckets_out,
     neg_rows_out, pos_rows_out, slots_out, user_out, loss_out, fits_out,
-    tabs, tall, mix, w1_raw, w1, w2, w3, turned, ids, neg_dest, neg_digits, counts, found_sums, sums, pieces, x,
+    tabs, tall, mix, w1_raw, w1, w1_own, w2, w3, turned, upright, lines_own, ids, side, neg_dest, neg_digits, counts, found_sums, sums, pieces, x,
     pre1, pre2, acts1, slopes1, acts2, slopes2, users, buckets, slots, picked, neg_all, pos_all, e_cols,
-    e_rows, probs, stats, g_send, g_recv, gu, rg_send, rg_recv, gp_all, loss_all,
-    local_sem, out_sem, count_sem, ids_s, ids_r, rs_s, rs_r, ag_s, ag_r, xx_s, xx_r, co_s, co_r,
+    e_rows, probs, stats, g_send, g_recv, gu, gps, gpf, gx, rg_send, rg_recv, gp_all, loss_all,
+    local_sem, out_sem, down_sem, count_sem, ids_s, ids_r, sd_s, sd_r, ic_s, ic_r, rs_s, rs_r, ag_s, ag_r, xx_s, xx_r, co_s, co_r,
     ne_s, ne_r, pe_s, pe_r, st_s, st_r, gs_s, gs_r, ga_s, ga_r, gx_s, gx_r, gc_s, gc_r,
     rg_s, rg_r, gp_s, gp_r, lo_s, lo_r,
 ):
@@ -415,15 +408,34 @@
 
     turned[...] = jnp.zeros((BAG_PAD, 128), I32)
     turned[0 : sz.bag, :] = (watch_ids[...] & 0xFFFF) | (search_ids[...] << 16)
-    packed = turned[...].T
+    upright[...] = turned[...].T
     for r4 in range(ROWS_IN_GROUP):
-        ids[b, 0 : sz.groups, r4 * BAG_PAD : (r4 + 1) * BAG_PAD] = packed[
-            r4 * sz.groups : (r4 + 1) * sz.groups, :
+        lines_own[:, r4 * BAG_PAD : (r4 + 1) * BAG_PAD] = upright[
+            pl.ds(r4, sz.groups, stride=ROWS_IN_GROUP), :
         ]
-    ids[b, sz.groups : sz.groups + 8, :] = jnp.zeros((8, CHUNK), I32)
-    ids[b, sz.groups : sz.groups + 1, 0:128] = pos_ids[...]
-    ids[b, sz.groups + 1 : sz.groups + 2, 0:128] = jnp.full((1, 128), valid_count[0], I32)
-    ids[b, sz.groups + 2 : sz.groups + 2 + demo_ids.shape[0], 0:128] = demo_ids[...]
+    share = sz.groups // nc
+
+    def share_of(col):
+        return pl.ds(pl.multiple_of(col * share, share), share)
+
+    ids[b, share_of(c), :] = lines_own[share_of(c), :]
+    side[b] = jnp.zeros((8, 128), I32)
+    side[b, 0:1, :] = pos_ids[...]
+    side[b, 1:2, :] = jnp.full((1, 128), valid_count[0], I32)
+    side[b, 2 : 2 + demo_ids.shape[0], :] = demo_ids[...]
+
+    pl.semaphore_wait(barrier, nb - 1 + nc - 1)
+    last_sends = []
+    for i in range(1, nb):
+        place = ids.at[b, share_of(c)]
+        copy = send(place, place, ids_s.at[i - 1], ids_r.at[i - 1], (batch_peer(i), c))
+        copy.start()
+        last_sends.append(copy)
+
+    for i in range(1, nb):
+        copy = send(side.at[b], side.at[b], sd_s.at[i - 1], sd_r.at[i - 1], (batch_peer(i), c))
+        copy.start()
+        last_sends.append(copy)
 
     negs = neg_ids[...]
     lines = sz.neg_lines
@@ -466,6 +478,14 @@
         slots[k, 0:1, :] = neg_high[:, k * CHUNK : (k + 1) * CHUNK]
         slots[k, 1:2, :] = neg_low[:, k * CHUNK : (k + 1) * CHUNK]
 
+    for i in range(1, nb):
+        place = ids.at[batch_from(i), share_of(c)]
+        send(place, place, ids_s.at[i - 1], ids_r.at[i - 1], (b, c)).wait_recv()
+    for i in range(1, nc):
+        place = ids.at[:, share_of(c)]
+        copy = send(place, place, ic_s.at[i - 1], ic_r.at[i - 1], (b, col_peer(i)))
+        copy.start()
+        last_sends.append(copy)
     for t in range(2):
         loads[t].wait()
 
@@ -477,13 +497,6 @@
         return 0
 
     lax.fori_loop(0, 2 * sz.high_parts, turn, 0)
-
-    pl.semaphore_wait(barrier, nb - 1 + nc - 1)
-    last_sends = []
-    for i in range(1, nb):
-        copy = send(ids.at[b], ids.at[b], ids_s.at[i - 1], ids_r.at[i - 1], (batch_peer(i), c))
-        copy.start()
-        last_sends.append(copy)
 
     loads[2].wait()
 
@@ -527,72 +540,70 @@
     loads[4].wait()
     loads[5].wait()
 
-    for i in range(1, nb):
-        src = batch_from(i)
-        send(ids.at[src], ids.at[src], ids_s.at[i - 1], ids_r.at[i - 1], (b, c)).wait_recv()
-
-    all_pos = jnp.concatenate([ids[j, sz.groups : sz.groups + 1, 0:128] for j in range(nb)], axis=0)
-    valid = jnp.concatenate([ids[j, sz.groups + 1 : sz.groups + 2, 0:128] for j in range(nb)], axis=0)
-    pos_local = all_pos - offset
-    pos_owned = (pos_local >= 0) & (pos_local < sz.vocab)
-    pos_pair = jnp.concatenate(
-        [
-            jnp.where(pos_owned, pos_local >> 8, 255).astype(F32),
-            (pos_local & 255).astype(F32),
-        ],
-        axis=0,
-    ).astype(BF16)
-    shape = (nb, CHUNK)
-    at_block = iota(shape, 1) // sz.quarter == iota(shape, 0)
-    for quarter in range(nc):
-        shape = (128, CHUNK)
-        pick = one_where(iota(shape, 0) == quarter * sz.quarter + iota(shape, 1) % sz.quarter, BF16)
-        wide = dot_as(pos_pair, pick, 1, 0)
-        high = jnp.sum(jnp.where(at_block, wide[0:nb], 0.0), axis=0, keepdims=True)
-        low = jnp.sum(jnp.where(at_block, wide[nb : 2 * nb], 0.0), axis=0, keepdims=True)
-        slots[sz.cap_tiles + quarter, 0:1, :] = jnp.where(high > 254.0, -1.0, high)
-        slots[sz.cap_tiles + quarter, 1:2, :] = low
-    slots_out[...] = slots[...]
-    lax.fori_loop(sz.cap_tiles, sz.tiles, pick_tile, 0)
-    pos_all[c] = picked[sz.cap_tiles + c]
+    w1_own[...] = jnp.zeros(w1_own.shape, BF16)
+    w1_own[0 : 2 * width, :] = w1[pl.ds(pl.multiple_of(c * 128, 128), 128), :]
+    w1_own[2 * width : 2 * width + sz.demo_width, :] = w1_raw[2 * embed :, :]
     for i in range(1, nc):
+        place = ids.at[:, share_of(col_from(i))]
+        send(place, place, ic_s.at[i - 1], ic_r.at[i - 1], (b, c)).wait_recv()
+
+    users_shape = (nb, CHUNK)
+    at_block = iota(users_shape, 1) // sz.quarter == iota(users_shape, 0)
+
+    def demo_part():
+        for i in range(1, nb):
+            place = side.at[batch_from(i)]
+            send(place, place, sd_s.at[i - 1], sd_r.at[i - 1], (b, c)).wait_recv()
+        bucket_total = jnp.zeros((buckets.shape[0], sz.total), BF16)
+        bucket_line = iota((buckets.shape[0], sz.total), 0).astype(BF16)
+        for field in range(demo_ids.shape[0]):
+            line = jnp.concatenate([side[j, 2 + field : 3 + field, :] for j in range(nb)], axis=1)
+            bucket_total = bucket_total + one_where(line.astype(F32).astype(BF16) == bucket_line, BF16)
+        buckets[...] = bucket_total
+        demo_rows = demo_table[...].astype(F32).T.astype(BF16)
+        x[:, nc * 128 :] = jnp.zeros((sz.total, 128), BF16)
+        x[:, nc * 128 : nc * 128 + sz.demo_width] = dot_as(bucket_total, demo_rows, 0, 0).astype(BF16)
+
+    def pos_part():
+        all_pos = jnp.concatenate([side[j, 0:1, :] for j in range(nb)], axis=0)
+        pos_local = all_pos - offset
+        pos_owned = (pos_local >= 0) & (pos_local < sz.vocab)
+        pos_pair = jnp.concatenate(
+            [
+                jnp.where(pos_owned, pos_local >> 8, 255).astype(F32),
+                (pos_local & 255).astype(F32),
+            ],
+            axis=0,
+        ).astype(BF16)
+        for quarter in range(nc):
+            shape = (128, CHUNK)
+            pick = one_where(iota(shape, 0) == quarter * sz.quarter + iota(shape, 1) % sz.quarter, BF16)
+            wide = dot_as(pos_pair, pick, 1, 0)
+            high = jnp.sum(jnp.where(at_block, wide[0:nb], 0.0), axis=0, keepdims=True)
+            low = jnp.sum(jnp.where(at_block, wide[nb : 2 * nb], 0.0), axis=0, keepdims=True)
+            slots[sz.cap_tiles + quarter, 0:1, :] = jnp.where(high > 254.0, -1.0, high)
+            slots[sz.cap_tiles + quarter, 1:2, :] = low
+        slots_out[...] = slots[...]
+        lax.fori_loop(sz.cap_tiles, sz.tiles, pick_tile, 0)
+        pos_all[c] = picked[sz.cap_tiles + c]
+        for i in range(1, nc):
+            pos_send(i).start()
+
+    def pos_send(i):
         to = col_peer(i)
-        copy = send(picked.at[sz.cap_tiles + to], pos_all.at[c], pe_s.at[i - 1], pe_r.at[i - 1], (b, to))
-        copy.start()
-        last_sends.append(copy)
-
-    valid_wide = jnp.concatenate([valid] * (sz.users // 128), axis=1).astype(F32)
-    live_count = jnp.sum(jnp.where(at_block, valid_wide, 0.0), axis=0, keepdims=True)
-    valid_total = jnp.sum(valid_wide, axis=0, keepdims=True)
-    user_place = c * sz.quarter + iota((1, sz.users), 1) % sz.quarter
-    weight = jnp.where(user_place.astype(F32) < live_count, 1.0 / valid_total, 0.0)
-
-    bucket_total = jnp.zeros((buckets.shape[0], sz.total), BF16)
-    bucket_line = iota((buckets.shape[0], sz.total), 0).astype(BF16)
-    for field in range(demo_ids.shape[0]):
-        row = sz.groups + 2 + field
-        line = jnp.concatenate([ids[j, row : row + 1, 0:128] for j in range(nb)], axis=1)
-        bucket_total = bucket_total + one_where(line.astype(F32).astype(BF16) == bucket_line, BF16)
-    buckets[...] = bucket_total
-    demo_rows = demo_table[...].astype(F32).T.astype(BF16)
-    x[:, nc * 128 :] = jnp.zeros((sz.total, 128), BF16)
-    x[:, nc * 128 : nc * 128 + sz.demo_width] = dot_as(bucket_total, demo_rows, 0, 0).astype(BF16)
-    buckets_copy = pltpu.make_async_copy(buckets, buckets_out, out_sem.at[0])
-    buckets_copy.start()
-
-    spread = spread_matrix(sz.rows)
+        return send(picked.at[sz.cap_tiles + to], pos_all.at[c], pe_s.at[i - 1], pe_r.at[i - 1], (b, to))
+
     span = sz.span
     piece = span // nb
-    span_lines = 4 * span
     lane_mod = iota((16, CHUNK), 1) % BAG_PAD
     lane_r4 = iota((16, CHUNK), 1) // BAG_PAD
     blocks = span // sz.rows
     parts_in_block = sz.groups // 16
 
     def count_copy(t, table, slot_at):
-        rows = pl.ds(pl.multiple_of(t * span_lines, span_lines), span_lines)
+        rows = pl.ds(pl.multiple_of(t * span, span), span)
         return pltpu.make_async_copy(
-            counts.at[table, slot_at], counts_out.at[table, :, rows], count_sem.at[table, slot_at]
+            counts.at[table, slot_at], counts_out.at[table, :, :, rows], count_sem.at[table, slot_at]
         )
 
     def bag_table(t, table):
@@ -613,32 +624,39 @@
             mine = (local >= 0) & (local < sz.vocab) & (lane_mod < sz.bag)
             code = jnp.where(mine, (local >> 8) * 4 + lane_r4, -1).astype(F32).astype(BF16)
             low = (local & 255).astype(F32).astype(BF16)
-            for g in range(16):
-                left = one_where(code[g : g + 1, :] == code_line, FP8)
-                right = one_where(low[g : g + 1, :] == low_line, FP8)
-                found = dot_as(left, right, 1, 1).astype(BF16)
-                line = pl.ds(pl.multiple_of(q * 256 + g * 16, 16), 16)
-                for hh in range(sz.high_parts):
-                    counts[table, slot_at, hh, line, :] = found[hh * 16 : (hh + 1) * 16, :]
+            low_half = iota((sz.high // 2, 8, LOW), 1) < 4
+            for quad in range(4):
+                pairs = []
+                for pair in range(2):
+                    found = []
+                    for g in (quad * 4 + pair * 2, quad * 4 + pair * 2 + 1):
+                        left = one_where(code[g : g + 1, :] == code_line, FP8)
+                        right = one_where(low[g : g + 1, :] == low_line, FP8)
+                        found.append(dot_as(left, right, 1, 1).reshape(sz.high // 2, 8, LOW))
+                    even = jnp.where(low_half, found[0], pltpu.roll(found[1], 4, 1))
+                    odd = jnp.where(low_half, pltpu.roll(found[0], 4, 1), found[1])
+                    pairs.append((even, odd))
+                line = pl.ds(pl.multiple_of(q * 64 + quad * 16, 16), 16)
+                for part in range(sz.high):
+                    both = [pairs[k][part % 2][part // 2] for k in range(2)]
+                    counts[table, slot_at, part // 4, part % 4, line, :] = jnp.concatenate(
+                        both, axis=0
+                    ).astype(BF16)
             return 0
 
         lax.fori_loop(0, blocks * parts_in_block, groups_of, 0)
         count_copy(t, table, slot_at).start()
-        left = jnp.concatenate([counts[table, slot_at, hh] for hh in range(sz.high_parts)], axis=1)
+        left = jnp.concatenate(
+            [counts[table, slot_at, hh].reshape(4 * span, LOW) for hh in range(sz.high_parts)], axis=1
+        )
         total = dot_as(left, mix[table], 1, 0)
-        shape = (span_lines, 4 * width)
-        total = jnp.where((iota(shape, 0) // 4) % 4 == iota(shape, 1) // width, total, 0.0)
-        half = (total[:, :128] + total[:, 128:]).astype(BF16)
-        for k in range(blocks):
-            found = dot_as(spread, half[k * 4 * sz.rows : (k + 1) * 4 * sz.rows], 1, 0)
-            found_sums[table, k * sz.rows : (k + 1) * sz.rows, :] = found + pltpu.roll(found, width, 1)
-
-    def bag_step(t):
-        def one_table(table, _):
-            bag_table(t, table)
-            return 0
-
-        lax.fori_loop(0, 2, one_table, 0)
+        left_side = iota((span, 128), 1) < width
+        first = jnp.where(left_side, total[0:span, 0:128], total[span : 2 * span, 0:128])
+        second = jnp.where(left_side, total[2 * span : 3 * span, 128:], total[3 * span :, 128:])
+        both = first + second
+        found_sums[table] = both + pltpu.roll(both, width, 1)
+
+    def bag_sums(t):
         joined = jnp.where(iota((span, 128), 1) < width, found_sums[0], found_sums[1])
         sums[t] = joined.astype(BF16)
         for i in range(1, nb):
@@ -701,38 +719,70 @@
         slopes1[at, :] = gelu_slope(pre1[at, :]).astype(BF16)
         slopes2[at, :] = gelu_slope(pre2[at, :]).astype(BF16)
 
-    def step(t, _):
-        @pl.when(t < sz.steps)
+    bag_ticks = 2 * sz.steps
+    last = sz.steps - 1
+
+    def tick(n, _):
+        half = n // 2
+        odd = lax.rem(n, 2) == 1
+
+        @pl.when(n < bag_ticks)
         def _():
-            bag_step(t)
-
-        @pl.when((t >= 1) & (t < sz.steps + 1))
+            bag_table(half, lax.rem(n, 2))
+
+        @pl.when((n < bag_ticks) & odd)
         def _():
-            reduce_step(t - 1)
-
-        @pl.when((t >= 2) & (t < sz.steps + 2))
+            bag_sums(half)
+
+        @pl.when(n == bag_ticks)
         def _():
-            cross_step(t - 2)
-
-        @pl.when((t >= 3) & (t < sz.steps + 3))
+            demo_part()
+
+        @pl.when(n == bag_ticks + 1)
         def _():
-            core_step(t - 3)
-
-        @pl.when(t >= 4)
+            pos_part()
+
+        @pl.when(odd & (n >= 5))
         def _():
-            full_step(t - 4)
-
-        @pl.when(t >= sz.steps)
+            full_step((n - 5) // 2)
+
+        done = jnp.where(n <= bag_ticks, 0, jnp.where(n <= bag_ticks + 2, 1, last))
+        ready = jnp.where(
+            n < bag_ticks, 0, jnp.where(n <= bag_ticks + 1, 1, jnp.where(n == bag_ticks + 2, last, sz.steps))
+        )
+
+        def some_tower(k, _):
+            tower(k)
+            return 0
+
+        lax.fori_loop(done, ready, some_tower, 0)
+
+        @pl.when((~odd) & (n >= 2) & (n <= bag_ticks))
         def _():
-            tower(t - sz.steps)
+            reduce_step(half - 1)
+
+        @pl.when(odd & (n >= 3) & (n <= bag_ticks + 1))
+        def _():
+            cross_step((n - 3) // 2)
+
+        @pl.when((~odd) & (n >= 4) & (n <= bag_ticks + 2))
+        def _():
+            core_step(half - 2)
 
         return 0
 
-    lax.fori_loop(0, sz.steps + 4, step, 0)
-
-    out_copies = [(x, x_out), (acts1, act1_out), (acts2, act2_out), (slopes1, slope1_out), (slopes2, slope2_out)]
-    out_copies = [pltpu.make_async_copy(s, d, out_sem.at[1 + i]) for i, (s, d) in enumerate(out_copies)]
-    for copy in out_copies[:3]:
+    lax.fori_loop(0, bag_ticks + 4, tick, 0)
+
+    valid = jnp.concatenate([side[j, 1:2, :] for j in range(nb)], axis=0)
+    valid_wide = jnp.concatenate([valid] * (sz.users // 128), axis=1).astype(F32)
+    live_count = jnp.sum(jnp.where(at_block, valid_wide, 0.0), axis=0, keepdims=True)
+    valid_total = jnp.sum(valid_wide, axis=0, keepdims=True)
+    user_place = c * sz.quarter + iota((1, sz.users), 1) % sz.quarter
+    weight = jnp.where(user_place.astype(F32) < live_count, 1.0 / valid_total, 0.0)
+
+    out_copies = [(x, x_out), (acts1, act1_out), (acts2, act2_out), (buckets, buckets_out)]
+    out_copies = [pltpu.make_async_copy(s, d, out_sem.at[i]) for i, (s, d) in enumerate(out_copies)]
+    for copy in out_copies:
         copy.start()
     user_out[...] = users[pl.ds(pl.multiple_of(b * sz.rows + c * sz.quarter, sz.quarter), sz.quarter), :]
 
@@ -824,8 +874,6 @@
             last_sends.append(copy)
     rg_recv[c] = rg_send[c]
     lax.fori_loop(sz.steps // 2, sz.steps, some_slopes, 0)
-    for copy in out_copies[3:]:
-        copy.start()
     for i in range(1, nb):
         send(g_send.at[0], g_recv.at[i - 1], gs_s.at[i - 1], gs_r.at[i - 1], (b, c)).wait_recv()
     total = g_send[b].astype(F32)
@@ -854,6 +902,68 @@
     copy.start()
     last_sends.append(copy)
 
+    def rows_at(ref, col):
+        return ref.at[:, pl.ds(pl.multiple_of(col * sz.quarter, sz.quarter), sz.quarter), :]
+
+    def down_copies(col, i):
+        return [
+            pltpu.make_async_copy(rows_at(kept, col), rows_at(out, col), down_sem.at[i, k])
+            for k, (kept, out) in enumerate(((gps, gps_out), (gpf, gpf_out), (gx, gx_out)))
+        ]
+
+    def down(i, col):
+        def spread_out(ref, value):
+            for j in range(nb):
+                ref[j, pl.ds(pl.multiple_of(col * sz.quarter, sz.quarter), sz.quarter), :] = value[
+                    j * sz.quarter : (j + 1) * sz.quarter
+                ]
+
+        def gathered(ref):
+            return jnp.concatenate(
+                [
+                    ref[pl.ds(pl.multiple_of(j * sz.rows + col * sz.quarter, sz.quarter), sz.quarter), :]
+                    for j in range(nb)
+                ],
+                axis=0,
+            )
+
+        top = jnp.concatenate(
+            [gu[j, pl.ds(pl.multiple_of(col * sz.quarter, sz.quarter), sz.quarter), :] for j in range(nb)],
+            axis=0,
+        )
+        second = (dot_as(top, w3[...], 1, 1) * gathered(slopes2).astype(F32)).astype(BF16)
+        spread_out(gps, second)
+        first = (dot_as(second, w2[...], 1, 1) * gathered(slopes1).astype(F32)).astype(BF16)
+        spread_out(gpf, first)
+        spread_out(gx, dot_as(first, w1_own[...], 1, 1).astype(BF16))
+        for copy in down_copies(col, i):
+            copy.start()
+
+    def quarter_down(i, _):
+        flip = jnp.where(i == 0, c, jnp.where(i == 1, cx, jnp.where(i == 2, ck, ckx)))
+
+        @pl.when(i == 1)
+        def _():
+            for k in range(nb):
+                src = batch_from(k)
+                send(gu_at(src, cx), gu_at(src, cx), gx_s.at[k], gx_r.at[k], (b, cx)).wait_recv()
+            send(gu_all(cx), gu_all(cx), gc_s.at[1], gc_r.at[1], (b, ck)).start()
+
+        @pl.when(i == 2)
+        def _():
+            send(gu_all(ck), gu_all(ck), gc_s.at[0], gc_r.at[0], (b, ck)).wait_recv()
+
+        @pl.when(i == 3)
+        def _():
+            send(gu_all(ckx), gu_all(ckx), gc_s.at[1], gc_r.at[1], (b, ck)).wait_recv()
+
+        down(i, flip)
+        return 0
+
+    lax.fori_loop(0, nc, quarter_down, 0)
+    gu_copy = pltpu.make_async_copy(gu, gu_out, out_sem.at[4])
+    gu_copy.start()
+
     pick_own = one_where(iota((width, embed), 1) == c * width + iota((width, embed), 0), BF16)
     for i in range(1, nc):
         src = col_from(i)
@@ -866,13 +976,6 @@
             mine, grad * own_part, 0.0
         ).astype(BF16)
 
-    for i in range(nb):
-        src = batch_from(i)
-        send(gu_at(src, cx), gu_at(src, cx), gx_s.at[i], gx_r.at[i], (b, cx)).wait_recv()
-    copy = send(gu_all(cx), gu_all(cx), gc_s.at[1], gc_r.at[1], (b, ck))
-    copy.start()
-    last_sends.append(copy)
-
     for i in range(1, nc):
         src = col_from(i)
         send(loss_all.at[src], loss_all.at[src], lo_s.at[i - 1], lo_r.at[i - 1], (b, c)).wait_recv()
@@ -885,11 +988,9 @@
     neg_rows_out[...] = neg_total.astype(BF16)
     loss_out[...] = loss[0:1, 0:1]
 
-    for i, col in enumerate((ck, ckx)):
-        send(gu_all(col), gu_all(col), gc_s.at[i], gc_r.at[i], (b, ck)).wait_recv()
-    gu_copy = pltpu.make_async_copy(gu, gu_out, out_sem.at[6])
-    gu_copy.start()
-
+    last_sends.append(send(gu_all(cx), gu_all(cx), gc_s.at[1], gc_r.at[1], (b, ck)))
+    for i in range(1, nc):
+        last_sends.append(pos_send(i))
     for copy in last_sends:
         copy.wait_send()
 
@@ -906,10 +1007,12 @@
     for table in range(2):
         for t in (sz.steps - 2, sz.steps - 1):
             count_copy(t, table, t % 2).wait()
-    buckets_copy.wait()
     gu_copy.wait()
     for copy in out_copies:
         copy.wait()
+    for i, col in enumerate((c, cx, ck, ckx)):
+        for copy in down_copies(col, i):
+            copy.wait()
 
 
 def front(sz, args):
@@ -919,7 +1022,6 @@
     first, second = args["w_second"].shape
     buckets = args["demo_table"].shape[0]
     x_width = sz.x_width
-    span_lines = 4 * sz.span
     vmem = pl.BlockSpec(memory_space=pltpu.VMEM)
     smem = pl.BlockSpec(memory_space=pltpu.SMEM)
     hbm = pl.BlockSpec(memory_space=pl.ANY)
@@ -929,10 +1031,10 @@
         return jax.ShapeDtypeStruct(dims, kind)
 
     outs = [
-        (shape((2, sz.high_parts, 4 * total, LOW)), hbm), (shape((total, x_width)), hbm),
-        (shape((total, first)), hbm), (shape((total, first)), hbm),
-        (shape((total, second)), hbm), (shape((total, second)), hbm),
-        (shape((nb, sz.rows, embed)), hbm), (shape((buckets, total)), hbm),
+        (shape((2, sz.high_parts, 4, total, LOW)), hbm), (shape((total, x_width)), hbm),
+        (shape((total, first)), hbm), (shape((total, second)), hbm), (shape((nb, sz.rows, embed)), hbm),
+        (shape((nb, sz.rows, second)), hbm), (shape((nb, sz.rows, first)), hbm),
+        (shape((nb, sz.rows, 256)), hbm), (shape((buckets, total)), hbm),
         (shape((width, cap)), vmem), (shape((width, total)), vmem),
         (shape((sz.tiles, 8, CHUNK), F32), vmem),
         (shape((sz.quarter, embed)), vmem), (shape((1, 1), F32), vmem), (shape((1, 1), I32), vmem),
@@ -943,13 +1045,17 @@
         pltpu.VMEM((2, sz.high_parts * LOW, 4 * width), BF16),
         pltpu.VMEM(args["w_first"].shape, BF16),
         pltpu.VMEM((x_width, first), BF16),
+        pltpu.VMEM((256, first), BF16),
         pltpu.VMEM((first, second), BF16),
         pltpu.VMEM((second, embed), BF16),
         pltpu.VMEM((BAG_PAD, 128), I32),
-        pltpu.VMEM((nb, sz.groups + 8, CHUNK), I32),
+        pltpu.VMEM((sz.rows, BAG_PAD), I32),
+        pltpu.VMEM((sz.groups, CHUNK), I32),
+        pltpu.VMEM((nb, sz.groups, CHUNK), I32),
+        pltpu.VMEM((nb, 8, 128), I32),
         pltpu.VMEM((sz.neg_lines, CHUNK), F32),
         pltpu.VMEM((4, sz.neg_lines, CHUNK), F32),
-        pltpu.VMEM((2, 2, sz.high_parts, span_lines, LOW), BF16),
+        pltpu.VMEM((2, 2, sz.high_parts, 4, sz.span, LOW), BF16),
         pltpu.VMEM((2, sz.span, 128), F32),
         pltpu.VMEM((sz.steps, sz.span, 128), BF16),
         pltpu.VMEM((sz.steps, nb - 1, sz.span // nb, 128), BF16),
@@ -973,12 +1079,15 @@
         pltpu.VMEM((nb, sz.quarter, embed), BF16),
         pltpu.VMEM((nb - 1, sz.quarter, embed), BF16),
         pltpu.VMEM((nb, sz.rows, embed), BF16),
+        pltpu.VMEM((nb, sz.rows, second), BF16),
+        pltpu.VMEM((nb, sz.rows, first), BF16),
+        pltpu.VMEM((nb, sz.rows, 256), BF16),
         pltpu.VMEM((nc, width, cap), BF16),
         pltpu.VMEM((nc, width, cap), BF16),
         pltpu.VMEM((nc, 8, users), F32),
         pltpu.VMEM((nc, 8, 128), F32),
-        dma((6,)), dma((7,)), dma((2, 2)),
-        dma((nb - 1,)), dma((nb - 1,)),
+        dma((6,)), dma((5,)), dma((nc, 3)), dma((2, 2)),
+        dma((nb - 1,)), dma((nb - 1,)), dma((nb - 1,)), dma((nb - 1,)), dma((nc - 1,)), dma((nc - 1,)),
         dma((sz.steps, nb - 1)), dma((sz.steps,)), dma((sz.steps, nb - 1)), dma((sz.steps,)),
         dma((sz.steps,)), dma((sz.steps,)), dma((sz.steps, 2)), dma((sz.steps, 2)),
         dma((nc - 1,)), dma((nc - 1,)), dma((nc - 1,)), dma((nc - 1,)),
@@ -1009,23 +1118,20 @@
 
 
 def back_kernel(
-    sz, neg_rows, pos_rows, slots, counts, x_in, act1_in, slope1_in, act2_in, slope2_in, gu_in,
-    buckets_in, w_first, w_second, w_third,
+    sz, neg_rows, pos_rows, slots, counts, x_in, act1_in, act2_in, gu_in, gps_in, gpf_in, gx_in, buckets_in,
     watch_out, search_out, table_out, gw1_out, gw2_out, gw3_out, demo_out, gb1_out, gb2_out, gb3_out,
-    x, act1, slope1, act2, slope2, gu, buckets, w1, w1_own, w2, w3, gps, gpf, gx, spread_grads, ring,
+    x, act1, act2, gu, gps, gpf, gx, buckets, grads, ring,
     lines, low_rows, gw1, gw2, gw3, in_sem, ring_sem, line_sem, out_sem,
 ):
     width, cap, total, nb = sz.width, sz.cap, sz.total, sz.batch
     parts, nc, embed = sz.high_parts, sz.col, sz.embed
-    c = lax.axis_index("col")
     depth = ring.shape[0]
     names = [
-        (gu_in, gu), (w_third, w3), (slope2_in, slope2), (w_second, w2), (slope1_in, slope1),
-        (w_first, w1), (act2_in, act2), (act1_in, act1), (x_in, x), (buckets_in, buckets),
+        (gx_in, gx), (act2_in, act2), (gu_in, gu), (act1_in, act1), (gps_in, gps), (x_in, x), (gpf_in, gpf),
+        (buckets_in, buckets),
     ]
     loads = [pltpu.make_async_copy(s, d, in_sem.at[i]) for i, (s, d) in enumerate(names)]
-    for load in loads:
-        load.start()
+    loads[0].start()
 
     def ring_load(n):
         return pltpu.make_async_copy(
@@ -1034,51 +1140,75 @@
 
     for n in range(depth):
         ring_load(n).start()
-
-    loads[5].wait()
-    w1_own[...] = jnp.zeros(w1_own.shape, BF16)
-    w1_own[0:width, :] = w1[pl.ds(pl.multiple_of(c * width, width), width), :]
-    w1_own[width : 2 * width, :] = w1[pl.ds(pl.multiple_of(embed + c * width, width), width), :]
-    w1_own[2 * width : 2 * width + sz.demo_width, :] = w1[2 * embed :, :]
-    for load in loads[:5]:
-        load.wait()
-    half_blocks = nb // 2
-    half = half_blocks * sz.rows
-
-    def down(k, _):
-        at = pl.ds(pl.multiple_of(k * half, half), half)
-        top = gu[pl.ds(k * half_blocks, half_blocks)].reshape(half, embed)
-        second = (dot_as(top, w3[...], 1, 1) * slope2[at, :].astype(F32)).astype(BF16)
-        gps[at, :] = second
-        first = (dot_as(second, w2[...], 1, 1) * slope1[at, :].astype(F32)).astype(BF16)
-        gpf[at, :] = first
-        gx[at, :] = dot_as(first, w1_own[...], 1, 1).astype(BF16)
+    for load in loads[1:]:
+        load.start()
+    loads[0].wait()
+
+    grads[...] = gx[...].reshape(total, gx.shape[2])[:, 0:128].T
+
+    def line_store(out, slot, hh):
+        at = pl.ds(pl.multiple_of(hh * 4 * LOW, 4 * LOW), 4 * LOW)
+        return pltpu.make_async_copy(lines.at[slot], out.at[:, at], line_sem.at[slot])
+
+    def put(slot, found, factor):
+        for i in range(4):
+            lines[slot, :, i * LOW : (i + 1) * LOW] = found[i] * factor
+
+    for k in range(sz.tiles):
+        low = slots[k, 1:2, :].astype(BF16)
+        hot = one_where(low == iota((LOW, CHUNK), 0).astype(BF16), BF16)
+        low_rows[k * CHUNK : (k + 1) * CHUNK, :] = hot.T
+    high = jnp.concatenate([slots[k, 0:1, :] for k in range(sz.tiles)], axis=1).astype(BF16)
+    values = jnp.concatenate([neg_rows[...], pos_rows[...]], axis=1)
+
+    def scatter(n, _):
+        left = []
+        for i in range(8):
+            at = (n * 8 + i).astype(F32).astype(BF16)
+            left.append(jnp.where(high == at, values, jnp.zeros((), BF16)))
+        found = dot_as(jnp.concatenate(left, axis=0), low_rows[...], 1, 0)
+        for j in range(2):
+
+            @pl.when(n >= 1)
+            def _():
+                line_store(table_out, 4 + j, (n - 1) * 2 + j).wait()
+
+            put(4 + j, [found[(j * 4 + i) * width : (j * 4 + i + 1) * width] for i in range(4)], 1.0)
+            line_store(table_out, 4 + j, n * 2 + j).start()
         return 0
 
-    lax.fori_loop(0, 2, down, 0)
-
-    spread = spread_matrix(sz.rows)
-    shape = (4 * width, 4 * sz.rows)
-    mask = iota(shape, 0) // width == (iota(shape, 1) // 4) % 4
-
-    def lay(t, _):
-        rows = gx[pl.ds(pl.multiple_of(t * sz.rows, sz.rows), sz.rows), 0:128]
-        at = pl.ds(pl.multiple_of(t * 4 * sz.rows, 4 * sz.rows), 4 * sz.rows)
-        for table in range(2):
-            part = rows[:, table * width : (table + 1) * width]
-            wide = jnp.concatenate([part] * 4, axis=1)
-            laid = dot_as(wide, spread, 0, 0)
-            spread_grads[table, :, at] = jnp.where(mask, laid, 0.0).astype(BF16)
+    lax.fori_loop(0, parts // 2, scatter, 0)
+    def bags(hh, _):
+        for table, out in enumerate((watch_out, search_out)):
+            n = hh * 2 + table
+            slot = table * 2 + lax.rem(hh, 2)
+            ring_load(n).wait()
+            own = grads[table * width : (table + 1) * width, :]
+            found = [dot_as(own, ring[lax.rem(n, depth), i], 1, 0) for i in range(4)]
+
+            @pl.when(n + depth < 2 * parts)
+            def _():
+                ring_load(n + depth).start()
+
+            @pl.when(hh >= 2)
+            def _():
+                line_store(out, slot, hh - 2).wait()
+
+            put(slot, found, 1.0 / sz.bag)
+            line_store(out, slot, hh).start()
         return 0
 
-    lax.fori_loop(0, nb, lay, 0)
-
-    for load in loads[6:]:
+    lax.fori_loop(0, parts, bags, 0)
+
+    for load in loads[1:]:
         load.wait()
     gu_rows = gu[...].reshape(total, embed)
+    second = gps[...].reshape(total, gps.shape[2])
+    first = gpf[...].reshape(total, gpf.shape[2])
+    demo_grad = gx[...].reshape(total, 256)[:, 128:]
     gw3[...] = dot_as(act2[...], gu_rows, 0, 0)
-    gw2[...] = dot_as(act1[...], gps[...], 0, 0)
-    gw1[...] = dot_as(x[...], gpf[...], 0, 0)
+    gw2[...] = dot_as(act1[...], second, 0, 0)
+    gw1[...] = dot_as(x[...], first, 0, 0)
     stores = [(gw3, gw3_out), (gw2, gw2_out)]
     for i in range(nc):
         stores.append((gw1.at[pl.ds(i * 128, width)], gw1_out.at[pl.ds(i * width, width)]))
@@ -1087,65 +1217,12 @@
     stores = [pltpu.make_async_copy(s, d, out_sem.at[i]) for i, (s, d) in enumerate(stores)]
     for store in stores:
         store.start()
-    demo = dot_as(buckets[...], gx[:, 128:256], 1, 0)
+    demo = dot_as(buckets[...], demo_grad, 1, 0)
     demo_out[...] = demo.T[0 : sz.demo_width, :]
-    gb1_out[...] = jnp.sum(gpf[...].astype(F32), axis=0, keepdims=True)
-    gb2_out[...] = jnp.sum(gps[...].astype(F32), axis=0, keepdims=True)
+    gb1_out[...] = jnp.sum(first.astype(F32), axis=0, keepdims=True)
+    gb2_out[...] = jnp.sum(second.astype(F32), axis=0, keepdims=True)
     gb3_out[...] = jnp.sum(gu_rows.astype(F32), axis=0, keepdims=True)
 
-    def line_store(out, slot, hh):
-        at = pl.ds(pl.multiple_of(hh * 4 * LOW, 4 * LOW), 4 * LOW)
-        return pltpu.make_async_copy(lines.at[slot], out.at[:, at], line_sem.at[slot])
-
-    def put(slot, found, factor):
-        for i in range(4):
-            lines[slot, :, i * LOW : (i + 1) * LOW] = found[i * width : (i + 1) * width] * factor
-
-    def bags(hh, _):
-        for table, out in enumerate((watch_out, search_out)):
-            n = hh * 2 + table
-            slot = table * 2 + lax.rem(hh, 2)
-            ring_load(n).wait()
-            found = dot_as(spread_grads[table], ring[lax.rem(n, depth)], 1, 0)
-
-            @pl.when(n + depth < 2 * parts)
-            def _():
-                ring_load(n + depth).start()
-
-            @pl.when(hh >= 2)
-            def _():
-                line_store(out, slot, hh - 2).wait()
-
-            put(slot, found, 1.0 / sz.bag)
-            line_store(out, slot, hh).start()
-        return 0
-
-    lax.fori_loop(0, parts, bags, 0)
-
-    for k in range(sz.tiles):
-        low = slots[k, 1:2, :].astype(BF16)
-        hot = one_where(low == iota((LOW, CHUNK), 0).astype(BF16), BF16)
-        low_rows[k * CHUNK : (k + 1) * CHUNK, :] = hot.T
-    high = jnp.concatenate([slots[k, 0:1, :] for k in range(sz.tiles)], axis=1).astype(BF16)
-    values = jnp.concatenate([neg_rows[...], pos_rows[...]], axis=1)
-
-    def scatter(n, _):
-        left = []
-        for i in range(8):
-            at = (n * 8 + i).astype(F32).astype(BF16)
-            left.append(jnp.where(high == at, values, jnp.zeros((), BF16)))
-        found = dot_as(jnp.concatenate(left, axis=0), low_rows[...], 1, 0)
-        for j in range(2):
-
-            @pl.when(n >= 1)
-            def _():
-                line_store(table_out, 4 + j, (n - 1) * 2 + j).wait()
-
-            put(4 + j, found[j * 4 * width : (j + 1) * 4 * width], 1.0)
-            line_store(table_out, 4 + j, n * 2 + j).start()
-        return 0
-
-    lax.fori_loop(0, parts // 2, scatter, 0)
     for table, out in enumerate((watch_out, search_out)):
         for hh in (parts - 2, parts - 1):
             line_store(out, table * 2 + hh % 2, hh).wait()
@@ -1176,25 +1253,22 @@
     return pl.pallas_call(
         functools.partial(back_kernel, sz),
         out_shape=[o for o, _ in outs],
-        in_specs=[vmem] * 3 + [hbm] * 11,
+        in_specs=[vmem] * 3 + [hbm] * 9,
         out_specs=[s for _, s in outs],
         scratch_shapes=[
             pltpu.VMEM((total, sz.x_width), BF16), pltpu.VMEM((total, first), BF16),
-            pltpu.VMEM((total, first), BF16), pltpu.VMEM((total, second), BF16),
             pltpu.VMEM((total, second), BF16), pltpu.VMEM((nb, sz.rows, embed), BF16),
-            pltpu.VMEM((buckets, total), BF16), pltpu.VMEM(args["w_first"].shape, BF16),
-            pltpu.VMEM((256, first), BF16), pltpu.VMEM((first, second), BF16),
-            pltpu.VMEM((second, embed), BF16), pltpu.VMEM((total, second), BF16),
-            pltpu.VMEM((total, first), BF16), pltpu.VMEM((total, 256), BF16),
-            pltpu.VMEM((2, 4 * sz.width, 4 * total), BF16), pltpu.VMEM((4, 4 * total, LOW), BF16),
+            pltpu.VMEM((nb, sz.rows, second), BF16), pltpu.VMEM((nb, sz.rows, first), BF16),
+            pltpu.VMEM((nb, sz.rows, 256), BF16), pltpu.VMEM((buckets, total), BF16),
+            pltpu.VMEM((128, total), BF16), pltpu.VMEM((8, 4, total, LOW), BF16),
             pltpu.VMEM((6, sz.width, 4 * LOW), F32), pltpu.VMEM((slots, LOW), BF16),
             pltpu.VMEM((sz.x_width, first), F32), pltpu.VMEM((first, second), F32),
             pltpu.VMEM((second, embed), F32),
-            dma((10,)), dma((4,)), dma((6,)), dma((3 + 2 * sz.col,)),
+            dma((8,)), dma((8,)), dma((6,)), dma((3 + 2 * sz.col,)),
         ],
         compiler_params=pltpu.CompilerParams(vmem_limit_bytes=62 * 2**20),
         name="back",
-    )(*kept, args["w_first"], args["w_second"], args["w_third"])
+    )(*kept)
 
 
 def fast_device(sz, *inputs):
@@ -1205,11 +1279,11 @@
     )
     args = dict(zip(names, inputs))
     (
-        counts, x, act1, slope1, act2, slope2, gu, buckets, neg_rows, pos_rows, slots, user_vecs, loss, fits,
+        counts, x, act1, act2, gu, gps, gpf, gx, buckets, neg_rows, pos_rows, slots, user_vecs, loss, fits,
     ) = front(sz, args)
 
     def finish(*operands):
-        kept = (neg_rows, pos_rows, slots, counts, x, act1, slope1, act2, slope2, gu, buckets)
+        kept = (neg_rows, pos_rows, slots, counts, x, act1, act2, gu, gps, gpf, gx, buckets)
         watch, search, table, gw1, gw2, gw3, demo, gb1, gb2, gb3 = back(sz, args, kept)
         return (
             user_vecs, loss.reshape(()), watch, search, table, demo.T, gw1, gb1.reshape(-1),

time: 128 us -> 112 us (0.88)
  Pallas kernels: 122 us -> 106 us
    pallas_call x1, Pallas kernels: 37.8 us -> 22.9 us  [back(): pl.pallas_call(functools.partial(back_kernel, sz), out_shape=[o for o, _...]
where the time goes in v3:
time: 112 us; the launch traced here: 111 us
  Pallas kernels  106 us (95%)
  between operations  3.66 us (3%)
  local copies, waits for them, and re-layouts  1.34 us (1%)
    pallas_call x1, Pallas kernels, front(): pl.pallas_call(functools.partial(front_kernel, sz), out_shape=[o for o, _...  83.2 us
    pallas_call x1, Pallas kernels, back(): pl.pallas_call(functools.partial(back_kernel, sz), out_shape=[o for o, _...  22.9 us

profile of v3, /device:TPU:1, one launch (start us, length us, event | category | flops | bytes accessed | tf_op | source)
XLA Modules:
  0.0 111.3 jit_solution(8263940524642739381)
XLA Ops:
  1.3 0.0 copy-start.25
  1.3 0.0 copy-start.35
  1.3 0.0 copy-start.46
  1.3 83.2 %front.1 = (bf16[2,8,4,1024,256]{4,3,2,1,0:T(8,128)(2,1)}, bf16[1024,640]{1,0:T(8,128)(2,1)}, bf16[1024,1024]{1,0:T(8,128)(2,1)}, bf16[1024,512]{1,0:T(8,128)(2,...) custom-call(s32[50,128]{1,0:T(8,128)} %bitcast.214.watch_ids, ...), custom_call_target="tpu_custom_call" | custom-call | tf_op jit(solution)/shard_map/front/pallas_call | solution.py:1107
  85.1 0.0 copy-done.25
  85.1 0.0 copy-done.35
  85.1 0.0 copy-done.46
  85.1 23.1 %conditional.1 = (bf16[32,256]{1,0:T(8,128)(2,1)}, f32[]{:T(128)}, f32[64,8192]{1,0:T(8,128)}, f32[64,8192]{1,0:T(8,128)}, f32[64,8192]{1,0:T(8,128)}, /*index=5...) conditional(s32[]{:T(128)} %bitcast.223, ...), branch_computations={%region_0.16_spmd, %region_10.17_spmd} | conditional | flops 10206007296 | bytes 624368768 | solution.py:1296
  85.3 22.9 %back.1 = (f32[64,8192]{1,0:T(8,128)}, f32[64,8192]{1,0:T(8,128)}, f32[64,8192]{1,0:T(8,128)}, f32[600,1024]{1,0:T(8,128)}, f32[1024,512]{1,0:T(8,128)}, /*index...) custom-call(bf16[64,768]{1,0:T(8,128)(2,1)} %get-tuple-element.150.neg_rows, ...), custom_call_target="tpu_custom_call" | custom-call | tf_op jit(solution)/shard_map/cond/branch_1_fun/back/pallas_call | solution.py:1253
  108.2 0.0 copy-start.42
  108.2 1.3 %copy.312 = bf16[32,256]{1,0:T(8,128)(2,1)} copy(bf16[32,256]{1,0:T(8,128)(2,1)} %get-tuple-element.574) | data formatting | bytes 32768
  110.1 0.0 copy-done.42
Async XLA Ops:
  1.3 83.8 %copy-start.25 = (s32[5120]{0:T(1024)S(1)}, s32[5120]{0:T(1024)}, u32[]{:S(2)}) copy-start(s32[5120]{0:T(1024)} %param.34) | copy-start | bytes 61444
  1.3 83.8 %copy-start.35 = (s32[128,4]{0,1:T(4,128)S(1)}, s32[128,4]{0,1:T(4,128)}, u32[]{:S(2)}) copy-start(s32[128,4]{0,1:T(4,128)} %param.32) | copy-start | bytes 6148
  1.3 83.8 %copy-start.46 = (s32[128]{0:T(128)S(1)}, s32[128]{0:T(128)}, u32[]{:S(2)}) copy-start(s32[128]{0:T(128)} %param.33) | copy-start | bytes 1540
  108.2 2.0 %copy-start.42 = (f32[1024]{0:T(1024)}, f32[1024]{0:T(1024)S(1)}, u32[]{:S(2)}) copy-start(f32[1024]{0:T(1024)S(1)} %get-tuple-element.581) | copy-start | bytes 12292

commit v4 on v3

--- a/solution.py
+++ b/solution.py
@@ -333,6 +333,23 @@
     )
 
 
+def flip_rows(value):
+    rows, lanes = value.shape
+    return pltpu.roll(value.reshape(rows // 8, 8, lanes), 4, 1).reshape(rows, lanes)
+
+
+def x_place(col):
+    return ((col % 2) * 2 + col // 2) * 128
+
+
+def scattered(n, high, values, low_rows):
+    left = []
+    for i in range(8):
+        at = (n * 8 + i).astype(F32).astype(BF16)
+        left.append(jnp.where(high == at, values, jnp.zeros((), BF16)))
+    return dot_as(jnp.concatenate(left, axis=0), low_rows, 1, 0)
+
+
 class Sizes:
     def __init__(self, batch, col, rows, bag, width, vocab, negs, embed, demo_width):
         self.batch, self.col, self.rows, self.bag = batch, col, rows, bag
@@ -358,12 +375,12 @@
     watch_ids, search_ids, demo_ids, pos_ids, neg_ids, demo_table, b_first, b_second, b_third, valid_count,
     watch_table, search_table, out_table, w_first, w_second, w_third,
     counts_out, x_out, act1_out, act2_out, gu_out, gps_out, gpf_out, gx_out, buckets_out,
-    neg_rows_out, pos_rows_out, slots_out, user_out, loss_out, fits_out,
+    neg_rows_out, pos_table_out, slots_out, user_out, loss_out, fits_out,
     tabs, tall, mix, w1_raw, w1, w1_own, w2, w3, turned, upright, lines_own, ids, side, neg_dest, neg_digits, counts, found_sums, sums, pieces, x,
     pre1, pre2, acts1, slopes1, acts2, slopes2, users, buckets, slots, picked, neg_all, pos_all, e_cols,
-    e_rows, probs, stats, g_send, g_recv, gu, gps, gpf, gx, rg_send, rg_recv, gp_all, loss_all,
+    e_rows, low_rows, pos_table, probs, stats, factors, home, g_send, g_recv, gu, gps, gpf, gx, rg_send, rg_recv, gp_all, loss_all,
     local_sem, out_sem, down_sem, count_sem, ids_s, ids_r, sd_s, sd_r, ic_s, ic_r, rs_s, rs_r, ag_s, ag_r, xx_s, xx_r, co_s, co_r,
-    ne_s, ne_r, pe_s, pe_r, st_s, st_r, gs_s, gs_r, ga_s, ga_r, gx_s, gx_r, gc_s, gc_r,
+    ne_s, ne_r, pe_s, pe_r, ho_s, ho_r, st_s, st_r, gs_s, gs_r, ga_s, ga_r, gx_s, gx_r, gc_s, gc_r,
     rg_s, rg_r, gp_s, gp_r, lo_s, lo_r,
 ):
     b, c = lax.axis_index("batch"), lax.axis_index("col")
@@ -534,14 +551,15 @@
     loads[3].wait()
     w1[nc * 128 :, :] = jnp.zeros((128, w1.shape[1]), BF16)
     for i in range(nc):
-        w1[i * 128 : i * 128 + width, :] = w1_raw[i * width : (i + 1) * width, :]
-        w1[i * 128 + width : (i + 1) * 128, :] = w1_raw[embed + i * width : embed + (i + 1) * width, :]
+        at = x_place(i)
+        w1[at : at + width, :] = w1_raw[i * width : (i + 1) * width, :]
+        w1[at + width : at + 128, :] = w1_raw[embed + i * width : embed + (i + 1) * width, :]
     w1[nc * 128 : nc * 128 + sz.demo_width, :] = w1_raw[2 * embed :, :]
     loads[4].wait()
     loads[5].wait()
 
     w1_own[...] = jnp.zeros(w1_own.shape, BF16)
-    w1_own[0 : 2 * width, :] = w1[pl.ds(pl.multiple_of(c * 128, 128), 128), :]
+    w1_own[0 : 2 * width, :] = w1[pl.ds(pl.multiple_of((lax.rem(c, 2) * 2 + c // 2) * 128, 128), 128), :]
     w1_own[2 * width : 2 * width + sz.demo_width, :] = w1_raw[2 * embed :, :]
     for i in range(1, nc):
         place = ids.at[:, share_of(col_from(i))]
@@ -589,6 +607,24 @@
         for i in range(1, nc):
             pos_send(i).start()
 
+    def slot_rows():
+        for i in range(1, nc):
+            src = col_from(i)
+            send(neg_all.at[src], neg_all.at[src], ne_s.at[i - 1], ne_r.at[i - 1], (b, c)).wait_recv()
+            send(pos_all.at[src], pos_all.at[src], pe_s.at[i - 1], pe_r.at[i - 1], (b, c)).wait_recv()
+        for i in range(nc):
+            for k in range(sz.cap_tiles):
+                e_cols[i * width : (i + 1) * width, k * CHUNK : (k + 1) * CHUNK] = neg_all[i, k]
+            e_cols[i * width : (i + 1) * width, cap:] = pos_all[i]
+        e_rows[...] = e_cols[...].T
+        for i in range(1, nb):
+            home_send(i).start()
+
+    def home_send(i):
+        to = batch_peer(i)
+        rows = e_rows.at[pl.ds(pl.multiple_of(cap + to * sz.quarter, sz.quarter), sz.quarter)]
+        return send(rows, home.at[i - 1], ho_s.at[i - 1], ho_r.at[i - 1], (to, c))
+
     def pos_send(i):
         to = col_peer(i)
         return send(picked.at[sz.cap_tiles + to], pos_all.at[c], pe_s.at[i - 1], pe_r.at[i - 1], (b, to))
@@ -597,6 +633,7 @@
     piece = span // nb
     lane_mod = iota((16, CHUNK), 1) % BAG_PAD
     lane_r4 = iota((16, CHUNK), 1) // BAG_PAD
+    odd_group = iota((16, CHUNK), 0) & 1
     blocks = span // sz.rows
     parts_in_block = sz.groups // 16
 
@@ -622,7 +659,7 @@
             value = lax.shift_right_logical(word, 16 * table) & 0xFFFF
             local = value - offset
             mine = (local >= 0) & (local < sz.vocab) & (lane_mod < sz.bag)
-            code = jnp.where(mine, (local >> 8) * 4 + lane_r4, -1).astype(F32).astype(BF16)
+            code = jnp.where(mine, ((local >> 8) ^ odd_group) * 4 + lane_r4, -1).astype(F32).astype(BF16)
             low = (local & 255).astype(F32).astype(BF16)
             low_half = iota((sz.high // 2, 8, LOW), 1) < 4
             for quad in range(4):
@@ -633,8 +670,8 @@
                         left = one_where(code[g : g + 1, :] == code_line, FP8)
                         right = one_where(low[g : g + 1, :] == low_line, FP8)
                         found.append(dot_as(left, right, 1, 1).reshape(sz.high // 2, 8, LOW))
-                    even = jnp.where(low_half, found[0], pltpu.roll(found[1], 4, 1))
-                    odd = jnp.where(low_half, pltpu.roll(found[0], 4, 1), found[1])
+                    even = jnp.where(low_half, found[0], found[1])
+                    odd = jnp.where(low_half, found[1], found[0])
                     pairs.append((even, odd))
                 line = pl.ds(pl.multiple_of(q * 64 + quad * 16, 16), 16)
                 for part in range(sz.high):
@@ -651,8 +688,8 @@
         )
         total = dot_as(left, mix[table], 1, 0)
         left_side = iota((span, 128), 1) < width
-        first = jnp.where(left_side, total[0:span, 0:128], total[span : 2 * span, 0:128])
-        second = jnp.where(left_side, total[2 * span : 3 * span, 128:], total[3 * span :, 128:])
+        first = jnp.where(left_side, total[0:span, 0:128], flip_rows(total[span : 2 * span, 0:128]))
+        second = jnp.where(left_side, total[2 * span : 3 * span, 128:], flip_rows(total[3 * span :, 128:]))
         both = first + second
         found_sums[table] = both + pltpu.roll(both, width, 1)
 
@@ -666,15 +703,21 @@
                 rs_s.at[t, i - 1], rs_r.at[t], (to, c),
             ).start()
 
+    def lanes_of(col):
+        return pl.ds(pl.multiple_of((lax.rem(col, 2) * 2 + col // 2) * 128, 128), 128)
+
     def x_at(t, col):
+        return x.at[pl.ds(pl.multiple_of(t * span, span), span), lanes_of(col)]
+
+    def x_pair(t, col):
         return x.at[
-            pl.ds(pl.multiple_of(t * span, span), span), pl.ds(pl.multiple_of(col * 128, 128), 128)
+            pl.ds(pl.multiple_of(t * span, span), span),
+            pl.ds(pl.multiple_of(lax.rem(col, 2) * 256, 256), 256),
         ]
 
     def x_piece(t, owner):
         return x.at[
-            pl.ds(pl.multiple_of(t * span + owner * piece, piece), piece),
-            pl.ds(pl.multiple_of(c * 128, 128), 128),
+            pl.ds(pl.multiple_of(t * span + owner * piece, piece), piece), lanes_of(c)
         ]
 
     def reduce_step(t):
@@ -683,8 +726,7 @@
         for i in range(nb - 1):
             total = total + pieces[t, i].astype(F32)
         x[
-            pl.ds(pl.multiple_of(t * span + b * piece, piece), piece),
-            pl.ds(pl.multiple_of(c * 128, 128), 128),
+            pl.ds(pl.multiple_of(t * span + b * piece, piece), piece), lanes_of(c)
         ] = (total / sz.bag).astype(BF16)
         for i in range(1, nb):
             send(x_piece(t, b), x_piece(t, b), ag_s.at[t, i - 1], ag_r.at[t], (batch_peer(i), c)).start()
@@ -695,12 +737,10 @@
 
     def core_step(t):
         send(x_at(t, cx), x_at(t, cx), xx_s.at[t], xx_r.at[t], (b, cx)).wait_recv()
-        send(x_at(t, c), x_at(t, c), co_s.at[t, 0], co_r.at[t, 0], (b, ck)).start()
-        send(x_at(t, cx), x_at(t, cx), co_s.at[t, 1], co_r.at[t, 1], (b, ck)).start()
+        send(x_pair(t, c), x_pair(t, c), co_s.at[t], co_r.at[t], (b, ck)).start()
 
     def full_step(t):
-        send(x_at(t, ck), x_at(t, ck), co_s.at[t, 0], co_r.at[t, 0], (b, ck)).wait_recv()
-        send(x_at(t, ckx), x_at(t, ckx), co_s.at[t, 1], co_r.at[t, 1], (b, ck)).wait_recv()
+        send(x_pair(t, ck), x_pair(t, ck), co_s.at[t], co_r.at[t], (b, ck)).wait_recv()
 
     def tower(k):
         at = pl.ds(pl.multiple_of(k * span, span), span)
@@ -742,6 +782,10 @@
         def _():
             pos_part()
 
+        @pl.when(n == bag_ticks + 3)
+        def _():
+            slot_rows()
+
         @pl.when(odd & (n >= 5))
         def _():
             full_step((n - 5) // 2)
@@ -785,16 +829,6 @@
     for copy in out_copies:
         copy.start()
     user_out[...] = users[pl.ds(pl.multiple_of(b * sz.rows + c * sz.quarter, sz.quarter), sz.quarter), :]
-
-    for i in range(1, nc):
-        src = col_from(i)
-        send(neg_all.at[src], neg_all.at[src], ne_s.at[i - 1], ne_r.at[i - 1], (b, c)).wait_recv()
-        send(pos_all.at[src], pos_all.at[src], pe_s.at[i - 1], pe_r.at[i - 1], (b, c)).wait_recv()
-    for i in range(nc):
-        for k in range(sz.cap_tiles):
-            e_cols[i * width : (i + 1) * width, k * CHUNK : (k + 1) * CHUNK] = neg_all[i, k]
-        e_cols[i * width : (i + 1) * width, cap:] = pos_all[i]
-    e_rows[...] = e_cols[...].T
 
     def users_of(quarter):
         return jnp.concatenate(
@@ -816,7 +850,8 @@
     peak = jnp.maximum(
         jnp.max(neg_logits, axis=0, keepdims=True), jnp.max(pos_masked, axis=0, keepdims=True)
     )
-    mass = jnp.sum(jnp.where(slot_ok, jnp.exp(neg_logits - peak), 0.0), axis=0, keepdims=True) + jnp.sum(
+    bare = jnp.where(slot_ok, jnp.exp(neg_logits - peak), 0.0)
+    mass = jnp.sum(bare, axis=0, keepdims=True) + jnp.sum(
         jnp.where(pos_ok, jnp.exp(pos_masked - peak), 0.0), axis=0, keepdims=True
     )
     pos_value = jnp.sum(jnp.where(pos_ok, pos_logits, 0.0), axis=0, keepdims=True)
@@ -826,14 +861,25 @@
         copy.start()
         last_sends.append(copy)
 
+    probs[...] = bare.astype(BF16)
+    grad_user = dot_as(probs[...], e_rows[0:cap, :], 0, 0)
+    for j in range(nb):
+        g_send[j] = grad_user[j * sz.quarter : (j + 1) * sz.quarter].astype(BF16)
+    for i in range(1, nb):
+        to = batch_peer(i)
+        copy = send(g_send.at[to], g_recv.at[i - 1], gs_s.at[i - 1], gs_r.at[i - 1], (to, c))
+        copy.start()
+        last_sends.append(copy)
+
     def some_slopes(k, _):
         slopes(k)
         return 0
 
-    lax.fori_loop(0, sz.steps // 2, some_slopes, 0)
+    lax.fori_loop(0, sz.steps, some_slopes, 0)
     for i in range(1, nb):
         src = batch_from(i)
         send(stats.at[src], stats.at[src], st_s.at[i - 1], st_r.at[i - 1], (b, c)).wait_recv()
+    order = [batch_from(i) for i in range(nb)]
     peaks = [stats[j, 0:1, :] for j in range(nb)]
     top = peaks[0]
     for j in range(1, nb):
@@ -846,39 +892,41 @@
     lse = top + jnp.log(full_mass)
     loss_part = jnp.sum(weight * (lse - pos_logit), axis=1, keepdims=True)
     scale = weight / full_mass
-    probs[0:cap] = jnp.where(slot_ok, jnp.exp(neg_logits - top) * scale, 0.0).astype(BF16)
     pos_grad = weight * (jnp.exp(pos_logit - top) / full_mass - 1.0)
-    probs[cap:] = jnp.where(pos_ok, pos_grad, 0.0).astype(BF16)
-    grad_user = dot_as(probs[...], e_rows[...], 0, 0)
-    for j in range(nb):
-        g_send[j] = grad_user[j * sz.quarter : (j + 1) * sz.quarter].astype(BF16)
-    for i in range(1, nb):
-        to = batch_peer(i)
-        copy = send(g_send.at[to], g_recv.at[i - 1], gs_s.at[i - 1], gs_r.at[i - 1], (to, c))
-        copy.start()
-        last_sends.append(copy)
-    rows_grad = dot_as(probs[0:cap, :], quarter_users, 1, 0)
-    rows_grad = rows_grad.T.astype(BF16)
-    for i in range(nc):
-        rg_send[i] = rows_grad[i * width : (i + 1) * width]
+    lines_of = [jnp.exp(stats[j, 0:1, :] - top) * scale for j in order]
+    lines_of += [pos_grad, jnp.zeros((16 - nb - 1, sz.users), F32)]
+    factors[...] = jnp.concatenate(lines_of, axis=0).T
+    probs[...] = jnp.where(slot_ok, jnp.exp(neg_logits - top) * scale, 0.0).astype(BF16)
     gp_all[c] = jnp.broadcast_to(jnp.where(pos_here >= 0.0, pos_grad, 0.0), (8, sz.users))
     loss_all[c] = jnp.broadcast_to(loss_part, (8, 128))
     for i in range(1, nc):
         to = col_peer(i)
         for copy in (
-            send(rg_send.at[to], rg_recv.at[c], rg_s.at[i - 1], rg_r.at[i - 1], (b, to)),
             send(gp_all.at[c], gp_all.at[c], gp_s.at[i - 1], gp_r.at[i - 1], (b, to)),
             send(loss_all.at[c], loss_all.at[c], lo_s.at[i - 1], lo_r.at[i - 1], (b, to)),
         ):
             copy.start()
             last_sends.append(copy)
+    rows_grad = dot_as(probs[...], quarter_users, 1, 0)
+    rows_grad = rows_grad.T.astype(BF16)
+    for i in range(nc):
+        rg_send[i] = rows_grad[i * width : (i + 1) * width]
+    for i in range(1, nc):
+        to = col_peer(i)
+        copy = send(rg_send.at[to], rg_recv.at[c], rg_s.at[i - 1], rg_r.at[i - 1], (b, to))
+        copy.start()
+        last_sends.append(copy)
     rg_recv[c] = rg_send[c]
-    lax.fori_loop(sz.steps // 2, sz.steps, some_slopes, 0)
     for i in range(1, nb):
         send(g_send.at[0], g_recv.at[i - 1], gs_s.at[i - 1], gs_r.at[i - 1], (b, c)).wait_recv()
-    total = g_send[b].astype(F32)
-    for i in range(nb - 1):
-        total = total + g_recv[i].astype(F32)
+    factor = factors[pl.ds(pl.multiple_of(b * sz.quarter, sz.quarter), sz.quarter), :]
+    total = factor[:, 0:1] * g_send[b].astype(F32)
+    own_pos = e_rows[pl.ds(pl.multiple_of(cap + b * sz.quarter, sz.quarter), sz.quarter), :].astype(F32)
+    for i in range(1, nb):
+        home_send(i).wait_recv()
+        total = total + factor[:, i : i + 1] * g_recv[i - 1].astype(F32)
+        own_pos = own_pos + home[i - 1].astype(F32)
+    total = total + factor[:, nb : nb + 1].astype(BF16).astype(F32) * own_pos
 
     def gu_at(block, col):
         return gu.at[block, pl.ds(pl.multiple_of(col * sz.quarter, sz.quarter), sz.quarter), :]
@@ -891,6 +939,38 @@
         copy = send(gu_at(b, c), gu_at(b, c), ga_s.at[i - 1], ga_r.at[i - 1], (batch_peer(i), c))
         copy.start()
         last_sends.append(copy)
+
+    for k in range(nc):
+        low = slots[sz.cap_tiles + k, 1:2, :].astype(BF16)
+        hot = one_where(low == iota((LOW, CHUNK), 0).astype(BF16), BF16)
+        low_rows[k * CHUNK : (k + 1) * CHUNK, :] = hot.T
+    pick_own = one_where(iota((width, embed), 1) == c * width + iota((width, embed), 0), BF16)
+    for i in range(1, nc):
+        src = col_from(i)
+        send(gp_all.at[src], gp_all.at[src], gp_s.at[i - 1], gp_r.at[i - 1], (b, c)).wait_recv()
+    pos_rows = []
+    for quarter in range(nc):
+        own_part = dot_as(pick_own, users_of(quarter), 1, 1)
+        grad = gp_all[quarter, 0:1, :].astype(BF16).astype(F32)
+        mine = slots[sz.cap_tiles + quarter, 0:1, :] >= 0.0
+        pos_rows.append(jnp.where(mine, grad * own_part, 0.0).astype(BF16))
+    pos_rows = jnp.concatenate(pos_rows, axis=1)
+    pos_parts = jnp.concatenate(
+        [slots[sz.cap_tiles + k, 0:1, :] for k in range(nc)], axis=1
+    ).astype(BF16)
+
+    def pos_scatter(n, _):
+        found = scattered(n, pos_parts, pos_rows, low_rows[...])
+        for j in range(2):
+            for i in range(4):
+                pos_table[n * 2 + j, :, i * LOW : (i + 1) * LOW] = found[
+                    (j * 4 + i) * width : (j * 4 + i + 1) * width
+                ]
+        return 0
+
+    lax.fori_loop(0, sz.high_parts // 2, pos_scatter, 0)
+    pos_copy = pltpu.make_async_copy(pos_table, pos_table_out, out_sem.at[5])
+    pos_copy.start()
     for i in range(nb):
         src = batch_from(i)
         if i > 0:
@@ -940,19 +1020,19 @@
             copy.start()
 
     def quarter_down(i, _):
-        flip = jnp.where(i == 0, c, jnp.where(i == 1, cx, jnp.where(i == 2, ck, ckx)))
+        flip = jnp.where(i == 0, c, jnp.where(i == 1, ck, jnp.where(i == 2, cx, ckx)))
 
         @pl.when(i == 1)
+        def _():
+            send(gu_all(ck), gu_all(ck), gc_s.at[0], gc_r.at[0], (b, ck)).wait_recv()
+
+        @pl.when(i == 2)
         def _():
             for k in range(nb):
                 src = batch_from(k)
                 send(gu_at(src, cx), gu_at(src, cx), gx_s.at[k], gx_r.at[k], (b, cx)).wait_recv()
             send(gu_all(cx), gu_all(cx), gc_s.at[1], gc_r.at[1], (b, ck)).start()
 
-        @pl.when(i == 2)
-        def _():
-            send(gu_all(ck), gu_all(ck), gc_s.at[0], gc_r.at[0], (b, ck)).wait_recv()
-
         @pl.when(i == 3)
         def _():
             send(gu_all(ckx), gu_all(ckx), gc_s.at[1], gc_r.at[1], (b, ck)).wait_recv()
@@ -963,18 +1043,6 @@
     lax.fori_loop(0, nc, quarter_down, 0)
     gu_copy = pltpu.make_async_copy(gu, gu_out, out_sem.at[4])
     gu_copy.start()
-
-    pick_own = one_where(iota((width, embed), 1) == c * width + iota((width, embed), 0), BF16)
-    for i in range(1, nc):
-        src = col_from(i)
-        send(gp_all.at[src], gp_all.at[src], gp_s.at[i - 1], gp_r.at[i - 1], (b, c)).wait_recv()
-    for quarter in range(nc):
-        own_part = dot_as(pick_own, users_of(quarter), 1, 1)
-        grad = gp_all[quarter, 0:1, :].astype(BF16).astype(F32)
-        mine = slots[sz.cap_tiles + quarter, 0:1, :] >= 0.0
-        pos_rows_out[:, quarter * sz.users : (quarter + 1) * sz.users] = jnp.where(
-            mine, grad * own_part, 0.0
-        ).astype(BF16)
 
     for i in range(1, nc):
         src = col_from(i)
@@ -991,6 +1059,8 @@
     last_sends.append(send(gu_all(cx), gu_all(cx), gc_s.at[1], gc_r.at[1], (b, ck)))
     for i in range(1, nc):
         last_sends.append(pos_send(i))
+    for i in range(1, nb):
+        last_sends.append(home_send(i))
     for copy in last_sends:
         copy.wait_send()
 
@@ -999,8 +1069,7 @@
             send(sums.at[t, pl.ds(0, piece)], pieces.at[t, 0], rs_s.at[t, i - 1], rs_r.at[t], (b, c)).wait_send()
             send(x_piece(t, b), x_piece(t, b), ag_s.at[t, i - 1], ag_r.at[t], (b, c)).wait_send()
         send(x_at(t, c), x_at(t, c), xx_s.at[t], xx_r.at[t], (b, cx)).wait_send()
-        send(x_at(t, c), x_at(t, c), co_s.at[t, 0], co_r.at[t, 0], (b, ck)).wait_send()
-        send(x_at(t, cx), x_at(t, cx), co_s.at[t, 1], co_r.at[t, 1], (b, ck)).wait_send()
+        send(x_pair(t, c), x_pair(t, c), co_s.at[t], co_r.at[t], (b, ck)).wait_send()
         return 0
 
     lax.fori_loop(0, sz.steps, drain, 0)
@@ -1008,9 +1077,10 @@
         for t in (sz.steps - 2, sz.steps - 1):
             count_copy(t, table, t % 2).wait()
     gu_copy.wait()
+    pos_copy.wait()
     for copy in out_copies:
         copy.wait()
-    for i, col in enumerate((c, cx, ck, ckx)):
+    for i, col in enumerate((c, ck, cx, ckx)):
         for copy in down_copies(col, i):
             copy.wait()
 
@@ -1035,7 +1105,7 @@
         (shape((total, first)), hbm), (shape((total, second)), hbm), (shape((nb, sz.rows, embed)), hbm),
         (shape((nb, sz.rows, second)), hbm), (shape((nb, sz.rows, first)), hbm),
         (shape((nb, sz.rows, 256)), hbm), (shape((buckets, total)), hbm),
-        (shape((width, cap)), vmem), (shape((width, total)), vmem),
+        (shape((width, cap)), vmem), (shape((sz.high_parts, width, 4 * LOW), F32), hbm),
         (shape((sz.tiles, 8, CHUNK), F32), vmem),
         (shape((sz.quarter, embed)), vmem), (shape((1, 1), F32), vmem), (shape((1, 1), I32), vmem),
     ]
@@ -1074,8 +1144,12 @@
         pltpu.VMEM((nc, width, users), BF16),
         pltpu.VMEM((embed, slots), BF16),
         pltpu.VMEM((slots, embed), BF16),
-        pltpu.VMEM((slots, users), BF16),
+        pltpu.VMEM((nc * CHUNK, LOW), BF16),
+        pltpu.VMEM((sz.high_parts, width, 4 * LOW), F32),
+        pltpu.VMEM((cap, users), BF16),
         pltpu.VMEM((nb, 8, users), F32),
+        pltpu.VMEM((users, 16), F32),
+        pltpu.VMEM((nb - 1, sz.quarter, embed), BF16),
         pltpu.VMEM((nb, sz.quarter, embed), BF16),
         pltpu.VMEM((nb - 1, sz.quarter, embed), BF16),
         pltpu.VMEM((nb, sz.rows, embed), BF16),
@@ -1086,11 +1160,11 @@
         pltpu.VMEM((nc, width, cap), BF16),
         pltpu.VMEM((nc, 8, users), F32),
         pltpu.VMEM((nc, 8, 128), F32),
-        dma((6,)), dma((5,)), dma((nc, 3)), dma((2, 2)),
+        dma((6,)), dma((6,)), dma((nc, 3)), dma((2, 2)),
         dma((nb - 1,)), dma((nb - 1,)), dma((nb - 1,)), dma((nb - 1,)), dma((nc - 1,)), dma((nc - 1,)),
         dma((sz.steps, nb - 1)), dma((sz.steps,)), dma((sz.steps, nb - 1)), dma((sz.steps,)),
-        dma((sz.steps,)), dma((sz.steps,)), dma((sz.steps, 2)), dma((sz.steps, 2)),
-        dma((nc - 1,)), dma((nc - 1,)), dma((nc - 1,)), dma((nc - 1,)),
+        dma((sz.steps,)), dma((sz.steps,)), dma((sz.steps,)), dma((sz.steps,)),
+        dma((nc - 1,)), dma((nc - 1,)), dma((nc - 1,)), dma((nc - 1,)), dma((nb - 1,)), dma((nb - 1,)),
         dma((nb - 1,)), dma((nb - 1,)), dma((nb - 1,)), dma((nb - 1,)),
         dma((nb - 1,)), dma((nb - 1,)), dma((nb,)), dma((nb,)), dma((2,)), dma((2,)),
         dma((nc - 1,)), dma((nc - 1,)), dma((nc - 1,)), dma((nc - 1,)), dma((nc - 1,)), dma((nc - 1,)),
@@ -1118,33 +1192,41 @@
 
 
 def back_kernel(
-    sz, neg_rows, pos_rows, slots, counts, x_in, act1_in, act2_in, gu_in, gps_in, gpf_in, gx_in, buckets_in,
-    watch_out, search_out, table_out, gw1_out, gw2_out, gw3_out, demo_out, gb1_out, gb2_out, gb3_out,
-    x, act1, act2, gu, gps, gpf, gx, buckets, grads, ring,
+    sz, neg_rows, slots, user_in, loss_in, pos_in, counts, x_in, act1_in, act2_in, gu_in, gps_in, gpf_in, gx_in, buckets_in,
+    watch_out, search_out, table_out, gw1_out, gw2_out, gw3_out, demo_out, gb1_out, gb2_out, gb3_out, user_out, loss_out,
+    pos_table, x, act1, act2, gu, gps, gpf, gx, buckets, grads, ring,
     lines, low_rows, gw1, gw2, gw3, in_sem, ring_sem, line_sem, out_sem,
 ):
     width, cap, total, nb = sz.width, sz.cap, sz.total, sz.batch
     parts, nc, embed = sz.high_parts, sz.col, sz.embed
     depth = ring.shape[0]
     names = [
-        (gx_in, gx), (act2_in, act2), (gu_in, gu), (act1_in, act1), (gps_in, gps), (x_in, x), (gpf_in, gpf),
+        (gx_in, gx), (pos_in, pos_table), (act2_in, act2), (gu_in, gu), (act1_in, act1), (gps_in, gps), (x_in, x), (gpf_in, gpf),
         (buckets_in, buckets),
     ]
     loads = [pltpu.make_async_copy(s, d, in_sem.at[i]) for i, (s, d) in enumerate(names)]
     loads[0].start()
+    loads[1].start()
+    user_out[...] = user_in[...]
+    loss_out[...] = loss_in[...]
 
     def ring_load(n):
         return pltpu.make_async_copy(
             counts.at[lax.rem(n, 2), n // 2], ring.at[lax.rem(n, depth)], ring_sem.at[lax.rem(n, depth)]
         )
 
-    for n in range(depth):
+    early = depth - 2
+    for n in range(early):
         ring_load(n).start()
-    for load in loads[1:]:
+    for load in loads[2:]:
         load.start()
+    for n in range(early, depth):
+        ring_load(n).start()
     loads[0].wait()
 
-    grads[...] = gx[...].reshape(total, gx.shape[2])[:, 0:128].T
+    own_grads = gx[...].reshape(total, gx.shape[2])[:, 0:128]
+    grads[0] = own_grads.T
+    grads[1] = flip_rows(own_grads.astype(F32)).astype(BF16).T
 
     def line_store(out, slot, hh):
         at = pl.ds(pl.multiple_of(hh * 4 * LOW, 4 * LOW), 4 * LOW)
@@ -1154,26 +1236,24 @@
         for i in range(4):
             lines[slot, :, i * LOW : (i + 1) * LOW] = found[i] * factor
 
-    for k in range(sz.tiles):
+    for k in range(sz.cap_tiles):
         low = slots[k, 1:2, :].astype(BF16)
         hot = one_where(low == iota((LOW, CHUNK), 0).astype(BF16), BF16)
         low_rows[k * CHUNK : (k + 1) * CHUNK, :] = hot.T
-    high = jnp.concatenate([slots[k, 0:1, :] for k in range(sz.tiles)], axis=1).astype(BF16)
-    values = jnp.concatenate([neg_rows[...], pos_rows[...]], axis=1)
+    high = jnp.concatenate([slots[k, 0:1, :] for k in range(sz.cap_tiles)], axis=1).astype(BF16)
+    loads[1].wait()
 
     def scatter(n, _):
-        left = []
-        for i in range(8):
-            at = (n * 8 + i).astype(F32).astype(BF16)
-            left.append(jnp.where(high == at, values, jnp.zeros((), BF16)))
-        found = dot_as(jnp.concatenate(left, axis=0), low_rows[...], 1, 0)
+        found = scattered(n, high, neg_rows[...], low_rows[...])
         for j in range(2):
 
             @pl.when(n >= 1)
             def _():
                 line_store(table_out, 4 + j, (n - 1) * 2 + j).wait()
 
-            put(4 + j, [found[(j * 4 + i) * width : (j * 4 + i + 1) * width] for i in range(4)], 1.0)
+            rows = [found[(j * 4 + i) * width : (j * 4 + i + 1) * width] for i in range(4)]
+            rows = [rows[i] + pos_table[n * 2 + j, :, i * LOW : (i + 1) * LOW] for i in range(4)]
+            put(4 + j, rows, 1.0)
             line_store(table_out, 4 + j, n * 2 + j).start()
         return 0
 
@@ -1183,8 +1263,10 @@
             n = hh * 2 + table
             slot = table * 2 + lax.rem(hh, 2)
             ring_load(n).wait()
-            own = grads[table * width : (table + 1) * width, :]
-            found = [dot_as(own, ring[lax.rem(n, depth), i], 1, 0) for i in range(4)]
+            found = [
+                dot_as(grads[i % 2, table * width : (table + 1) * width, :], ring[lax.rem(n, depth), i], 1, 0)
+                for i in range(4)
+            ]
 
             @pl.when(n + depth < 2 * parts)
             def _():
@@ -1198,9 +1280,9 @@
             line_store(out, slot, hh).start()
         return 0
 
-    lax.fori_loop(0, parts, bags, 0)
-
-    for load in loads[1:]:
+    lax.fori_loop(0, parts // 2, bags, 0)
+
+    for load in loads[2:]:
         load.wait()
     gu_rows = gu[...].reshape(total, embed)
     second = gps[...].reshape(total, gps.shape[2])
@@ -1211,8 +1293,9 @@
     gw1[...] = dot_as(x[...], first, 0, 0)
     stores = [(gw3, gw3_out), (gw2, gw2_out)]
     for i in range(nc):
-        stores.append((gw1.at[pl.ds(i * 128, width)], gw1_out.at[pl.ds(i * width, width)]))
-        stores.append((gw1.at[pl.ds(i * 128 + width, width)], gw1_out.at[pl.ds(embed + i * width, width)]))
+        at = x_place(i)
+        stores.append((gw1.at[pl.ds(at, width)], gw1_out.at[pl.ds(i * width, width)]))
+        stores.append((gw1.at[pl.ds(at + width, width)], gw1_out.at[pl.ds(embed + i * width, width)]))
     stores.append((gw1.at[pl.ds(nc * 128, sz.demo_width)], gw1_out.at[pl.ds(2 * embed, sz.demo_width)]))
     stores = [pltpu.make_async_copy(s, d, out_sem.at[i]) for i, (s, d) in enumerate(stores)]
     for store in stores:
@@ -1223,6 +1306,8 @@
     gb2_out[...] = jnp.sum(second.astype(F32), axis=0, keepdims=True)
     gb3_out[...] = jnp.sum(gu_rows.astype(F32), axis=0, keepdims=True)
 
+    lax.fori_loop(parts // 2, parts, bags, 0)
+
     for table, out in enumerate((watch_out, search_out)):
         for hh in (parts - 2, parts - 1):
             line_store(out, table * 2 + hh % 2, hh).wait()
@@ -1247,24 +1332,25 @@
     outs = [(table, hbm)] * 3 + [
         (shape((args["w_first"].shape)), hbm), (shape((first, second)), hbm), (shape((second, embed)), hbm),
         (shape((sz.demo_width, buckets)), vmem), (shape((1, first)), vmem), (shape((1, second)), vmem),
-        (shape((1, embed)), vmem),
+        (shape((1, embed)), vmem), (shape((sz.quarter, embed), BF16), vmem), (shape((1, 1)), vmem),
     ]
-    slots = sz.tiles * CHUNK
+    slots = sz.cap
     return pl.pallas_call(
         functools.partial(back_kernel, sz),
         out_shape=[o for o, _ in outs],
-        in_specs=[vmem] * 3 + [hbm] * 9,
+        in_specs=[vmem] * 4 + [hbm] * 10,
         out_specs=[s for _, s in outs],
         scratch_shapes=[
+            pltpu.VMEM((sz.high_parts, sz.width, 4 * LOW), F32),
             pltpu.VMEM((total, sz.x_width), BF16), pltpu.VMEM((total, first), BF16),
             pltpu.VMEM((total, second), BF16), pltpu.VMEM((nb, sz.rows, embed), BF16),
             pltpu.VMEM((nb, sz.rows, second), BF16), pltpu.VMEM((nb, sz.rows, first), BF16),
             pltpu.VMEM((nb, sz.rows, 256), BF16), pltpu.VMEM((buckets, total), BF16),
-            pltpu.VMEM((128, total), BF16), pltpu.VMEM((8, 4, total, LOW), BF16),
+            pltpu.VMEM((2, 128, total), BF16), pltpu.VMEM((8, 4, total, LOW), BF16),
             pltpu.VMEM((6, sz.width, 4 * LOW), F32), pltpu.VMEM((slots, LOW), BF16),
             pltpu.VMEM((sz.x_width, first), F32), pltpu.VMEM((first, second), F32),
             pltpu.VMEM((second, embed), F32),
-            dma((8,)), dma((8,)), dma((6,)), dma((3 + 2 * sz.col,)),
+            dma((9,)), dma((8,)), dma((6,)), dma((3 + 2 * sz.col,)),
         ],
         compiler_params=pltpu.CompilerParams(vmem_limit_bytes=62 * 2**20),
         name="back",
@@ -1279,14 +1365,14 @@
     )
     args = dict(zip(names, inputs))
     (
-        counts, x, act1, act2, gu, gps, gpf, gx, buckets, neg_rows, pos_rows, slots, user_vecs, loss, fits,
+        counts, x, act1, act2, gu, gps, gpf, gx, buckets, neg_rows, pos_table, slots, user_vecs, loss, fits,
     ) = front(sz, args)
 
     def finish(*operands):
-        kept = (neg_rows, pos_rows, slots, counts, x, act1, act2, gu, gps, gpf, gx, buckets)
-        watch, search, table, gw1, gw2, gw3, demo, gb1, gb2, gb3 = back(sz, args, kept)
+        kept = (neg_rows, slots, user_vecs, loss, pos_table, counts, x, act1, act2, gu, gps, gpf, gx, buckets)
+        watch, search, table, gw1, gw2, gw3, demo, gb1, gb2, gb3, user, mean = back(sz, args, kept)
         return (
-            user_vecs, loss.reshape(()), watch, search, table, demo.T, gw1, gb1.reshape(-1),
+            user, mean.reshape(()), watch, search, table, demo.T, gw1, gb1.reshape(-1),
             gw2, gb2.reshape(-1), gw3, gb3.reshape(-1),
         )
 

time: 112 us -> 103 us (0.920)
  Pallas kernels: 106 us -> 100 us
  between operations: 3.66 us -> 1.94 us
    pallas_call x1, Pallas kernels: 83.2 us -> 79 us  [front(): pl.pallas_call(functools.partial(front_kernel, sz), out_shape=[o for o, _...]
    pallas_call x1, Pallas kernels: 22.9 us -> 21.4 us  [back(): pl.pallas_call(functools.partial(back_kernel, sz), out_shape=[o for o, _...]
where the time goes in v4:
time: 103 us
  Pallas kernels  100 us (97%)
  between operations  1.94 us (2%)
    pallas_call x1, Pallas kernels, front(): pl.pallas_call(functools.partial(front_kernel, sz), out_shape=[o for o, _...  79 us
    pallas_call x1, Pallas kernels, back(): pl.pallas_call(functools.partial(back_kernel, sz), out_shape=[o for o, _...  21.4 us

profile of v4, /device:TPU:1, one launch (start us, length us, event | category | flops | bytes accessed | tf_op | source)
XLA Modules:
  0.0 103.1 jit_solution(5997686827153551978)
XLA Ops:
  1.3 0.0 copy-start.25
  1.3 0.0 copy-start.35
  1.3 0.0 copy-start.46
  1.3 79.0 %front.1 = (bf16[2,8,4,1024,256]{4,3,2,1,0:T(8,128)(2,1)}, bf16[1024,640]{1,0:T(8,128)(2,1)}, bf16[1024,1024]{1,0:T(8,128)(2,1)}, bf16[1024,512]{1,0:T(8,128)(2,...) custom-call(s32[50,128]{1,0:T(8,128)} %bitcast.214.watch_ids, ...), custom_call_target="tpu_custom_call" | custom-call | tf_op jit(solution)/shard_map/front/pallas_call | solution.py:1181
  80.9 0.0 copy-done.25
  80.9 0.0 copy-done.35
  80.9 0.0 copy-done.46
  80.9 21.6 %conditional.1 = (bf16[32,256]{1,0:T(8,128)(2,1)}, f32[]{:T(128)}, f32[64,8192]{1,0:T(8,128)}, f32[64,8192]{1,0:T(8,128)}, f32[64,8192]{1,0:T(8,128)}, /*index=5...) conditional(s32[]{:T(128)} %bitcast.223, ...), branch_computations={%region_0.16_spmd, %region_10.17_spmd} | conditional | flops 10206007296 | bytes 624368768 | solution.py:1382
  81.2 21.4 %back.1 = (f32[64,8192]{1,0:T(8,128)}, f32[64,8192]{1,0:T(8,128)}, f32[64,8192]{1,0:T(8,128)}, f32[600,1024]{1,0:T(8,128)}, f32[1024,512]{1,0:T(8,128)}, /*index...) custom-call(bf16[64,768]{1,0:T(8,128)(2,1)} %get-tuple-element.148.n, ...), custom_call_target="tpu_custom_call" | custom-call | tf_op jit(solution)/shard_map/cond/branch_1_fun/back/pallas_call | solution.py:1338
  102.5 0.0 copy-start.41
  102.6 0.6 copy-done.41
Async XLA Ops:
  1.3 79.6 %copy-start.25 = (s32[5120]{0:T(1024)S(1)}, s32[5120]{0:T(1024)}, u32[]{:S(2)}) copy-start(s32[5120]{0:T(1024)} %param.34) | copy-start | bytes 61444
  1.3 79.6 %copy-start.35 = (s32[128,4]{0,1:T(4,128)S(1)}, s32[128,4]{0,1:T(4,128)}, u32[]{:S(2)}) copy-start(s32[128,4]{0,1:T(4,128)} %param.32) | copy-start | bytes 6148
  1.3 79.6 %copy-start.46 = (s32[128]{0:T(128)S(1)}, s32[128]{0:T(128)}, u32[]{:S(2)}) copy-start(s32[128]{0:T(128)} %param.33) | copy-start | bytes 1540
  102.5 0.6 copy-start.41

commit v5 on v4

--- a/solution.py
+++ b/solution.py
@@ -379,7 +379,7 @@
     tabs, tall, mix, w1_raw, w1, w1_own, w2, w3, turned, upright, lines_own, ids, side, neg_dest, neg_digits, counts, found_sums, sums, pieces, x,
     pre1, pre2, acts1, slopes1, acts2, slopes2, users, buckets, slots, picked, neg_all, pos_all, e_cols,
     e_rows, low_rows, pos_table, probs, stats, factors, home, g_send, g_recv, gu, gps, gpf, gx, rg_send, rg_recv, gp_all, loss_all,
-    local_sem, out_sem, down_sem, count_sem, ids_s, ids_r, sd_s, sd_r, ic_s, ic_r, rs_s, rs_r, ag_s, ag_r, xx_s, xx_r, co_s, co_r,
+    local_sem, out_sem, down_sem, count_sem, ids_s, ids_r, sd_s, sd_r, dx_s, dx_r, rs_s, rs_r, ag_s, ag_r, xx_s, xx_r, co_s, co_r,
     ne_s, ne_r, pe_s, pe_r, ho_s, ho_r, st_s, st_r, gs_s, gs_r, ga_s, ga_r, gx_s, gx_r, gc_s, gc_r,
     rg_s, rg_r, gp_s, gp_r, lo_s, lo_r,
 ):
@@ -410,10 +410,12 @@
         )
 
     barrier = pltpu.get_barrier_semaphore()
-    for i in range(1, nb):
-        pl.semaphore_signal(barrier, inc=1, device_id=(batch_peer(i), c), device_id_type=MESH)
-    for i in range(1, nc):
-        pl.semaphore_signal(barrier, inc=1, device_id=(b, col_peer(i)), device_id_type=MESH)
+    for i in range(nb):
+        for k in range(nc):
+            if i + k > 0:
+                pl.semaphore_signal(
+                    barrier, inc=1, device_id=(batch_peer(i), col_peer(k)), device_id_type=MESH
+                )
 
     loads = [
         (watch_table, tabs.at[0]), (search_table, tabs.at[1]), (out_table, tabs.at[2]),
@@ -435,19 +437,20 @@
     def share_of(col):
         return pl.ds(pl.multiple_of(col * share, share), share)
 
-    ids[b, share_of(c), :] = lines_own[share_of(c), :]
+    ids[b] = lines_own[...]
     side[b] = jnp.zeros((8, 128), I32)
     side[b, 0:1, :] = pos_ids[...]
     side[b, 1:2, :] = jnp.full((1, 128), valid_count[0], I32)
     side[b, 2 : 2 + demo_ids.shape[0], :] = demo_ids[...]
 
-    pl.semaphore_wait(barrier, nb - 1 + nc - 1)
+    pl.semaphore_wait(barrier, nb * nc - 1)
     last_sends = []
     for i in range(1, nb):
-        place = ids.at[b, share_of(c)]
-        copy = send(place, place, ids_s.at[i - 1], ids_r.at[i - 1], (batch_peer(i), c))
-        copy.start()
-        last_sends.append(copy)
+        for k in range(nc):
+            place = ids.at[b, share_of(c)]
+            copy = send(place, place, ids_s.at[k, i - 1], ids_r.at[k], (batch_peer(i), col_peer(k)))
+            copy.start()
+            last_sends.append(copy)
 
     for i in range(1, nb):
         copy = send(side.at[b], side.at[b], sd_s.at[i - 1], sd_r.at[i - 1], (batch_peer(i), c))
@@ -495,14 +498,6 @@
         slots[k, 0:1, :] = neg_high[:, k * CHUNK : (k + 1) * CHUNK]
         slots[k, 1:2, :] = neg_low[:, k * CHUNK : (k + 1) * CHUNK]
 
-    for i in range(1, nb):
-        place = ids.at[batch_from(i), share_of(c)]
-        send(place, place, ids_s.at[i - 1], ids_r.at[i - 1], (b, c)).wait_recv()
-    for i in range(1, nc):
-        place = ids.at[:, share_of(c)]
-        copy = send(place, place, ic_s.at[i - 1], ic_r.at[i - 1], (b, col_peer(i)))
-        copy.start()
-        last_sends.append(copy)
     for t in range(2):
         loads[t].wait()
 
@@ -561,9 +556,9 @@
     w1_own[...] = jnp.zeros(w1_own.shape, BF16)
     w1_own[0 : 2 * width, :] = w1[pl.ds(pl.multiple_of((lax.rem(c, 2) * 2 + c // 2) * 128, 128), 128), :]
     w1_own[2 * width : 2 * width + sz.demo_width, :] = w1_raw[2 * embed :, :]
-    for i in range(1, nc):
-        place = ids.at[:, share_of(col_from(i))]
-        send(place, place, ic_s.at[i - 1], ic_r.at[i - 1], (b, c)).wait_recv()
+    for k in range(nc):
+        place = ids.at[pl.ds(0, nb - 1), share_of(col_from(k))]
+        send(place, place, ids_s.at[k, 0], ids_r.at[k], (b, c)).wait_recv()
 
     users_shape = (nb, CHUNK)
     at_block = iota(users_shape, 1) // sz.quarter == iota(users_shape, 0)
@@ -643,7 +638,7 @@
             counts.at[table, slot_at], counts_out.at[table, :, :, rows], count_sem.at[table, slot_at]
         )
 
-    def bag_table(t, table):
+    def bag_table(t, table, between):
         slot_at = lax.rem(t, 2)
 
         @pl.when(t >= 2)
@@ -683,6 +678,7 @@
 
         lax.fori_loop(0, blocks * parts_in_block, groups_of, 0)
         count_copy(t, table, slot_at).start()
+        between()
         left = jnp.concatenate(
             [counts[table, slot_at, hh].reshape(4 * span, LOW) for hh in range(sz.high_parts)], axis=1
         )
@@ -720,7 +716,7 @@
             pl.ds(pl.multiple_of(t * span + owner * piece, piece), piece), lanes_of(c)
         ]
 
-    def reduce_step(t):
+    def reduce_step(t, direct=False):
         send(pieces.at[t], pieces.at[t], rs_s.at[t, 0], rs_r.at[t], (b, c)).wait_recv()
         total = sums[t, pl.ds(pl.multiple_of(b * piece, piece), piece), :].astype(F32)
         for i in range(nb - 1):
@@ -730,6 +726,21 @@
         ] = (total / sz.bag).astype(BF16)
         for i in range(1, nb):
             send(x_piece(t, b), x_piece(t, b), ag_s.at[t, i - 1], ag_r.at[t], (batch_peer(i), c)).start()
+        if direct:
+            for i in range(nb):
+                for k in range(1, nc):
+                    direct_send(t, i, k).start()
+
+    def direct_send(t, i, k):
+        return send(
+            x_piece(t, b), x_piece(t, b), dx_s.at[k - 1, i], dx_r.at[k - 1], (batch_peer(i), col_peer(k))
+        )
+
+    def direct_wait(t):
+        send(pieces.at[t], pieces.at[t], ag_s.at[t, 0], ag_r.at[t], (b, c)).wait_recv()
+        for k in range(1, nc):
+            place = x_at(t, col_from(k))
+            send(place, place, dx_s.at[k - 1, 0], dx_r.at[k - 1], (b, c)).wait_recv()
 
     def cross_step(t):
         send(pieces.at[t], pieces.at[t], ag_s.at[t, 0], ag_r.at[t], (b, c)).wait_recv()
@@ -766,9 +777,14 @@
         half = n // 2
         odd = lax.rem(n, 2) == 1
 
+        def between():
+            @pl.when(odd & (n >= 3))
+            def _():
+                reduce_step((n - 3) // 2)
+
         @pl.when(n < bag_ticks)
         def _():
-            bag_table(half, lax.rem(n, 2))
+            bag_table(half, lax.rem(n, 2), between)
 
         @pl.when((n < bag_ticks) & odd)
         def _():
@@ -786,9 +802,9 @@
         def _():
             slot_rows()
 
-        @pl.when(odd & (n >= 5))
+        @pl.when((~odd) & (n >= 6) & (n <= bag_ticks))
         def _():
-            full_step((n - 5) // 2)
+            full_step((n - 6) // 2)
 
         done = jnp.where(n <= bag_ticks, 0, jnp.where(n <= bag_ticks + 2, 1, last))
         ready = jnp.where(
@@ -796,22 +812,30 @@
         )
 
         def some_tower(k, _):
+            @pl.when(k == last - 1)
+            def _():
+                full_step(k)
+
+            @pl.when(k == last)
+            def _():
+                direct_wait(last)
+
             tower(k)
             return 0
 
         lax.fori_loop(done, ready, some_tower, 0)
 
-        @pl.when((~odd) & (n >= 2) & (n <= bag_ticks))
+        @pl.when((~odd) & (n >= 4) & (n <= bag_ticks))
         def _():
-            reduce_step(half - 1)
-
-        @pl.when(odd & (n >= 3) & (n <= bag_ticks + 1))
+            cross_step((n - 4) // 2)
+
+        @pl.when(n == bag_ticks)
         def _():
-            cross_step((n - 3) // 2)
-
-        @pl.when((~odd) & (n >= 4) & (n <= bag_ticks + 2))
+            reduce_step(last, direct=True)
+
+        @pl.when(odd & (n >= 5) & (n <= bag_ticks + 1))
         def _():
-            core_step(half - 2)
+            core_step((n - 5) // 2)
 
         return 0
 
@@ -939,6 +963,10 @@
         copy = send(gu_at(b, c), gu_at(b, c), ga_s.at[i - 1], ga_r.at[i - 1], (batch_peer(i), c))
         copy.start()
         last_sends.append(copy)
+    for i in range(nb):
+        copy = send(gu_at(b, c), gu_at(b, c), gx_s.at[i], gx_r.at[i], (batch_peer(i), cx))
+        copy.start()
+        last_sends.append(copy)
 
     for k in range(nc):
         low = slots[sz.cap_tiles + k, 1:2, :].astype(BF16)
@@ -971,13 +999,9 @@
     lax.fori_loop(0, sz.high_parts // 2, pos_scatter, 0)
     pos_copy = pltpu.make_async_copy(pos_table, pos_table_out, out_sem.at[5])
     pos_copy.start()
-    for i in range(nb):
+    for i in range(1, nb):
         src = batch_from(i)
-        if i > 0:
-            send(gu_at(src, c), gu_at(src, c), ga_s.at[i - 1], ga_r.at[i - 1], (b, c)).wait_recv()
-        copy = send(gu_at(src, c), gu_at(src, c), gx_s.at[i], gx_r.at[i], (b, cx))
-        copy.start()
-        last_sends.append(copy)
+        send(gu_at(src, c), gu_at(src, c), ga_s.at[i - 1], ga_r.at[i - 1], (b, c)).wait_recv()
     copy = send(gu_all(c), gu_all(c), gc_s.at[0], gc_r.at[0], (b, ck))
     copy.start()
     last_sends.append(copy)
@@ -1068,11 +1092,18 @@
         for i in range(1, nb):
             send(sums.at[t, pl.ds(0, piece)], pieces.at[t, 0], rs_s.at[t, i - 1], rs_r.at[t], (b, c)).wait_send()
             send(x_piece(t, b), x_piece(t, b), ag_s.at[t, i - 1], ag_r.at[t], (b, c)).wait_send()
-        send(x_at(t, c), x_at(t, c), xx_s.at[t], xx_r.at[t], (b, cx)).wait_send()
-        send(x_pair(t, c), x_pair(t, c), co_s.at[t], co_r.at[t], (b, ck)).wait_send()
+
+        @pl.when(t < last)
+        def _():
+            send(x_at(t, c), x_at(t, c), xx_s.at[t], xx_r.at[t], (b, cx)).wait_send()
+            send(x_pair(t, c), x_pair(t, c), co_s.at[t], co_r.at[t], (b, ck)).wait_send()
+
         return 0
 
     lax.fori_loop(0, sz.steps, drain, 0)
+    for i in range(nb):
+        for k in range(1, nc):
+            direct_send(last, i, k).wait_send()
     for table in range(2):
         for t in (sz.steps - 2, sz.steps - 1):
             count_copy(t, table, t % 2).wait()
@@ -1161,7 +1192,7 @@
         pltpu.VMEM((nc, 8, users), F32),
         pltpu.VMEM((nc, 8, 128), F32),
         dma((6,)), dma((6,)), dma((nc, 3)), dma((2, 2)),
-        dma((nb - 1,)), dma((nb - 1,)), dma((nb - 1,)), dma((nb - 1,)), dma((nc - 1,)), dma((nc - 1,)),
+        dma((nc, nb - 1)), dma((nc,)), dma((nb - 1,)), dma((nb - 1,)), dma((nc - 1, nb)), dma((nc - 1,)),
         dma((sz.steps, nb - 1)), dma((sz.steps,)), dma((sz.steps, nb - 1)), dma((sz.steps,)),
         dma((sz.steps,)), dma((sz.steps,)), dma((sz.steps,)), dma((sz.steps,)),
         dma((nc - 1,)), dma((nc - 1,)), dma((nc - 1,)), dma((nc - 1,)), dma((nb - 1,)), dma((nb - 1,)),

time: 103 us -> 101 us (0.981)
  Pallas kernels: 100 us -> 97.5 us
    pallas_call x1, Pallas kernels: 79 us -> 76.2 us  [front(): pl.pallas_call(functools.partial(front_kernel, sz), out_shape=[o for o, _...]
where the time goes in v5:
time: 101 us; the launch traced here: 100 us
  Pallas kernels  97.5 us (97%)
  between operations  1.94 us (2%)
    pallas_call x1, Pallas kernels, front(): pl.pallas_call(functools.partial(front_kernel, sz), out_shape=[o for o, _...  76.2 us
    pallas_call x1, Pallas kernels, back(): pl.pallas_call(functools.partial(back_kernel, sz), out_shape=[o for o, _...  21.4 us

profile of v5, /device:TPU:1, one launch (start us, length us, event | category | flops | bytes accessed | tf_op | source)
XLA Modules:
  0.0 100.3 jit_solution(8288928818295525652)
XLA Ops:
  1.3 0.0 copy-start.25
  1.3 0.0 copy-start.35
  1.3 0.0 copy-start.46
  1.3 76.2 %front.1 = (bf16[2,8,4,1024,256]{4,3,2,1,0:T(8,128)(2,1)}, bf16[1024,640]{1,0:T(8,128)(2,1)}, bf16[1024,1024]{1,0:T(8,128)(2,1)}, bf16[1024,512]{1,0:T(8,128)(2,...) custom-call(s32[50,128]{1,0:T(8,128)} %bitcast.214.watch_ids, ...), custom_call_target="tpu_custom_call" | custom-call | tf_op jit(solution)/shard_map/front/pallas_call | solution.py:1212
  78.1 0.0 copy-done.25
  78.1 0.0 copy-done.35
  78.1 0.0 copy-done.46
  78.1 21.6 %conditional.1 = (bf16[32,256]{1,0:T(8,128)(2,1)}, f32[]{:T(128)}, f32[64,8192]{1,0:T(8,128)}, f32[64,8192]{1,0:T(8,128)}, f32[64,8192]{1,0:T(8,128)}, /*index=5...) conditional(s32[]{:T(128)} %bitcast.223, ...), branch_computations={%region_0.16_spmd, %region_10.17_spmd} | conditional | flops 10206007296 | bytes 624368768 | solution.py:1413
  78.3 21.4 %back.1 = (f32[64,8192]{1,0:T(8,128)}, f32[64,8192]{1,0:T(8,128)}, f32[64,8192]{1,0:T(8,128)}, f32[600,1024]{1,0:T(8,128)}, f32[1024,512]{1,0:T(8,128)}, /*index...) custom-call(bf16[64,768]{1,0:T(8,128)(2,1)} %get-tuple-element.148.n, ...), custom_call_target="tpu_custom_call" | custom-call | tf_op jit(solution)/shard_map/cond/branch_1_fun/back/pallas_call | solution.py:1369
  99.7 0.0 copy-start.41
  99.7 0.6 copy-done.41
Async XLA Ops:
  1.3 76.8 %copy-start.25 = (s32[5120]{0:T(1024)S(1)}, s32[5120]{0:T(1024)}, u32[]{:S(2)}) copy-start(s32[5120]{0:T(1024)} %param.34) | copy-start | bytes 61444
  1.3 76.8 %copy-start.35 = (s32[128,4]{0,1:T(4,128)S(1)}, s32[128,4]{0,1:T(4,128)}, u32[]{:S(2)}) copy-start(s32[128,4]{0,1:T(4,128)} %param.32) | copy-start | bytes 6148
  1.3 76.8 %copy-start.46 = (s32[128]{0:T(128)S(1)}, s32[128]{0:T(128)}, u32[]{:S(2)}) copy-start(s32[128]{0:T(128)} %param.33) | copy-start | bytes 1540
  99.7 0.6 copy-start.41

commit v6 on v5

--- a/solution.py
+++ b/solution.py
@@ -564,9 +564,6 @@
     at_block = iota(users_shape, 1) // sz.quarter == iota(users_shape, 0)
 
     def demo_part():
-        for i in range(1, nb):
-            place = side.at[batch_from(i)]
-            send(place, place, sd_s.at[i - 1], sd_r.at[i - 1], (b, c)).wait_recv()
         bucket_total = jnp.zeros((buckets.shape[0], sz.total), BF16)
         bucket_line = iota((buckets.shape[0], sz.total), 0).astype(BF16)
         for field in range(demo_ids.shape[0]):
@@ -578,6 +575,9 @@
         x[:, nc * 128 : nc * 128 + sz.demo_width] = dot_as(bucket_total, demo_rows, 0, 0).astype(BF16)
 
     def pos_part():
+        for i in range(1, nb):
+            place = side.at[batch_from(i)]
+            send(place, place, sd_s.at[i - 1], sd_r.at[i - 1], (b, c)).wait_recv()
         all_pos = jnp.concatenate([side[j, 0:1, :] for j in range(nb)], axis=0)
         pos_local = all_pos - offset
         pos_owned = (pos_local >= 0) & (pos_local < sz.vocab)
@@ -765,6 +765,18 @@
         acts2[at, :] = value
         users[at, :] = (dot_as(value, w3[...], 1, 0) + b_third[...]).astype(BF16)
 
+    def tower_quarter():
+        places = [
+            pl.ds(pl.multiple_of(last * span + j * sz.rows + c * sz.quarter, sz.quarter), sz.quarter)
+            for j in range(blocks)
+        ]
+        rows = jnp.concatenate([x[at, :] for at in places], axis=0)
+        value = gelu(dot_as(rows, w1[...], 1, 0) + b_first[...]).astype(BF16)
+        value = gelu(dot_as(value, w2[...], 1, 0) + b_second[...]).astype(BF16)
+        found = (dot_as(value, w3[...], 1, 0) + b_third[...]).astype(BF16)
+        for j, at in enumerate(places):
+            users[at, :] = found[j * sz.quarter : (j + 1) * sz.quarter]
+
     def slopes(k):
         at = pl.ds(pl.multiple_of(k * span, span), span)
         slopes1[at, :] = gelu_slope(pre1[at, :]).astype(BF16)
@@ -792,11 +804,11 @@
 
         @pl.when(n == bag_ticks)
         def _():
-            demo_part()
+            pos_part()
 
         @pl.when(n == bag_ticks + 1)
         def _():
-            pos_part()
+            demo_part()
 
         @pl.when(n == bag_ticks + 3)
         def _():
@@ -806,9 +818,9 @@
         def _():
             full_step((n - 6) // 2)
 
-        done = jnp.where(n <= bag_ticks, 0, jnp.where(n <= bag_ticks + 2, 1, last))
+        done = jnp.where(n <= bag_ticks + 1, 0, jnp.where(n == bag_ticks + 2, 1, last))
         ready = jnp.where(
-            n < bag_ticks, 0, jnp.where(n <= bag_ticks + 1, 1, jnp.where(n == bag_ticks + 2, last, sz.steps))
+            n <= bag_ticks, 0, jnp.where(n == bag_ticks + 1, 1, last)
         )
 
         def some_tower(k, _):
@@ -816,10 +828,6 @@
             def _():
                 full_step(k)
 
-            @pl.when(k == last)
-            def _():
-                direct_wait(last)
-
             tower(k)
             return 0
 
@@ -840,6 +848,8 @@
         return 0
 
     lax.fori_loop(0, bag_ticks + 4, tick, 0)
+    direct_wait(last)
+    tower_quarter()
 
     valid = jnp.concatenate([side[j, 1:2, :] for j in range(nb)], axis=0)
     valid_wide = jnp.concatenate([valid] * (sz.users // 128), axis=1).astype(F32)
@@ -848,10 +858,6 @@
     user_place = c * sz.quarter + iota((1, sz.users), 1) % sz.quarter
     weight = jnp.where(user_place.astype(F32) < live_count, 1.0 / valid_total, 0.0)
 
-    out_copies = [(x, x_out), (acts1, act1_out), (acts2, act2_out), (buckets, buckets_out)]
-    out_copies = [pltpu.make_async_copy(s, d, out_sem.at[i]) for i, (s, d) in enumerate(out_copies)]
-    for copy in out_copies:
-        copy.start()
     user_out[...] = users[pl.ds(pl.multiple_of(b * sz.rows + c * sz.quarter, sz.quarter), sz.quarter), :]
 
     def users_of(quarter):
@@ -899,7 +905,7 @@
         slopes(k)
         return 0
 
-    lax.fori_loop(0, sz.steps, some_slopes, 0)
+    lax.fori_loop(0, last, some_slopes, 0)
     for i in range(1, nb):
         src = batch_from(i)
         send(stats.at[src], stats.at[src], st_s.at[i - 1], st_r.at[i - 1], (b, c)).wait_recv()
@@ -968,6 +974,12 @@
         copy.start()
         last_sends.append(copy)
 
+    tower(last)
+    slopes(last)
+    out_copies = [(x, x_out), (acts1, act1_out), (acts2, act2_out), (buckets, buckets_out)]
+    out_copies = [pltpu.make_async_copy(s, d, out_sem.at[i]) for i, (s, d) in enumerate(out_copies)]
+    for copy in out_copies:
+        copy.start()
     for k in range(nc):
         low = slots[sz.cap_tiles + k, 1:2, :].astype(BF16)
         hot = one_where(low == iota((LOW, CHUNK), 0).astype(BF16), BF16)
@@ -993,7 +1005,7 @@
             for i in range(4):
                 pos_table[n * 2 + j, :, i * LOW : (i + 1) * LOW] = found[
                     (j * 4 + i) * width : (j * 4 + i + 1) * width
-                ]
+                ].astype(BF16)
         return 0
 
     lax.fori_loop(0, sz.high_parts // 2, pos_scatter, 0)
@@ -1136,7 +1148,7 @@
         (shape((total, first)), hbm), (shape((total, second)), hbm), (shape((nb, sz.rows, embed)), hbm),
         (shape((nb, sz.rows, second)), hbm), (shape((nb, sz.rows, first)), hbm),
         (shape((nb, sz.rows, 256)), hbm), (shape((buckets, total)), hbm),
-        (shape((width, cap)), vmem), (shape((sz.high_parts, width, 4 * LOW), F32), hbm),
+        (shape((width, cap)), vmem), (shape((sz.high_parts, width, 4 * LOW)), hbm),
         (shape((sz.tiles, 8, CHUNK), F32), vmem),
         (shape((sz.quarter, embed)), vmem), (shape((1, 1), F32), vmem), (shape((1, 1), I32), vmem),
     ]
@@ -1176,7 +1188,7 @@
         pltpu.VMEM((embed, slots), BF16),
         pltpu.VMEM((slots, embed), BF16),
         pltpu.VMEM((nc * CHUNK, LOW), BF16),
-        pltpu.VMEM((sz.high_parts, width, 4 * LOW), F32),
+        pltpu.VMEM((sz.high_parts, width, 4 * LOW), BF16),
         pltpu.VMEM((cap, users), BF16),
         pltpu.VMEM((nb, 8, users), F32),
         pltpu.VMEM((users, 16), F32),
@@ -1241,12 +1253,11 @@
     user_out[...] = user_in[...]
     loss_out[...] = loss_in[...]
 
-    def ring_load(n):
-        return pltpu.make_async_copy(
-            counts.at[lax.rem(n, 2), n // 2], ring.at[lax.rem(n, depth)], ring_sem.at[lax.rem(n, depth)]
-        )
-
-    early = depth - 2
+    def ring_load(hh):
+        at = lax.rem(hh, depth)
+        return pltpu.make_async_copy(counts.at[:, hh], ring.at[at], ring_sem.at[at])
+
+    early = depth - 1
     for n in range(early):
         ring_load(n).start()
     for load in loads[2:]:
@@ -1283,25 +1294,23 @@
                 line_store(table_out, 4 + j, (n - 1) * 2 + j).wait()
 
             rows = [found[(j * 4 + i) * width : (j * 4 + i + 1) * width] for i in range(4)]
-            rows = [rows[i] + pos_table[n * 2 + j, :, i * LOW : (i + 1) * LOW] for i in range(4)]
+            rows = [rows[i] + pos_table[n * 2 + j, :, i * LOW : (i + 1) * LOW].astype(F32) for i in range(4)]
             put(4 + j, rows, 1.0)
             line_store(table_out, 4 + j, n * 2 + j).start()
         return 0
 
     lax.fori_loop(0, parts // 2, scatter, 0)
     def bags(hh, _):
+        ring_load(hh).wait()
         for table, out in enumerate((watch_out, search_out)):
-            n = hh * 2 + table
             slot = table * 2 + lax.rem(hh, 2)
-            ring_load(n).wait()
             found = [
-                dot_as(grads[i % 2, table * width : (table + 1) * width, :], ring[lax.rem(n, depth), i], 1, 0)
+                dot_as(
+                    grads[i % 2, table * width : (table + 1) * width, :],
+                    ring[lax.rem(hh, depth), table, i], 1, 0,
+                )
                 for i in range(4)
             ]
-
-            @pl.when(n + depth < 2 * parts)
-            def _():
-                ring_load(n + depth).start()
 
             @pl.when(hh >= 2)
             def _():
@@ -1309,6 +1318,11 @@
 
             put(slot, found, 1.0 / sz.bag)
             line_store(out, slot, hh).start()
+
+        @pl.when(hh + depth < parts)
+        def _():
+            ring_load(hh + depth).start()
+
         return 0
 
     lax.fori_loop(0, parts // 2, bags, 0)
@@ -1372,16 +1386,16 @@
         in_specs=[vmem] * 4 + [hbm] * 10,
         out_specs=[s for _, s in outs],
         scratch_shapes=[
-            pltpu.VMEM((sz.high_parts, sz.width, 4 * LOW), F32),
+            pltpu.VMEM((sz.high_parts, sz.width, 4 * LOW), BF16),
             pltpu.VMEM((total, sz.x_width), BF16), pltpu.VMEM((total, first), BF16),
             pltpu.VMEM((total, second), BF16), pltpu.VMEM((nb, sz.rows, embed), BF16),
             pltpu.VMEM((nb, sz.rows, second), BF16), pltpu.VMEM((nb, sz.rows, first), BF16),
             pltpu.VMEM((nb, sz.rows, 256), BF16), pltpu.VMEM((buckets, total), BF16),
-            pltpu.VMEM((2, 128, total), BF16), pltpu.VMEM((8, 4, total, LOW), BF16),
+            pltpu.VMEM((2, 128, total), BF16), pltpu.VMEM((4, 2, 4, total, LOW), BF16),
             pltpu.VMEM((6, sz.width, 4 * LOW), F32), pltpu.VMEM((slots, LOW), BF16),
             pltpu.VMEM((sz.x_width, first), F32), pltpu.VMEM((first, second), F32),
             pltpu.VMEM((second, embed), F32),
-            dma((9,)), dma((8,)), dma((6,)), dma((3 + 2 * sz.col,)),
+            dma((9,)), dma((4,)), dma((6,)), dma((3 + 2 * sz.col,)),
         ],
         compiler_params=pltpu.CompilerParams(vmem_limit_bytes=62 * 2**20),
         name="back",

time: 101 us -> 100 us (0.990)
  no operation moved by 1% of the time
where the time goes in v6:
time: 100 us
  Pallas kernels  97.4 us (97%)
  between operations  1.92 us (2%)
    pallas_call x1, Pallas kernels, front(): pl.pallas_call(functools.partial(front_kernel, sz), out_shape=[o for o, _...  76 us
    pallas_call x1, Pallas kernels, back(): pl.pallas_call(functools.partial(back_kernel, sz), out_shape=[o for o, _...  21.3 us

profile of v6, /device:TPU:1, one launch (start us, length us, event | category | flops | bytes accessed | tf_op | source)
XLA Modules:
  0.0 100.1 jit_solution(4535180251514027693)
XLA Ops:
  1.3 0.0 copy-start.25
  1.3 0.0 copy-start.35
  1.3 0.0 copy-start.46
  1.3 76.0 %front.1 = (bf16[2,8,4,1024,256]{4,3,2,1,0:T(8,128)(2,1)}, bf16[1024,640]{1,0:T(8,128)(2,1)}, bf16[1024,1024]{1,0:T(8,128)(2,1)}, bf16[1024,512]{1,0:T(8,128)(2,...) custom-call(s32[50,128]{1,0:T(8,128)} %bitcast.214.watch_ids, ...), custom_call_target="tpu_custom_call" | custom-call | tf_op jit(solution)/shard_map/front/pallas_call | solution.py:1224
  77.9 0.0 copy-done.25
  77.9 0.0 copy-done.35
  77.9 0.0 copy-done.46
  77.9 21.6 %conditional.1 = (bf16[32,256]{1,0:T(8,128)(2,1)}, f32[]{:T(128)}, f32[64,8192]{1,0:T(8,128)}, f32[64,8192]{1,0:T(8,128)}, f32[64,8192]{1,0:T(8,128)}, /*index=5...) conditional(s32[]{:T(128)} %bitcast.223, ...), branch_computations={%region_0.16_spmd, %region_10.17_spmd} | conditional | flops 10206007296 | bytes 624368768 | solution.py:1427
  78.2 21.3 %back.1 = (f32[64,8192]{1,0:T(8,128)}, f32[64,8192]{1,0:T(8,128)}, f32[64,8192]{1,0:T(8,128)}, f32[600,1024]{1,0:T(8,128)}, f32[1024,512]{1,0:T(8,128)}, /*index...) custom-call(bf16[64,768]{1,0:T(8,128)(2,1)} %get-tuple-element.148.n, ...), custom_call_target="tpu_custom_call" | custom-call | tf_op jit(solution)/shard_map/cond/branch_1_fun/back/pallas_call | solution.py:1383
  99.5 0.0 copy-start.41
  99.5 0.6 copy-done.41
Async XLA Ops:
  1.3 76.6 %copy-start.25 = (s32[5120]{0:T(1024)S(1)}, s32[5120]{0:T(1024)}, u32[]{:S(2)}) copy-start(s32[5120]{0:T(1024)} %param.34) | copy-start | bytes 61444
  1.3 76.6 %copy-start.35 = (s32[128,4]{0,1:T(4,128)S(1)}, s32[128,4]{0,1:T(4,128)}, u32[]{:S(2)}) copy-start(s32[128,4]{0,1:T(4,128)} %param.32) | copy-start | bytes 6148
  1.3 76.6 %copy-start.46 = (s32[128]{0:T(128)S(1)}, s32[128]{0:T(128)}, u32[]{:S(2)}) copy-start(s32[128]{0:T(128)} %param.33) | copy-start | bytes 1540
  99.5 0.6 copy-start.41
